TPU v7x, 128 devices: a whole 4x4x4 slice. The times are simulated.
128 devices in a mesh: dp: 32 (over z, x, core), feat: 4 (over y).
Axes of the slice: x: 4, y: 4, z: 4, core: 2. Of those that a mesh axis runs over, the one named last changes fastest.
Arguments:
- samples: bfloat16 [98304, 8192], P('dp', 'feat'), may hold values from -6 to 6
- factors: float32 [256, 8192], P('dp', 'feat'), may hold values from -1 to 1
- weights: float32 [256], replicated, may hold values from 0.2 to 1
- counts: int32 [32], replicated, may hold values from 1024 to 3072, as said below
Outputs:
- gradient: float32 [256, 8192], P('dp', 'feat')
Inputs may be any that keep to these rules, and one draw needn't show every extreme that they name: Only the first counts[i] slots of block i are live; some block holds 3072 live samples and some 3072 // 3.
All inputs are finite; a program needn't handle non-finite values.
Results may differ from a plain program's by a relative error of at most 0.0046.
Values may be sent and summed in bfloat16 or wider, within the bound.
No kernel may reach another device: no remote copies, remote signals or barrier semaphores. Data moves between devices by JAX's collectives and lax.ppermute only.
A program may use at most 64 MiB of HBM per device.

v0:
```python
import jax
import jax.numpy as jnp
from jax import lax
from jax.sharding import PartitionSpec as P


def on_device(samples, factors, weights, counts):
    owned_rows = factors.shape[0]
    device_number = lax.axis_index("dp")
    live_count = counts[device_number]
    sample_total = jnp.sum(counts).astype(jnp.float32)
    gathered = lax.all_gather(factors, "dp", axis=0, tiled=True)
    gram_matrix = lax.psum(jnp.dot(gathered, gathered.T, precision=lax.Precision.HIGHEST), "feat")
    first_owned = device_number * owned_rows
    gram_owned = lax.dynamic_slice_in_dim(gram_matrix, first_owned, owned_rows, 0)
    weight_owned = lax.dynamic_slice_in_dim(weights, first_owned, owned_rows, 0)
    coupling = weight_owned[:, None] * weights[None, :] * gram_owned**3
    model_term = jnp.dot(coupling, gathered, precision=lax.Precision.HIGHEST)
    narrow = gathered.astype(jnp.bfloat16)
    partial_value = lax.dot_general(
        samples, narrow, (((1,), (1,)), ((), ())), preferred_element_type=jnp.float32
    )
    positions = 0 + jnp.arange(samples.shape[0], dtype=jnp.int32)
    live_rows = (positions < live_count).astype(jnp.float32)[:, None]
    projection = lax.psum(partial_value, "feat")
    cubes_low = (live_rows * weights[None, :] * projection**3).astype(jnp.bfloat16)
    cross_sum = lax.dot_general(
        cubes_low, samples, (((0,), (0,)), ((), ())), preferred_element_type=jnp.float32
    )
    cross_term = lax.psum_scatter(cross_sum, "dp", scatter_dimension=0, tiled=True)
    return 8.0 * model_term - 8.0 / sample_total * cross_term


def solution(mesh):
    in_specs = (P("dp", "feat"), P("dp", "feat"), P(), P())
    out_specs = P("dp", "feat")
    return jax.shard_map(
        on_device, mesh=mesh, in_specs=in_specs, out_specs=out_specs, check_vma=False
    )
```

profile of v0, /device:TPU:0, one launch (start us, length us, event | category | flops | bytes accessed | tf_op | source)
XLA Modules:
  0.0 248.9 jit_solution(4513812368270546045)
XLA Ops:
  6.5 0.0 all-gather.2.cloned.1.call-start
  6.5 0.7 all-gather.2.cloned.1.call-update
  7.3 0.0 all-reduce.3.cloned.1.call-start
  7.3 48.8 %all-gather.2.cloned.1.call-done = f32[256,2048]{1,0:T(8,128)} async-done(((f32[8,2048]{1,0:T(8,128)}), f32[256,2048]{1,0:T(8,128)}) %all-gather.2.cloned.1.call-update) | async-done | bytes 2097168 | tf_op jit(solution)/shard_map/all_gather | solution.py:12
  56.1 0.0 copy-start
  56.1 4.9 %fusion.17 = f32[256,256]{1,0:T(8,128)} fusion(f32[256,2048]{1,0:T(8,128)} %all-gather.2.cloned.1.call-done), kind=kOutput, calls=%fused_computation.19 | convolution fusion | flops 1610612736 | bytes 2359296 | tf_op jit(solution)/shard_map/dot_general | solution.py:13
  61.0 0.0 copy-done
  61.0 9.7 %fusion.7 = f32[3072,256]{1,0:T(8,128)} fusion(bf16[3072,2048]{1,0:T(8,128)(2,1)} %param.4, f32[256,2048]{1,0:T(8,128)S(1)} %copy-done), kind=kOutput, calls=%fused_computation.8 | convolution fusion | flops 3221749760 | bytes 17825792 | tf_op jit(solution)/shard_map/dot_general | solution.py:20
  70.8 0.0 copy-start.2
  70.8 0.0 copy-start.1
  70.8 0.0 all-reduce.3.cloned.1.call-update
  70.8 0.0 reduce-scatter.2.cloned.1.call-start
  70.8 0.6 copy-done.2
  71.4 0.6 dynamic_slice.11
  72.0 0.6 fusion.9
  72.7 77.8 %all-reduce.3.cloned.1.call-done = (f32[3072,256]{1,0:T(8,128)}, f32[256,256]{1,0:T(8,128)}) async-done(((f32[3072,256]{1,0:T(8,128)}, f32[256,256]{1,0:T(8,128)}), (f32[3072,256]{1,0:T(8,128)}, f32[256,256]{1,0:T(8,128)})) %all-reduce.3.cloned.1.call-update) | async-done | bytes 3407888 | tf_op jit(solution)/shard_map/psum | solution.py:25
  150.4 0.0 copy-done.1
  150.4 10.4 %fusion.3 = f32[256,2048]{1,0:T(8,128)} fusion(bf16[3072,2048]{1,0:T(8,128)(2,1)} %param.4, f32[3072,256]{1,0:T(8,128)} %get-tuple-element.5, f32[256]{0:T(256)S(1)} %copy-done.1, f32[3072]{0:T(1024)S(1)} %fusion.9), kind=kOutput, calls=%fused_computation.5 | convolution fusion | flops 3225157632 | bytes 17839104 | tf_op jit(solution)/shard_map/dot_general | solution.py:27
  160.8 0.0 reduce-scatter.2.cloned.1.call-update
  160.9 0.6 reduce_sum.9
  162.2 0.1 dynamic_slice.9
  162.3 77.5 %reduce-scatter.2.cloned.1.call-done = f32[8,2048]{1,0:T(8,128)} async-done(((f32[256,2048]{1,0:T(8,128)}), f32[8,2048]{1,0:T(8,128)}) %reduce-scatter.2.cloned.1.call-update) | async-done | bytes 65552 | tf_op jit(solution)/shard_map/reduce_scatter | solution.py:30
  239.8 2.6 %fusion.2 = f32[8,2048]{1,0:T(8,128)} fusion(f32[256,2048]{1,0:T(8,128)S(1)} %copy-done, f32[8,2048]{1,0:T(8,128)} %reduce-scatter.2.cloned.1.call-done, f32[]{:T(128)S(6)} %div.3, f32[256,256]{1,0:T(8,128)} %get-tuple-element.6, s32[]{:T(128)S(6)} %select_n.7, f32[256]{0:T(256)S(1)} %copy-done.1, f32[8]{0:T(128)S(1)} %dynamic_slice.9), kind=kOutput, calls=%fused_computation.4 | convolution fusion | flops 50388992 | bytes 2237480 | tf_op jit(solution)/shard_map/dot_general | solution.py:18
Async XLA Ops:
  6.5 49.5 %all-gather.2.cloned.1.call-start = ((), (), s32[]{:S(2)}) async-start(), calls=%async_computation.1 | async-start | bytes 2162688 | tf_op jit(solution)/shard_map/all_gather | solution.py:12
  7.3 143.2 %all-reduce.3.cloned.1.call-start = ((), (), s32[]{:S(2)}) async-start(), calls=%async_computation.3 | async-start | bytes 6815744 | tf_op jit(solution)/shard_map/psum | solution.py:25
  56.1 5.0 %copy-start = (f32[256,2048]{1,0:T(8,128)S(1)}, f32[256,2048]{1,0:T(8,128)}, u32[]{:S(2)}) copy-start(f32[256,2048]{1,0:T(8,128)} %all-gather.2.cloned.1.call-done) | copy-start | bytes 6291460
  70.8 0.7 copy-start.2
  70.8 79.7 %copy-start.1 = (f32[256]{0:T(256)S(1)}, f32[256]{0:T(256)}, u32[]{:S(2)}) copy-start(f32[256]{0:T(256)} %param.6) | copy-start | bytes 3076
  70.8 169.0 %reduce-scatter.2.cloned.1.call-start = ((), (), s32[]{:S(2)}) async-start(), calls=%async_computation.2 | async-start | bytes 2162688 | tf_op jit(solution)/shard_map/reduce_scatter | solution.py:30
Sparse Core Ops, SparseCore 0:
  9.6 46.4 all-gather.1
  70.9 79.4 all-reduce.2
  161.0 78.7 reduce-scatter.1
where the time goes:
time: 249 us
  waiting for transfers between devices  205 us (82%)
  matrix products  27.7 us (11%)
  between operations  13.8 us (6%)
    psum x1, waiting for transfers between devices, on_device(): projection = lax.psum(partial_value, 'feat')  77.8 us
    reduce_scatter x1, waiting for transfers between devices, on_device(): lax.psum_scatter(cross_sum, 'dp', scatter_dimension=0, tiled=True)  77.5 us
    all_gather x1, waiting for transfers between devices, on_device(): gathered = lax.all_gather(factors, 'dp', axis=0, tiled=True)  48.8 us
    dot_general x1, matrix products, on_device(): lax.dot_general(cubes_low, samples, (((0,), (0,)), ((), ())), preferred_e...  10.4 us
    dot_general x1, matrix products, on_device(): lax.dot_general(samples, narrow, (((1,), (1,)), ((), ())), preferred_elem...  9.73 us
  transfers between devices with their start and end apart: 3, of which 3 were waited for; matrix products, arithmetic and copies ran while one was open for 1% of the time, Pallas kernels for 0%

commit v1 on v0

v1 whole, which is shorter than its diff:
```python
import functools

import jax
import jax.numpy as jnp
from jax import lax
from jax.experimental import pallas as pl
from jax.experimental.pallas import tpu as pltpu
from jax.sharding import PartitionSpec as P

BF16 = jnp.bfloat16
F32 = jnp.float32
N_DP = 32
N_FEAT = 4
PLANES = [[2 * chip + core for chip in range(N_DP // 2)] for core in range(2)]


def partner_first(core, y):
    return y ^ 1 if core == 0 else 3 - y


def partner_second(core, y):
    return 3 - y if core == 0 else y ^ 1


def feat_swap(x, partner):
    pairs = []
    for dp in range(N_DP):
        for y in range(N_FEAT):
            pairs.append((dp * N_FEAT + y, dp * N_FEAT + partner(dp % 2, y)))
    return lax.ppermute(x, ("dp", "feat"), pairs)


def core_swap(x):
    return lax.ppermute(x, "dp", [(i, i ^ 1) for i in range(N_DP)])


def plane_exchange(x):
    return lax.all_to_all(x, "dp", 0, 0, axis_index_groups=PLANES, tiled=True)


def projection_kernel(order, other, own, samples, sent0, kept0, sent1, kept1, rows):
    quarter = other.shape[0] // 4

    @pl.when(pl.program_id(0) == 0)
    def _():
        for c, ref in enumerate((other, own)):
            for i in range(4):
                start = pl.multiple_of(order[i] * quarter, quarter)
                rows[pl.ds((4 * c + i) * quarter, quarter), :] = ref[pl.ds(start, quarter), :]

    value = lax.dot_general(
        rows[...], samples[...], (((1,), (1,)), ((), ())), preferred_element_type=F32
    )
    sent0[...] = value[: 2 * quarter].astype(BF16)
    kept0[...] = value[2 * quarter : 4 * quarter]
    sent1[...] = value[4 * quarter : 6 * quarter].astype(BF16)
    kept1[...] = value[6 * quarter :]


def project(order, other, own, samples, tile=512):
    slots, depth = samples.shape
    half = other.shape[0] // 2
    whole = pl.BlockSpec((2 * half, depth), lambda i, s: (0, 0))
    out = pl.BlockSpec((half, tile), lambda i, s: (0, i))
    return pl.pallas_call(
        projection_kernel,
        grid_spec=pltpu.PrefetchScalarGridSpec(
            num_scalar_prefetch=1,
            grid=(slots // tile,),
            in_specs=[whole, whole, pl.BlockSpec((tile, depth), lambda i, s: (i, 0))],
            out_specs=[out] * 4,
            scratch_shapes=[pltpu.VMEM((4 * half, depth), BF16)],
        ),
        out_shape=[
            jax.ShapeDtypeStruct((half, slots), BF16),
            jax.ShapeDtypeStruct((half, slots), F32),
            jax.ShapeDtypeStruct((half, slots), BF16),
            jax.ShapeDtypeStruct((half, slots), F32),
        ],
        compiler_params=pltpu.CompilerParams(vmem_limit_bytes=32 << 20),
        cost_estimate=pl.CostEstimate(
            flops=2 * slots * depth * 4 * half, bytes_accessed=slots * depth * 2, transcendentals=0
        ),
        name="projection",
    )(order, other, own, samples)


def cross_kernel(add, order, cubes0, cubes1, cubes2, samples, *refs):
    if add:
        extra, out, rows = refs
    else:
        out, rows = refs
    quarter = cubes0.shape[0]

    @pl.when(pl.program_id(0) == 0)
    def _():
        pieces = (cubes2[:quarter], cubes2[quarter:], cubes0[...], cubes1[...])
        for i, piece in enumerate(pieces):
            rows[pl.ds(pl.multiple_of(order[i] * quarter, quarter), quarter), :] = piece

    value = lax.dot_general(
        rows[...], samples[...], (((1,), (0,)), ((), ())), preferred_element_type=F32
    )
    if add:
        value = value + extra[...].astype(F32)
    out[...] = value.astype(BF16)


def cross(order, cubes0, cubes1, cubes2, samples, extra=None, tile=512):
    slots, depth = samples.shape
    quarter = cubes0.shape[0]
    add = extra is not None
    one = pl.BlockSpec((quarter, slots), lambda i, s: (0, 0))
    two = pl.BlockSpec((2 * quarter, slots), lambda i, s: (0, 0))
    out = pl.BlockSpec((4 * quarter, tile), lambda i, s: (0, i))
    return pl.pallas_call(
        functools.partial(cross_kernel, add),
        grid_spec=pltpu.PrefetchScalarGridSpec(
            num_scalar_prefetch=1,
            grid=(depth // tile,),
            in_specs=[one, one, two, pl.BlockSpec((slots, tile), lambda i, s: (0, i))]
            + [out] * add,
            out_specs=out,
            scratch_shapes=[pltpu.VMEM((4 * quarter, slots), BF16)],
        ),
        out_shape=jax.ShapeDtypeStruct((4 * quarter, depth), BF16),
        compiler_params=pltpu.CompilerParams(vmem_limit_bytes=32 << 20),
        cost_estimate=pl.CostEstimate(
            flops=2 * slots * depth * 4 * quarter, bytes_accessed=slots * depth * 2, transcendentals=0
        ),
        name="cross",
    )(order, cubes0, cubes1, cubes2, samples, *([extra] if add else []))


def split_dot(left, right, dims):
    high = left.astype(BF16)
    low = (left - high.astype(F32)).astype(BF16)
    both = lax.dot_general(
        jnp.concatenate([high, low], 0), right, (dims, ((), ())), preferred_element_type=F32
    )
    return both[: left.shape[0]] + both[left.shape[0] :]


def on_device(samples, factors, weights, counts):
    owned, depth = factors.shape
    slots = samples.shape[0]
    half_rows = weights.shape[0] // 2
    quarter = half_rows // 4
    dp = lax.axis_index("dp")
    y = lax.axis_index("feat")
    core = lax.rem(dp, 2)
    chip = dp // 2
    first = jnp.where(core == 0, y ^ 1, 3 - y)
    second = jnp.where(core == 0, 3 - y, y ^ 1)
    order = jnp.stack([first, lax.rem(y + 2, 4), y, second]).astype(jnp.int32)
    total = jnp.sum(counts).astype(F32)

    narrow = factors.astype(BF16)
    own = plane_exchange(jnp.tile(narrow, (N_DP // 2, 1)))
    other = core_swap(own)

    sent0, kept0, sent1, kept1 = project(order, other, own, samples)

    by_core = weights.reshape(N_DP // 2, 2, owned).transpose(1, 0, 2).reshape(2, half_rows)
    live = (lax.iota(jnp.int32, slots) < counts[dp]).astype(F32)[None, :]

    def cubes_of(sent, kept, chunk):
        got = feat_swap(sent, partner_first).astype(F32)
        passed = feat_swap((kept[quarter:] + got[quarter:]).astype(BF16), partner_second)
        value = kept[:quarter] + got[:quarter] + passed.astype(F32)
        weight = lax.dynamic_slice(by_core, (chunk, y * quarter), (1, quarter))[0]
        cubes0 = (live * weight[:, None] * value**3).astype(BF16)
        cubes1 = feat_swap(cubes0, partner_second)
        cubes2 = feat_swap(jnp.concatenate([cubes0, cubes1], 0), partner_first)
        return cubes0, cubes1, cubes2

    cubes_other = cubes_of(sent0, kept0, 1 - core)
    cubes_own = cubes_of(sent1, kept1, core)
    cross_other = core_swap(cross(order, *cubes_other, samples))
    cross_own = cross(order, *cubes_own, samples, extra=cross_other)
    blocks = plane_exchange(cross_own).reshape(N_DP // 2, owned, depth)
    cross_term = jnp.sum(blocks.astype(F32), axis=0)

    gram = jnp.concatenate(
        [split_dot(factors, own, ((1,), (1,))), split_dot(factors, other, ((1,), (1,)))], 1
    )
    gram = gram + feat_swap(gram, partner_first)
    gram = gram + feat_swap(gram, partner_second)
    weight_own = lax.dynamic_slice(by_core, (core, 0), (1, half_rows))
    weight_other = lax.dynamic_slice(by_core, (1 - core, 0), (1, half_rows))
    weight_mine = lax.dynamic_slice(weight_own, (0, chip * owned), (1, owned))[0]
    coupling = weight_mine[:, None] * jnp.concatenate([weight_own, weight_other], 1) * gram**3
    mine = lax.broadcasted_iota(jnp.int32, coupling.shape, 0) + chip * owned
    here = lax.broadcasted_iota(jnp.int32, coupling.shape, 1) == mine
    diagonal = jnp.sum(jnp.where(here, coupling, 0.0), 1, keepdims=True)
    model_term = (
        split_dot(coupling[:, :half_rows], own, ((1,), (0,)))
        + split_dot(coupling[:, half_rows:], other, ((1,), (0,)))
        + diagonal * (factors - narrow.astype(F32))
    )
    return 8.0 * model_term - 8.0 / total * cross_term


def solution(mesh):
    in_specs = (P("dp", "feat"), P("dp", "feat"), P(), P())
    out_specs = P("dp", "feat")
    return jax.shard_map(
        on_device, mesh=mesh, in_specs=in_specs, out_specs=out_specs, check_vma=False
    )
```

time: 249 us -> 104 us (0.42)
  waiting for transfers between devices: 205 us -> 42.4 us
  starting transfers between devices: 0.08 us -> 28.9 us
  matrix products: 27.7 us -> 0.84 us
  Pallas kernels: 0 us -> 14.1 us
  between operations: 13.8 us -> 0.95 us
  local copies, waits for them, and re-layouts: 1.24 us -> 12.4 us
  other arithmetic: 1.28 us -> 3.79 us
    psum x1 -> x0, waiting for transfers between devices: 77.8 us -> none  [on_device(): projection = lax.psum(partial_value, 'feat')]
    reduce_scatter x1 -> x0, waiting for transfers between devices: 77.5 us -> none  [on_device(): lax.psum_scatter(cross_sum, 'dp', scatter_dimension=0, tiled=True)]
    all_gather x1 -> x0, waiting for transfers between devices: 48.8 us -> none  [on_device(): gathered = lax.all_gather(factors, 'dp', axis=0, tiled=True)]
    dot_general x4, matrix products: 27.7 us -> 0.84 us  [split_dot(): lax.dot_general(jnp.concatenate([high, low], 0), right, (dims, ((), ())),...]
    ppermute x0 -> x12, waiting for transfers between devices: none -> 23.5 us  [the longest x10 22.4 us: feat_swap(): return lax.ppermute(x, ('dp', 'feat'), pairs)]
    all_to_all x0 -> x2, waiting for transfers between devices: none -> 19 us  [plane_exchange(): return lax.all_to_all(x, 'dp', 0, 0, axis_index_groups=PLANES, tiled=True)]
    ppermute x0 -> x12, starting transfers between devices: none -> 17.4 us  [the longest x10 17.3 us: feat_swap(): return lax.ppermute(x, ('dp', 'feat'), pairs)]
    pallas_call x0 -> x3, Pallas kernels: none -> 14.1 us  [the longest x2 8.79 us: cross(): pl.pallas_call(functools.partial(cross_kernel, add), grid_spec=pltpu.Pref...]
  transfers between devices with their start and end apart: 3 -> 14, of which waited for: 3 -> 10; matrix products, arithmetic and copies ran while one was open for 1% -> 5% of each run, Pallas kernels for 0% -> 4%
where the time goes in v1:
time: 104 us; the launch traced here: 103 us
  waiting for transfers between devices  42.4 us (41%)
  starting transfers between devices  28.9 us (28%)
  Pallas kernels  14.1 us (14%)
  local copies, waits for them, and re-layouts  12.4 us (12%)
  other arithmetic  3.79 us (4%)
    ppermute x10, waiting for transfers between devices, feat_swap(): return lax.ppermute(x, ('dp', 'feat'), pairs)  22.4 us
    all_to_all x2, waiting for transfers between devices, plane_exchange(): return lax.all_to_all(x, 'dp', 0, 0, axis_index_groups=PLANES, tiled=True)  19 us
    ppermute x10, starting transfers between devices, feat_swap(): return lax.ppermute(x, ('dp', 'feat'), pairs)  17.3 us
    all_to_all x2, starting transfers between devices, plane_exchange(): return lax.all_to_all(x, 'dp', 0, 0, axis_index_groups=PLANES, tiled=True)  11.5 us
    unnamed x14, local copies, waits for them, and re-layouts  9.17 us
    pallas_call x2, Pallas kernels, cross(): pl.pallas_call(functools.partial(cross_kernel, add), grid_spec=pltpu.Pref...  8.79 us
    pallas_call x1, Pallas kernels, project(): pl.pallas_call(projection_kernel, grid_spec=pltpu.PrefetchScalarGridSpec(...  5.28 us
  transfers between devices with their start and end apart: 14, of which 10 were waited for; matrix products, arithmetic and copies ran while one was open for 5% of the time, Pallas kernels for 4%

profile of v1, /device:TPU:0, one launch (start us, length us, event | category | flops | bytes accessed | tf_op | source)
XLA Modules:
  0.0 103.3 jit_solution(4703611553303088750)
XLA Ops:
  0.0 0.9 fusion.12
  0.9 0.9 tile.2
  1.8 8.0 %all-to-all-start = ((bf16[16,8,2048]{2,1,0:T(8,128)(2,1)}), bf16[16,8,2048]{2,1,0:T(8,128)(2,1)S(1)}, u32[]{:S(2)}, u32[]{:S(2)}) async-start(bf16[16,8,2048]{2,1,0:T(8,128)(2,1)} %tile.2), calls=%async_computation | async-start | bytes 1048576 | tf_op jit(solution)/shard_map/all_to_all | solution.py:38
  9.8 0.8 reshape.26
  10.6 0.1 reshape.27
  10.7 1.3 %dynamic_slice.21 = s32[1]{0:T(128)} dynamic-slice(s32[32]{0:T(128)} %param.7, s32[]{:T(128)S(6)} %select_n.46), dynamic_slice_sizes={1} | dynamic-slice | bytes 12 | tf_op jit(solution)/shard_map/dynamic_slice | solution.py:165
  12.0 9.3 %all-to-all-done = bf16[16,8,2048]{2,1,0:T(8,128)(2,1)S(1)} async-done(((bf16[16,8,2048]{2,1,0:T(8,128)(2,1)}), bf16[16,8,2048]{2,1,0:T(8,128)(2,1)S(1)}, u32[]{:S(2)}, u32[]{:S(2)}) %all-to-all-start) | async-done | bytes 524320 | tf_op jit(solution)/shard_map/all_to_all | solution.py:38
  21.3 0.1 pad_add_fusion.order
  21.4 0.1 dynamic-slice_bitcast_fusion
  21.5 0.7 fusion.15
  22.1 1.1 %collective-permute-done.other = bf16[128,2048]{1,0:T(8,128)(2,1)S(1)} collective-permute-done((bf16[128,2048]{1,0:T(8,128)(2,1)S(1)}, bf16[128,2048]{1,0:T(8,128)(2,1)S(1)}, u32[]{:S(2)}, u32[]{:S(2)}) %collective-permute-start) | collective-permute-done | bytes 524320 | tf_op jit(solution)/shard_map/ppermute | solution.py:34
  23.2 4.6 %copy-done = bf16[3072,2048]{1,0:T(8,128)(2,1)S(1)} copy-done((bf16[3072,2048]{1,0:T(8,128)(2,1)S(1)}, bf16[3072,2048]{1,0:T(8,128)(2,1)}, u32[]{:S(2)}) %copy-start) | copy-done | bytes 12582936
  27.8 5.3 %projection.1 = (bf16[64,3072]{1,0:T(8,128)(2,1)S(1)}, f32[64,3072]{1,0:T(8,128)S(1)}, bf16[64,3072]{1,0:T(8,128)(2,1)S(1)}, f32[64,3072]{1,0:T(8,128)S(1)}) custom-call(s32[4]{0:T(128)S(1)} %pad_add_fusion.order, bf16[128,2048]{1,0:T(8,128)(2,1)S(1)} %collective-permute-done.other, bf16[128,2048]{1,0:T(8,128)(2,1)S(1)} %bitcast.24, ...), custom_call_target="tpu_custom_call" | custom-call | flops 3221225472 | bytes 12582912 | tf_op jit(solution)/shard_map/projection/pallas_call | solution.py:65
  33.1 1.7 %collective-permute-start.7 = (bf16[64,3072]{1,0:T(8,128)(2,1)S(1)}, bf16[64,3072]{1,0:T(8,128)(2,1)S(1)}, u32[]{:S(2)}, u32[]{:S(2)}) collective-permute-start(bf16[64,3072]{1,0:T(8,128)(2,1)S(1)} %get-tuple-element.12), channel_id=1, source_target_pairs={{0,1},{1,0},{2,3},{3,2},{4,7},{5,6},{6,5},{7,4},{8,9},{9,8},{10,11... | collective-permute-start | bytes 1179656 | tf_op jit(solution)/shard_map/ppermute | solution.py:30
  34.7 0.2 fusion.14
  35.0 0.5 collective-permute-start.3
  35.5 5.5 %collective-permute-done.7 = bf16[64,3072]{1,0:T(8,128)(2,1)S(1)} collective-permute-done((bf16[64,3072]{1,0:T(8,128)(2,1)S(1)}, bf16[64,3072]{1,0:T(8,128)(2,1)S(1)}, u32[]{:S(2)}, u32[]{:S(2)}) %collective-permute-start.7) | collective-permute-done | bytes 393248 | tf_op jit(solution)/shard_map/ppermute | solution.py:30
  40.9 0.1 convert_element_type.84
  41.1 3.1 %collective-permute-start.8 = (bf16[32,3072]{1,0:T(8,128)(2,1)S(1)}, bf16[32,3072]{1,0:T(8,128)(2,1)S(1)}, u32[]{:S(2)}, u32[]{:S(2)}) collective-permute-start(bf16[32,3072]{1,0:T(8,128)(2,1)S(1)} %fusion.4), channel_id=1, source_target_pairs={{0,3},{1,2},{2,1},{3,0},{4,5},{5,4},{6,7},{7,6},{8,11},{9,10},{10,... | collective-permute-start | bytes 589832 | tf_op jit(solution)/shard_map/ppermute | solution.py:30
  44.2 2.2 %collective-permute-done.3 = bf16[64,3072]{1,0:T(8,128)(2,1)S(1)} collective-permute-done((bf16[64,3072]{1,0:T(8,128)(2,1)S(1)}, bf16[64,3072]{1,0:T(8,128)(2,1)S(1)}, u32[]{:S(2)}, u32[]{:S(2)}) %collective-permute-start.3) | collective-permute-done | bytes 393248 | tf_op jit(solution)/shard_map/ppermute | solution.py:30
  46.3 0.1 convert_element_type.80
  46.4 3.1 %collective-permute-start.4 = (bf16[32,3072]{1,0:T(8,128)(2,1)S(1)}, bf16[32,3072]{1,0:T(8,128)(2,1)S(1)}, u32[]{:S(2)}, u32[]{:S(2)}) collective-permute-start(bf16[32,3072]{1,0:T(8,128)(2,1)S(1)} %fusion.6), channel_id=1, source_target_pairs={{0,3},{1,2},{2,1},{3,0},{4,5},{5,4},{6,7},{7,6},{8,11},{9,10},{10,... | collective-permute-start | bytes 589832 | tf_op jit(solution)/shard_map/ppermute | solution.py:30
  49.5 0.2 fusion.13
  49.7 3.6 %collective-permute-done.4 = bf16[32,3072]{1,0:T(8,128)(2,1)S(1)} collective-permute-done((bf16[32,3072]{1,0:T(8,128)(2,1)S(1)}, bf16[32,3072]{1,0:T(8,128)(2,1)S(1)}, u32[]{:S(2)}, u32[]{:S(2)}) %collective-permute-start.4) | collective-permute-done | bytes 196640 | tf_op jit(solution)/shard_map/ppermute | solution.py:30
  53.4 0.2 fusion.3
  53.6 3.1 %collective-permute-start.9 = (bf16[32,3072]{1,0:T(8,128)(2,1)S(1)}, bf16[32,3072]{1,0:T(8,128)(2,1)S(1)}, u32[]{:S(2)}, u32[]{:S(2)}) collective-permute-start(bf16[32,3072]{1,0:T(8,128)(2,1)S(1)} %get-tuple-element.21.cubes0), channel_id=1, source_target_pairs={{0,3},{1,2},{2,1},{3,0},{4,5},{5,4},{6,7},{7,6},{8,11},{9,10},{10,... | collective-permute-start | bytes 589832 | tf_op jit(solution)/shard_map/ppermute | solution.py:30
  56.7 0.2 collective-permute-start.5
  56.9 5.4 %collective-permute-done.9.cubes1 = bf16[32,3072]{1,0:T(8,128)(2,1)S(1)} collective-permute-done((bf16[32,3072]{1,0:T(8,128)(2,1)S(1)}, bf16[32,3072]{1,0:T(8,128)(2,1)S(1)}, u32[]{:S(2)}, u32[]{:S(2)}) %collective-permute-start.9) | collective-permute-done | bytes 196640 | tf_op jit(solution)/shard_map/ppermute | solution.py:30
  62.4 0.4 collective-permute-start.10
  62.8 1.7 %collective-permute-start.1 = (f32[8,256]{1,0:T(8,128)S(1)}, f32[8,256]{1,0:T(8,128)S(1)}, u32[]{:S(2)}, u32[]{:S(2)}) collective-permute-start(f32[8,256]{1,0:T(8,128)S(1)} %pad_maximum_fusion.5), channel_id=1, source_target_pairs={{0,1},{1,0},{2,3},{3,2},{4,7},{5,6},{6,5},{7,4},{8,9},{9,8},{10,11... | collective-permute-start | bytes 24584 | tf_op jit(solution)/shard_map/ppermute | solution.py:30
  64.5 2.1 %collective-permute-done.5.cubes1 = bf16[32,3072]{1,0:T(8,128)(2,1)S(1)} collective-permute-done((bf16[32,3072]{1,0:T(8,128)(2,1)S(1)}, bf16[32,3072]{1,0:T(8,128)(2,1)S(1)}, u32[]{:S(2)}, u32[]{:S(2)}) %collective-permute-start.5) | collective-permute-done | bytes 196640 | tf_op jit(solution)/shard_map/ppermute | solution.py:30
  66.6 0.4 collective-permute-start.6
  67.1 3.2 %collective-permute-done.10.cubes2 = bf16[64,3072]{1,0:T(8,128)(2,1)S(1)} collective-permute-done((bf16[64,3072]{1,0:T(8,128)(2,1)S(1)}, bf16[64,3072]{1,0:T(8,128)(2,1)S(1)}, u32[]{:S(2)}, u32[]{:S(2)}) %collective-permute-start.10) | collective-permute-done | bytes 393248 | tf_op jit(solution)/shard_map/ppermute | solution.py:30
  70.3 4.1 %cross.2 = bf16[128,2048]{1,0:T(8,128)(2,1)S(1)} custom-call(s32[4]{0:T(128)S(1)} %pad_add_fusion.order, bf16[32,3072]{1,0:T(8,128)(2,1)S(1)} %get-tuple-element.21.cubes0, bf16[32,3072]{1,0:T(8,128)(2,1)S(1)} %collective-permute-done.9.cubes1, bf16[64,3072]{1,0:T(8,128)(2,1)S(1)} %collective-permute-done.10.cubes2, bf16[3072,2048]{1,0:T(8,128)(2,1)S(1)} %bitcast.22), custom_call_target="tpu_custom_call" | custom-call | flops 1610612736 | bytes 12582912 | tf_op jit(solution)/shard_map/cross/pallas_call | solution.py:116
  74.3 0.1 collective-permute-start.11
  74.5 3.1 %collective-permute-start.2 = (f32[8,256]{1,0:T(8,128)S(1)}, f32[8,256]{1,0:T(8,128)S(1)}, u32[]{:S(2)}, u32[]{:S(2)}) collective-permute-start(f32[8,256]{1,0:T(8,128)S(1)} %fusion.31), channel_id=1, source_target_pairs={{0,3},{1,2},{2,1},{3,0},{4,5},{5,4},{6,7},{7,6},{8,11},{9,10},{10,... | collective-permute-start | bytes 24584 | tf_op jit(solution)/shard_map/ppermute | solution.py:30
  77.6 0.1 dynamic-slice_bitcast_fusion.2
  77.7 0.6 reduce_sum.28
  79.0 0.4 collective-permute-done.2
  79.4 0.2 select_reduce_fusion
  79.6 4.6 %copy-done.1 = bf16[3072,2048]{1,0:T(8,128)(2,1)S(1)} copy-done((bf16[3072,2048]{1,0:T(8,128)(2,1)S(1)}, bf16[3072,2048]{1,0:T(8,128)(2,1)}, u32[]{:S(2)}) %copy-start.1) | copy-done | bytes 12582936
  84.2 4.7 %cross.3 = bf16[128,2048]{1,0:T(8,128)(2,1)} custom-call(s32[4]{0:T(128)S(1)} %pad_add_fusion.order, bf16[32,3072]{1,0:T(8,128)(2,1)S(1)} %get-tuple-element.22.cubes0, bf16[32,3072]{1,0:T(8,128)(2,1)S(1)} %collective-permute-done.5.cubes1, bf16[64,3072]{1,0:T(8,128)(2,1)S(1)} %collective-permute-done.6.cubes2, bf16[3072,2048]{1,0:T(8,128)(2,1)S(1)} %copy-done.1, ...), custom_call_target="tpu_custom_call" | custom-call | flops 1610612736 | bytes 12582912 | tf_op jit(solution)/shard_map/cross/pallas_call | solution.py:116
  88.9 3.6 %all-to-all-start.1 = ((bf16[16,8,2048]{2,1,0:T(8,128)(2,1)}), bf16[16,8,2048]{2,1,0:T(8,128)(2,1)S(1)}, u32[]{:S(2)}, u32[]{:S(2)}) async-start(bf16[16,8,2048]{2,1,0:T(8,128)(2,1)} %bitcast.11), calls=%async_computation.1 | async-start | bytes 1048576 | tf_op jit(solution)/shard_map/all_to_all | solution.py:38
  92.5 0.2 fusion.21
  92.7 0.2 fusion.17
  92.9 9.7 %all-to-all-done.1 = bf16[16,8,2048]{2,1,0:T(8,128)(2,1)S(1)} async-done(((bf16[16,8,2048]{2,1,0:T(8,128)(2,1)}), bf16[16,8,2048]{2,1,0:T(8,128)(2,1)S(1)}, u32[]{:S(2)}, u32[]{:S(2)}) %all-to-all-start.1) | async-done | bytes 524320 | tf_op jit(solution)/shard_map/all_to_all | solution.py:38
  102.5 0.1 convert_reduce_fusion
  102.6 0.7 fusion.11
  (31 shorter events, 0.2 us)
Async XLA Ops:
  1.8 19.5 %all-to-all-start = ((bf16[16,8,2048]{2,1,0:T(8,128)(2,1)}), bf16[16,8,2048]{2,1,0:T(8,128)(2,1)S(1)}, u32[]{:S(2)}, u32[]{:S(2)}) async-start(bf16[16,8,2048]{2,1,0:T(8,128)(2,1)} %tile.2), calls=%async_computation | async-start | bytes 1048576 | tf_op jit(solution)/shard_map/all_to_all | solution.py:38
  21.3 1.9 %collective-permute-start = (bf16[128,2048]{1,0:T(8,128)(2,1)S(1)}, bf16[128,2048]{1,0:T(8,128)(2,1)S(1)}, u32[]{:S(2)}, u32[]{:S(2)}) collective-permute-start(bf16[128,2048]{1,0:T(8,128)(2,1)S(1)} %bitcast.23), channel_id=1, source_target_pairs={{0,4},{4,0},{8,12},{12,8},{16,20},{20,16},{24,28},{28,24},{32,36},... | collective-permute-start | bytes 1572872 | tf_op jit(solution)/shard_map/ppermute | solution.py:34
  23.2 4.6 %copy-start = (bf16[3072,2048]{1,0:T(8,128)(2,1)S(1)}, bf16[3072,2048]{1,0:T(8,128)(2,1)}, u32[]{:S(2)}) copy-start(bf16[3072,2048]{1,0:T(8,128)(2,1)} %samples.5) | copy-start | bytes 37748740
  27.8 42.5 %slice-start = ((s8[12582912]{0:T(1024)(128)(4,1)}), s8[4194304]{0:T(1024)(128)(4,1)S(1)}, s32[]{:S(2)}) async-start(s8[12582912]{0:T(1024)(128)(4,1)} %bitcast.21), calls=%async_computation.2 | async-start | bytes 8388608
  27.8 42.5 %slice-start.1 = ((s8[12582912]{0:T(1024)(128)(4,1)}), s8[4194304]{0:T(1024)(128)(4,1)S(1)}, s32[]{:S(2)}) async-start(s8[12582912]{0:T(1024)(128)(4,1)} %bitcast.21), calls=%async_computation.3 | async-start | bytes 8388608
  33.1 44.6 %copy-start.3 = (s32[32]{0:T(128)S(1)}, s32[32]{0:T(128)}, u32[]{:S(2)}) copy-start(s32[32]{0:T(128)} %param.7) | copy-start | bytes 388
  33.1 7.9 %collective-permute-start.7 = (bf16[64,3072]{1,0:T(8,128)(2,1)S(1)}, bf16[64,3072]{1,0:T(8,128)(2,1)S(1)}, u32[]{:S(2)}, u32[]{:S(2)}) collective-permute-start(bf16[64,3072]{1,0:T(8,128)(2,1)S(1)} %get-tuple-element.12), channel_id=1, source_target_pairs={{0,1},{1,0},{2,3},{3,2},{4,7},{5,6},{6,5},{7,4},{8,9},{9,8},{10,11... | collective-permute-start | bytes 1179656 | tf_op jit(solution)/shard_map/ppermute | solution.py:30
  35.0 11.3 %collective-permute-start.3 = (bf16[64,3072]{1,0:T(8,128)(2,1)S(1)}, bf16[64,3072]{1,0:T(8,128)(2,1)S(1)}, u32[]{:S(2)}, u32[]{:S(2)}) collective-permute-start(bf16[64,3072]{1,0:T(8,128)(2,1)S(1)} %get-tuple-element.10), channel_id=1, source_target_pairs={{0,1},{1,0},{2,3},{3,2},{4,7},{5,6},{6,5},{7,4},{8,9},{9,8},{10,11... | collective-permute-start | bytes 1179656 | tf_op jit(solution)/shard_map/ppermute | solution.py:30
  41.0 29.3 %slice-start.2 = ((s8[12582912]{0:T(1024)(128)(4,1)}), s8[4194304]{0:T(1024)(128)(4,1)S(1)}, s32[]{:S(2)}) async-start(s8[12582912]{0:T(1024)(128)(4,1)} %bitcast.21), calls=%async_computation.4 | async-start | bytes 8388608
  41.1 8.7 %collective-permute-start.8 = (bf16[32,3072]{1,0:T(8,128)(2,1)S(1)}, bf16[32,3072]{1,0:T(8,128)(2,1)S(1)}, u32[]{:S(2)}, u32[]{:S(2)}) collective-permute-start(bf16[32,3072]{1,0:T(8,128)(2,1)S(1)} %fusion.4), channel_id=1, source_target_pairs={{0,3},{1,2},{2,1},{3,0},{4,5},{5,4},{6,7},{7,6},{8,11},{9,10},{10,... | collective-permute-start | bytes 589832 | tf_op jit(solution)/shard_map/ppermute | solution.py:30
  46.4 7.0 %collective-permute-start.4 = (bf16[32,3072]{1,0:T(8,128)(2,1)S(1)}, bf16[32,3072]{1,0:T(8,128)(2,1)S(1)}, u32[]{:S(2)}, u32[]{:S(2)}) collective-permute-start(bf16[32,3072]{1,0:T(8,128)(2,1)S(1)} %fusion.6), channel_id=1, source_target_pairs={{0,3},{1,2},{2,1},{3,0},{4,5},{5,4},{6,7},{7,6},{8,11},{9,10},{10,... | collective-permute-start | bytes 589832 | tf_op jit(solution)/shard_map/ppermute | solution.py:30
  53.6 8.7 %collective-permute-start.9 = (bf16[32,3072]{1,0:T(8,128)(2,1)S(1)}, bf16[32,3072]{1,0:T(8,128)(2,1)S(1)}, u32[]{:S(2)}, u32[]{:S(2)}) collective-permute-start(bf16[32,3072]{1,0:T(8,128)(2,1)S(1)} %get-tuple-element.21.cubes0), channel_id=1, source_target_pairs={{0,3},{1,2},{2,1},{3,0},{4,5},{5,4},{6,7},{7,6},{8,11},{9,10},{10,... | collective-permute-start | bytes 589832 | tf_op jit(solution)/shard_map/ppermute | solution.py:30
  56.7 9.9 %collective-permute-start.5 = (bf16[32,3072]{1,0:T(8,128)(2,1)S(1)}, bf16[32,3072]{1,0:T(8,128)(2,1)S(1)}, u32[]{:S(2)}, u32[]{:S(2)}) collective-permute-start(bf16[32,3072]{1,0:T(8,128)(2,1)S(1)} %get-tuple-element.22.cubes0), channel_id=1, source_target_pairs={{0,3},{1,2},{2,1},{3,0},{4,5},{5,4},{6,7},{7,6},{8,11},{9,10},{10,... | collective-permute-start | bytes 589832 | tf_op jit(solution)/shard_map/ppermute | solution.py:30
  62.4 7.9 %collective-permute-start.10 = (bf16[64,3072]{1,0:T(8,128)(2,1)S(1)}, bf16[64,3072]{1,0:T(8,128)(2,1)S(1)}, u32[]{:S(2)}, u32[]{:S(2)}) collective-permute-start(bf16[64,3072]{1,0:T(8,128)(2,1)S(1)} %pad_maximum_fusion.1), channel_id=1, source_target_pairs={{0,1},{1,0},{2,3},{3,2},{4,7},{5,6},{6,5},{7,4},{8,9},{9,8},{10,11... | collective-permute-start | bytes 1179656 | tf_op jit(solution)/shard_map/ppermute | solution.py:30
  62.8 11.6 %collective-permute-start.1 = (f32[8,256]{1,0:T(8,128)S(1)}, f32[8,256]{1,0:T(8,128)S(1)}, u32[]{:S(2)}, u32[]{:S(2)}) collective-permute-start(f32[8,256]{1,0:T(8,128)S(1)} %pad_maximum_fusion.5), channel_id=1, source_target_pairs={{0,1},{1,0},{2,3},{3,2},{4,7},{5,6},{6,5},{7,4},{8,9},{9,8},{10,11... | collective-permute-start | bytes 24584 | tf_op jit(solution)/shard_map/ppermute | solution.py:30
  66.6 36.0 %copy-start.2 = (f32[8,2048]{1,0:T(8,128)S(1)}, f32[8,2048]{1,0:T(8,128)}, u32[]{:S(2)}) copy-start(f32[8,2048]{1,0:T(8,128)} %param.5) | copy-start | bytes 196612
  66.6 13.0 %collective-permute-start.6 = (bf16[64,3072]{1,0:T(8,128)(2,1)S(1)}, bf16[64,3072]{1,0:T(8,128)(2,1)S(1)}, u32[]{:S(2)}, u32[]{:S(2)}) collective-permute-start(bf16[64,3072]{1,0:T(8,128)(2,1)S(1)} %pad_maximum_fusion), channel_id=1, source_target_pairs={{0,1},{1,0},{2,3},{3,2},{4,7},{5,6},{6,5},{7,4},{8,9},{9,8},{10,11... | collective-permute-start | bytes 1179656 | tf_op jit(solution)/shard_map/ppermute | solution.py:30
  74.3 5.2 %collective-permute-start.11 = (bf16[128,2048]{1,0:T(8,128)(2,1)S(1)}, bf16[128,2048]{1,0:T(8,128)(2,1)S(1)}, u32[]{:S(2)}, u32[]{:S(2)}) collective-permute-start(bf16[128,2048]{1,0:T(8,128)(2,1)S(1)} %cross.2), channel_id=1, source_target_pairs={{0,4},{4,0},{8,12},{12,8},{16,20},{20,16},{24,28},{28,24},{32,36},... | collective-permute-start | bytes 1572872 | tf_op jit(solution)/shard_map/ppermute | solution.py:34
  74.5 4.9 %collective-permute-start.2 = (f32[8,256]{1,0:T(8,128)S(1)}, f32[8,256]{1,0:T(8,128)S(1)}, u32[]{:S(2)}, u32[]{:S(2)}) collective-permute-start(f32[8,256]{1,0:T(8,128)S(1)} %fusion.31), channel_id=1, source_target_pairs={{0,3},{1,2},{2,1},{3,0},{4,5},{5,4},{6,7},{7,6},{8,11},{9,10},{10,... | collective-permute-start | bytes 24584 | tf_op jit(solution)/shard_map/ppermute | solution.py:30
  79.6 4.6 %copy-start.1 = (bf16[3072,2048]{1,0:T(8,128)(2,1)S(1)}, bf16[3072,2048]{1,0:T(8,128)(2,1)}, u32[]{:S(2)}) copy-start(bf16[3072,2048]{1,0:T(8,128)(2,1)} %samples.5) | copy-start | bytes 37748740
  88.9 13.6 %all-to-all-start.1 = ((bf16[16,8,2048]{2,1,0:T(8,128)(2,1)}), bf16[16,8,2048]{2,1,0:T(8,128)(2,1)S(1)}, u32[]{:S(2)}, u32[]{:S(2)}) async-start(bf16[16,8,2048]{2,1,0:T(8,128)(2,1)} %bitcast.11), calls=%async_computation.1 | async-start | bytes 1048576 | tf_op jit(solution)/shard_map/all_to_all | solution.py:38

commit v2 on v0

v2 whole, which is shorter than its diff:
```python
import functools

import jax
import jax.numpy as jnp
from jax import lax
from jax.experimental import pallas as pl
from jax.experimental.pallas import tpu as pltpu
from jax.sharding import PartitionSpec as P

BF16 = jnp.bfloat16
F32 = jnp.float32
N_DP = 32
N_FEAT = 4
CHIPS = N_DP // 2
PARTS = 2
TILES = (768, 768)
LOADS = 2
PLANES = [[2 * chip + core for chip in range(CHIPS)] for core in range(2)]
VMEM = pl.BlockSpec(memory_space=pltpu.VMEM)
SMEM = pl.BlockSpec(memory_space=pltpu.SMEM)
ANY = pl.BlockSpec(memory_space=pl.ANY)
PARAMS = pltpu.CompilerParams(vmem_limit_bytes=8 << 20)


def in_hbm(array):
    return pltpu.with_memory_space_constraint(array, pltpu.HBM)


def in_vmem(array):
    return pltpu.with_memory_space_constraint(array, pltpu.VMEM)


def partner_first(core, y):
    return y ^ 1 if core == 0 else 3 - y


def partner_second(core, y):
    return 3 - y if core == 0 else y ^ 1


PARTNERS = (partner_first, partner_second)
ALTERNATE = False


def feat_swap(x, partner):
    pairs = []
    for dp in range(N_DP):
        for y in range(N_FEAT):
            pairs.append((dp * N_FEAT + y, dp * N_FEAT + partner(dp % 2, y)))
    return lax.ppermute(x, ("dp", "feat"), pairs)


def core_swap(x):
    return lax.ppermute(x, "dp", [(i, i ^ 1) for i in range(N_DP)])


def plane_exchange(x):
    return lax.all_to_all(x, "dp", 0, 0, axis_index_groups=PLANES, tiled=True)


def spread_kernel(factors, out):
    width = out.shape[1]
    block = jnp.concatenate([factors[:, :width], factors[:, width:]], 0).astype(BF16)
    for chip in range(CHIPS):
        out[pl.ds(16 * chip, 16), :] = block


def spread(factors):
    return pl.pallas_call(
        spread_kernel,
        in_specs=[VMEM],
        out_specs=VMEM,
        out_shape=jax.ShapeDtypeStruct((16 * CHIPS, factors.shape[1] // 2), BF16),
        compiler_params=PARAMS,
        name="spread",
    )(in_hbm(factors))


def unpack(packed, out, top):
    for pair in range(CHIPS // 2):
        block = packed[pl.ds(32 * pair, 32), :].astype(F32)
        upper = jnp.concatenate([block[:8], block[8:16]], 1)
        lower = jnp.concatenate([block[16:24], block[24:]], 1)
        out[pl.ds(top + 16 * pair, 16), :] = jnp.concatenate([upper, lower], 0).astype(BF16)


def parts_of(value):
    high = value.astype(BF16)
    return high, (value - high.astype(F32)).astype(BF16)


def gram_message(gram):
    return jnp.concatenate([part.astype(F32) for part in parts_of(gram)], 0).astype(BF16)


def gram_of(message):
    value = message.astype(F32)
    return value[:8] + value[8:16]


def load_kernel(samples, near, sem):
    rows = near.shape[0] // LOADS
    copies = []
    for i in range(LOADS):
        part = pl.ds(i * rows, rows)
        copies.append(pltpu.make_async_copy(samples.at[part, :], near.at[part, :], sem.at[i]))
        copies[-1].start()
    for copy in copies:
        copy.wait()


def load(samples):
    shape = (samples.shape[0] // PARTS, samples.shape[1])
    return pl.pallas_call(
        load_kernel,
        in_specs=[ANY],
        out_specs=VMEM,
        out_shape=pltpu.VMEM(shape, samples.dtype),
        scratch_shapes=[pltpu.SemaphoreType.DMA((LOADS,))],
        compiler_params=PARAMS,
        cost_estimate=pl.CostEstimate(
            flops=0, bytes_accessed=4 * shape[0] * shape[1], transcendentals=0
        ),
        name="load",
    )(in_hbm(samples))


def arrange(scalars, rows, scratch, pattern):
    block = rows.shape[0] // 4
    for i in range(4):
        at = pl.multiple_of(scalars[4 * pattern + i] * block, block)
        scratch[i * block : (i + 1) * block, :] = rows[pl.ds(at, block), :]


def project_part(scalars, scratch, near, sent, kept, top):
    half = kept.shape[0]
    start = 0
    for tile in TILES:
        rows = slice(start, start + tile)
        value = lax.dot_general(
            scratch[...], near[rows, :], (((1,), (1,)), ((), ())), preferred_element_type=F32
        )
        slot = top + start + lax.broadcasted_iota(jnp.int32, (1, tile), 1)
        value = jnp.where(slot < scalars[8], value, 0.0)
        sent[:, rows] = value[:half].astype(BF16)
        kept[:, rows] = value[half:]
        start += tile


def first_kernel(scalars, packed_other, packed_own, factors, near, samples, *refs):
    sent, kept, rows, gram, later, scratch, mine, sem, sems = refs
    first = pltpu.make_async_copy(factors, mine, sem)
    first.start()
    slots = kept.shape[1]
    copies = []
    for i in range(LOADS):
        part = pl.ds(i * slots // LOADS, slots // LOADS)
        rest = pl.ds(slots + i * slots // LOADS, slots // LOADS)
        copies.append(
            pltpu.make_async_copy(samples.at[rest, :], later.at[part, :], sems.at[i])
        )
        copies[-1].start()
    unpack(packed_other, rows, 0)
    unpack(packed_own, rows, rows.shape[0] // 2)
    arrange(scalars, rows, scratch, 0)
    first.wait()
    value = gram_of(
        lax.dot_general(
            gram_message(mine[...]),
            rows[...],
            (((1,), (1,)), ((), ())),
            preferred_element_type=F32,
        )
    )
    gram[...] = value
    sent[16:, slots:] = jnp.zeros((sent.shape[0] - 16, value.shape[1]), BF16)
    sent[:16, slots:] = gram_message(value)
    project_part(scalars, scratch, near, sent, kept, 0)
    for copy in copies:
        copy.wait()


def second_kernel(scalars, rows, near, sent, kept, scratch, *, pattern):
    arrange(scalars, rows, scratch, pattern)
    project_part(scalars, scratch, near, sent, kept, kept.shape[1])


def estimate(slots, depth, rows):
    return pl.CostEstimate(
        flops=2 * slots * depth * rows, bytes_accessed=2 * slots * depth, transcendentals=0
    )


def project_first(scalars, packed_other, packed_own, factors, near, samples):
    slots, depth = near.shape
    rows = packed_own.shape[0]
    return pl.pallas_call(
        first_kernel,
        in_specs=[SMEM, VMEM, VMEM, ANY, VMEM, ANY],
        out_specs=[VMEM] * 5,
        out_shape=[
            jax.ShapeDtypeStruct((rows // 2, slots + rows), BF16),
            jax.ShapeDtypeStruct((rows // 2, slots), F32),
            jax.ShapeDtypeStruct((rows, depth), BF16),
            jax.ShapeDtypeStruct((factors.shape[0], rows), F32),
            pltpu.VMEM((slots, depth), BF16),
        ],
        scratch_shapes=[
            pltpu.VMEM((rows, depth), BF16),
            pltpu.VMEM(factors.shape, F32),
            pltpu.SemaphoreType.DMA,
            pltpu.SemaphoreType.DMA((LOADS,)),
        ],
        compiler_params=PARAMS,
        cost_estimate=estimate(slots, depth, rows),
        name="project_first",
    )(scalars, packed_other, packed_own, in_hbm(factors), in_vmem(near), in_hbm(samples))


def project_second(scalars, rows, near):
    slots, depth = near.shape
    half = rows.shape[0] // 2
    return pl.pallas_call(
        functools.partial(second_kernel, pattern=1 if ALTERNATE else 0),
        in_specs=[SMEM, VMEM, VMEM],
        out_specs=[VMEM] * 2,
        out_shape=[
            jax.ShapeDtypeStruct((half, slots), BF16),
            jax.ShapeDtypeStruct((half, slots), F32),
        ],
        scratch_shapes=[pltpu.VMEM(rows.shape, BF16)],
        compiler_params=PARAMS,
        cost_estimate=estimate(slots, depth, rows.shape[0]),
        name="project_second",
    )(scalars, rows, in_vmem(near))


def cross_kernel(scalars, mine, other, near, *refs, pattern, sides, add, tile):
    terms, refs = (refs[0] if add else None), refs[add:]
    outs, rows = refs[:-1], refs[-1]
    block = mine.shape[0] // 2
    half = 2 * block
    for i, piece in enumerate((other[:block], other[block:], mine[:block], mine[block:])):
        at = pl.multiple_of(scalars[4 * pattern + i] * block, block)
        rows[pl.ds(at, block), :] = piece
    width = outs[0].shape[1]
    first = sides[0] * half
    used = slice(first, first + len(sides) * half)

    @pl.loop(0, width // tile)
    def _(i):
        here = pl.ds(pl.multiple_of(i * tile, tile), tile)
        there = pl.ds(pl.multiple_of(width + i * tile, tile), tile)
        left, right = (
            jnp.dot(rows[used, :], near[:, at], preferred_element_type=F32) for at in (here, there)
        )
        for place, out in enumerate(outs):
            for chip in range(CHIPS):
                at = place * half + 8 * chip
                to = slice(16 * chip, 16 * chip + 16)
                value = jnp.concatenate([left[at : at + 8], right[at : at + 8]], 0)
                if add:
                    value = value + terms[to, here]
                out[to, here] = value.astype(out.dtype)


def cross(scalars, pieces, near, pattern, sides, out_type, term=None, tile=1024):
    slots, depth = near.shape
    rows = 2 * pieces[0].shape[0]
    add = term is not None
    out = jax.ShapeDtypeStruct((rows, depth // 2), out_type)
    return pl.pallas_call(
        functools.partial(cross_kernel, pattern=pattern, sides=sides, add=add, tile=tile),
        in_specs=[SMEM] + [VMEM] * (3 + add),
        out_specs=[VMEM] * len(sides),
        out_shape=[out] * len(sides),
        scratch_shapes=[pltpu.VMEM((rows, slots), BF16)],
        compiler_params=PARAMS,
        cost_estimate=estimate(slots, depth, rows),
        name="cross",
    )(scalars, *pieces, in_vmem(near), *([term] if add else []))


def split_dot(left, right, dims):
    both = lax.dot_general(
        jnp.concatenate(parts_of(left), 0), right, (dims, ((), ())), preferred_element_type=F32
    )
    return both[: left.shape[0]] + both[left.shape[0] :]


def on_device(samples, factors, weights, counts):
    owned, depth = factors.shape
    all_rows = weights.shape[0]
    half_rows = all_rows // 2
    block = all_rows // 4
    slots = samples.shape[0] // PARTS
    dp = lax.axis_index("dp")
    y = lax.axis_index("feat")
    core = lax.rem(dp, 2)
    chip = dp // 2
    first = jnp.where(core == 0, y ^ 1, 3 - y)
    second = jnp.where(core == 0, 3 - y, y ^ 1)
    across = lax.rem(y + 2, 4)
    order = []
    for one, two in ((first, second), (second, first)):
        for pair in ((one, across), (y, two)):
            order += [jnp.minimum(*pair), jnp.maximum(*pair)]
    scalars = jnp.stack(order + [counts[dp]]).astype(jnp.int32)
    total = jnp.sum(counts).astype(F32)
    by_core = weights.reshape(CHIPS, 2, owned).transpose(1, 0, 2).reshape(2, half_rows)
    weight_own = lax.dynamic_slice(by_core, (core, 0), (1, half_rows))[0]
    weight_other = lax.dynamic_slice(by_core, (1 - core, 0), (1, half_rows))[0]
    weight = jnp.concatenate([weight_other, weight_own])
    scales = []
    for part in range(PARTS):
        pattern = part if ALTERNATE else 0
        starts = [order[4 * pattern + i] * block for i in (2, 3)]
        scales.append(
            jnp.concatenate([lax.dynamic_slice(weight, (start,), (block,)) for start in starts])
        )
    weight_mine = lax.dynamic_slice(weight_own, (chip * owned,), (owned,))
    pairs = weight_mine[:, None] * weight[None, :]
    mine = lax.broadcasted_iota(jnp.int32, pairs.shape, 0) + half_rows + chip * owned
    here = (lax.broadcasted_iota(jnp.int32, pairs.shape, 1) == mine).astype(F32)
    factor = jnp.full((1, 1), 8.0, F32) / total[None, None]

    packed_own = plane_exchange(spread(factors))
    packed_own, scalars, scales, pairs, here, factor, samples = lax.optimization_barrier(
        (packed_own, scalars, scales, pairs, here, factor, samples)
    )
    near0 = load(samples)
    packed_other = core_swap(packed_own)

    sent0, kept0, rows, gram, near1 = project_first(
        scalars, packed_other, packed_own, factors, near0, samples
    )
    sent1, kept1 = project_second(scalars, rows, near1)

    def cubes_of(part, sent, kept, gram=None):
        pattern = part if ALTERNATE else 0
        one, two = PARTNERS[::-1] if pattern else PARTNERS
        got = feat_swap(sent, one)
        if gram is not None:
            gram = gram + gram_of(got[:16, slots:])
            got = got[:, :slots]
        value = kept + got.astype(F32)
        message = value.astype(BF16)
        if gram is not None:
            extra = jnp.pad(gram_message(gram), ((0, value.shape[0] - 16), (0, 0)))
            message = jnp.concatenate([message, extra], 1)
        passed = feat_swap(message, two)
        if gram is not None:
            gram = gram + gram_of(passed[:16, slots:])
            passed = passed[:, :slots]
        value = value + passed.astype(F32)
        cubes = (scales[part][:, None] * value**3).astype(BF16)
        return [cubes, feat_swap(cubes, one)], gram

    pieces0, gram = cubes_of(0, sent0, kept0, gram)
    pieces1, _ = cubes_of(1, sent1, kept1)
    other0, own0 = cross(scalars, pieces0, near0, 0, (0, 1), F32)
    pattern = 1 if ALTERNATE else 0
    (other1,) = cross(scalars, pieces1, near1, pattern, (0,), BF16, other0)
    (own1,) = cross(scalars, pieces1, near1, pattern, (1,), F32, own0)
    total_own = (own1 + core_swap(other1).astype(F32)).astype(BF16)
    blocks = plane_exchange(total_own).reshape(CHIPS, 2 * owned, depth // 2)
    cross_term = jnp.sum(blocks.astype(F32), axis=0)
    cross_term = jnp.concatenate([cross_term[:owned], cross_term[owned:]], 1)

    coupling = pairs * gram**3
    diagonal = jnp.sum(here * coupling, 1, keepdims=True)
    model_term = split_dot(coupling, rows, ((1,), (0,))) + diagonal * (
        factors - factors.astype(BF16).astype(F32)
    )
    return 8.0 * model_term - factor * cross_term


def solution(mesh):
    in_specs = (P("dp", "feat"), P("dp", "feat"), P(), P())
    out_specs = P("dp", "feat")
    return jax.shard_map(
        on_device, mesh=mesh, in_specs=in_specs, out_specs=out_specs, check_vma=False
    )
```

time: 249 us -> 82.5 us (0.33)
  waiting for transfers between devices: 205 us -> 33.9 us
  matrix products: 27.7 us -> 0.25 us
  starting transfers between devices: 0.08 us -> 22.3 us
  Pallas kernels: 0 us -> 17.1 us
  between operations: 13.8 us -> 1 us
  other arithmetic: 1.28 us -> 4.12 us
    psum x1 -> x0, waiting for transfers between devices: 77.8 us -> none  [on_device(): projection = lax.psum(partial_value, 'feat')]
    reduce_scatter x1 -> x0, waiting for transfers between devices: 77.5 us -> none  [on_device(): lax.psum_scatter(cross_sum, 'dp', scatter_dimension=0, tiled=True)]
    all_gather x1 -> x0, waiting for transfers between devices: 48.8 us -> none  [on_device(): gathered = lax.all_gather(factors, 'dp', axis=0, tiled=True)]
    dot_general x4 -> x1, matrix products: 27.7 us -> 0.25 us  [split_dot(): lax.dot_general(jnp.concatenate(parts_of(left), 0), right, (dims, ((), ()...]
    all_to_all x0 -> x2, waiting for transfers between devices: none -> 18 us  [plane_exchange(): return lax.all_to_all(x, 'dp', 0, 0, axis_index_groups=PLANES, tiled=True)]
    pallas_call x0 -> x7, Pallas kernels: none -> 17.1 us  [the longest x3 5.72 us: cross(): pl.pallas_call(functools.partial(cross_kernel, pattern=pattern, sides=sid...]
    ppermute x0 -> x8, waiting for transfers between devices: none -> 15.9 us  [the longest x6 15.7 us: feat_swap(): return lax.ppermute(x, ('dp', 'feat'), pairs)]
    all_to_all x0 -> x2, starting transfers between devices: none -> 11.5 us  [plane_exchange(): return lax.all_to_all(x, 'dp', 0, 0, axis_index_groups=PLANES, tiled=True)]
  transfers between devices with their start and end apart: 3 -> 10, of which waited for: 3 -> 9; matrix products, arithmetic and copies ran while one was open for 1% -> 7% of each run, Pallas kernels for 0% -> 11%
where the time goes in v2:
time: 82.5 us; the launch traced here: 81.7 us
  waiting for transfers between devices  33.9 us (41%)
  starting transfers between devices  22.3 us (27%)
  Pallas kernels  17.1 us (21%)
  other arithmetic  4.12 us (5%)
  local copies, waits for them, and re-layouts  2.92 us (4%)
  between operations  1 us (1%)
    all_to_all x2, waiting for transfers between devices, plane_exchange(): return lax.all_to_all(x, 'dp', 0, 0, axis_index_groups=PLANES, tiled=True)  18 us
    ppermute x6, waiting for transfers between devices, feat_swap(): return lax.ppermute(x, ('dp', 'feat'), pairs)  15.7 us
    all_to_all x2, starting transfers between devices, plane_exchange(): return lax.all_to_all(x, 'dp', 0, 0, axis_index_groups=PLANES, tiled=True)  11.5 us
    ppermute x6, starting transfers between devices, feat_swap(): return lax.ppermute(x, ('dp', 'feat'), pairs)  10.7 us
    pallas_call x3, Pallas kernels, cross(): pl.pallas_call(functools.partial(cross_kernel, pattern=pattern, sides=sid...  5.72 us
    pallas_call x1, Pallas kernels, project_first(): pl.pallas_call(first_kernel, in_specs=[SMEM, VMEM, VMEM, ANY, VMEM, ANY],...  4.51 us
    pallas_call x1, Pallas kernels, load(): pl.pallas_call(load_kernel, in_specs=[ANY], out_specs=VMEM, out_shape=plt...  2.86 us
    pallas_call x1, Pallas kernels, project_second(): pl.pallas_call(functools.partial(second_kernel, pattern=1 if ALTERNATE el...  2.37 us
  transfers between devices with their start and end apart: 10, of which 9 were waited for; matrix products, arithmetic and copies ran while one was open for 7% of the time, Pallas kernels for 11%

profile of v2, /device:TPU:0, one launch (start us, length us, event | category | flops | bytes accessed | tf_op | source)
XLA Modules:
  0.0 81.7 jit_solution(17997189849841853574)
XLA Ops:
  0.0 1.7 %spread.1 = bf16[256,1024]{1,0:T(8,128)(2,1)} custom-call(f32[8,2048]{1,0:T(8,128)} %factors.3), custom_call_target="tpu_custom_call" | custom-call | tf_op jit(solution)/shard_map/spread/pallas_call | solution.py:69
  1.7 8.0 %all-to-all-start = ((bf16[16,16,1024]{2,1,0:T(8,128)(2,1)}), bf16[16,16,1024]{2,1,0:T(8,128)(2,1)S(1)}, u32[]{:S(2)}, u32[]{:S(2)}) async-start(bf16[16,16,1024]{2,1,0:T(8,128)(2,1)} %bitcast), calls=%async_computation | async-start | bytes 1048576 | tf_op jit(solution)/shard_map/all_to_all | solution.py:58
  9.7 0.8 reshape.21
  10.5 0.1 reshape.22
  10.6 0.1 dynamic-slice_bitcast_fusion
  10.7 0.1 fusion.24
  10.8 0.1 pad_maximum_fusion.2
  10.9 1.4 %reduce_sum.27 = s32[]{:T(128)} reduce(s32[32]{0:T(128)} %param.7, s32[]{:T(128)} %constant.48.clone.1), dimensions={0}, to_apply=%region_0.1 | reduce | flops 31 | bytes 136 | tf_op jit(solution)/shard_map/reduce_sum | solution.py:309
  12.9 1.2 %dynamic_slice.20 = s32[1]{0:T(128)} dynamic-slice(s32[32]{0:T(128)} %param.7, s32[]{:T(128)S(6)} %select_n.37), dynamic_slice_sizes={1} | dynamic-slice | bytes 12 | tf_op jit(solution)/shard_map/dynamic_slice | solution.py:308
  14.2 0.6 stack.35.scalars
  14.8 0.1 fusion.19
  14.9 0.1 broadcast_multiply_fusion
  15.0 6.2 %all-to-all-done = bf16[16,16,1024]{2,1,0:T(8,128)(2,1)S(1)} async-done(((bf16[16,16,1024]{2,1,0:T(8,128)(2,1)}), bf16[16,16,1024]{2,1,0:T(8,128)(2,1)S(1)}, u32[]{:S(2)}, u32[]{:S(2)}) %all-to-all-start) | async-done | bytes 524320 | tf_op jit(solution)/shard_map/all_to_all | solution.py:58
  21.2 0.0 collective-permute-start
  21.2 2.9 %load.1.near = bf16[1536,2048]{1,0:T(8,128)(2,1)S(1)} custom-call(bf16[3072,2048]{1,0:T(8,128)(2,1)} %samples.1), custom_call_target="tpu_custom_call" | custom-call | bytes 12582912 | tf_op jit(solution)/shard_map/load/pallas_call | solution.py:114
  24.1 0.0 collective-permute-done.packed_other
  24.1 4.5 %project_first.1 = (bf16[128,1792]{1,0:T(8,128)(2,1)S(1)}, f32[128,1536]{1,0:T(8,128)S(1)}, bf16[256,2048]{1,0:T(8,128)(2,1)S(1)}, f32[8,256]{1,0:T(8,128)S(1)}, bf16[1536,2048]{1,0:T(8,128)(2,1)S(1)}) custom-call(s32[9]{0:T(128)S(1)} %stack.35.scalars, bf16[256,1024]{1,0:T(8,128)(2,1)S(1)} %collective-permute-done.packed_other, ...), custom_call_target="tpu_custom_call" | custom-call | flops 1610612736 | bytes 6291456 | tf_op jit(solution)/shard_map/project_first/pallas_call | solution.py:197
  28.6 1.7 %collective-permute-start.1 = (bf16[128,1792]{1,0:T(8,128)(2,1)S(1)}, bf16[128,1792]{1,0:T(8,128)(2,1)S(1)}, u32[]{:S(2)}, u32[]{:S(2)}) collective-permute-start(bf16[128,1792]{1,0:T(8,128)(2,1)S(1)} %get-tuple-element.27), channel_id=1, source_target_pairs={{0,1},{1,0},{2,3},{3,2},{4,7},{5,6},{6,5},{7,4},{8,9},{9,8},{10,11... | collective-permute-start | bytes 1376264 | tf_op jit(solution)/shard_map/ppermute | solution.py:50
  30.2 2.4 %project_second.1 = (bf16[128,1536]{1,0:T(8,128)(2,1)S(1)}, f32[128,1536]{1,0:T(8,128)S(1)}) custom-call(s32[9]{0:T(128)S(1)} %stack.35.scalars, bf16[256,2048]{1,0:T(8,128)(2,1)S(1)} %get-tuple-element.29.rows, bf16[1536,2048]{1,0:T(8,128)(2,1)S(1)} %get-tuple-element.33.near), custom_call_target="tpu_custom_call" | custom-call | flops 1610612736 | bytes 6291456 | tf_op jit(solution)/shard_map/project_second/pallas_call | solution.py:223
  32.6 0.5 collective-permute-start.3
  33.2 4.0 %collective-permute-done.1 = bf16[128,1792]{1,0:T(8,128)(2,1)S(1)} collective-permute-done((bf16[128,1792]{1,0:T(8,128)(2,1)S(1)}, bf16[128,1792]{1,0:T(8,128)(2,1)S(1)}, u32[]{:S(2)}, u32[]{:S(2)}) %collective-permute-start.1) | collective-permute-done | bytes 458784 | tf_op jit(solution)/shard_map/ppermute | solution.py:50
  37.2 0.1 fusion.4
  37.3 3.1 %collective-permute-start.2 = (bf16[128,1792]{1,0:T(8,128)(2,1)S(1)}, bf16[128,1792]{1,0:T(8,128)(2,1)S(1)}, u32[]{:S(2)}, u32[]{:S(2)}) collective-permute-start(bf16[128,1792]{1,0:T(8,128)(2,1)S(1)} %pad_maximum_fusion), channel_id=1, source_target_pairs={{0,3},{1,2},{2,1},{3,0},{4,5},{5,4},{6,7},{7,6},{8,11},{9,10},{10,... | collective-permute-start | bytes 1376264 | tf_op jit(solution)/shard_map/ppermute | solution.py:50
  40.4 1.7 %collective-permute-done.3 = bf16[128,1536]{1,0:T(8,128)(2,1)S(1)} collective-permute-done((bf16[128,1536]{1,0:T(8,128)(2,1)S(1)}, bf16[128,1536]{1,0:T(8,128)(2,1)S(1)}, u32[]{:S(2)}, u32[]{:S(2)}) %collective-permute-start.3) | collective-permute-done | bytes 393248 | tf_op jit(solution)/shard_map/ppermute | solution.py:50
  42.1 0.1 fusion.5
  42.2 3.1 %collective-permute-start.4 = (bf16[128,1536]{1,0:T(8,128)(2,1)S(1)}, bf16[128,1536]{1,0:T(8,128)(2,1)S(1)}, u32[]{:S(2)}, u32[]{:S(2)}) collective-permute-start(bf16[128,1536]{1,0:T(8,128)(2,1)S(1)} %fusion.5), channel_id=1, source_target_pairs={{0,3},{1,2},{2,1},{3,0},{4,5},{5,4},{6,7},{7,6},{8,11},{9,10},{10,... | collective-permute-start | bytes 1179656 | tf_op jit(solution)/shard_map/ppermute | solution.py:50
  45.3 2.0 %collective-permute-done.2 = bf16[128,1792]{1,0:T(8,128)(2,1)S(1)} collective-permute-done((bf16[128,1792]{1,0:T(8,128)(2,1)S(1)}, bf16[128,1792]{1,0:T(8,128)(2,1)S(1)}, u32[]{:S(2)}, u32[]{:S(2)}) %collective-permute-start.2) | collective-permute-done | bytes 458784 | tf_op jit(solution)/shard_map/ppermute | solution.py:50
  47.3 0.2 fusion.3.mine
  47.5 0.2 collective-permute-start.6
  47.7 4.6 %collective-permute-done.4 = bf16[128,1536]{1,0:T(8,128)(2,1)S(1)} collective-permute-done((bf16[128,1536]{1,0:T(8,128)(2,1)S(1)}, bf16[128,1536]{1,0:T(8,128)(2,1)S(1)}, u32[]{:S(2)}, u32[]{:S(2)}) %collective-permute-start.4) | collective-permute-done | bytes 393248 | tf_op jit(solution)/shard_map/ppermute | solution.py:50
  52.4 0.2 fusion.1.mine
  52.6 2.1 %collective-permute-start.5 = (bf16[128,1536]{1,0:T(8,128)(2,1)S(1)}, bf16[128,1536]{1,0:T(8,128)(2,1)S(1)}, u32[]{:S(2)}, u32[]{:S(2)}) collective-permute-start(bf16[128,1536]{1,0:T(8,128)(2,1)S(1)} %fusion.1.mine), channel_id=1, source_target_pairs={{0,1},{1,0},{2,3},{3,2},{4,7},{5,6},{6,5},{7,4},{8,9},{9,8},{10,11... | collective-permute-start | bytes 1179656 | tf_op jit(solution)/shard_map/ppermute | solution.py:50
  54.7 0.6 collective-permute-done.6.other
  55.4 2.5 %cross.3 = (f32[256,1024]{1,0:T(8,128)S(1)}, f32[256,1024]{1,0:T(8,128)S(1)}) custom-call(s32[9]{0:T(128)S(1)} %stack.35.scalars, bf16[128,1536]{1,0:T(8,128)(2,1)S(1)} %fusion.3.mine, bf16[128,1536]{1,0:T(8,128)(2,1)S(1)} %collective-permute-done.6.other, bf16[1536,2048]{1,0:T(8,128)(2,1)S(1)} %load.1.near), custom_call_target="tpu_custom_call" | custom-call | flops 1610612736 | bytes 6291456 | tf_op jit(solution)/shard_map/cross/pallas_call | solution.py:272
  57.8 2.7 %collective-permute-done.5.other = bf16[128,1536]{1,0:T(8,128)(2,1)S(1)} collective-permute-done((bf16[128,1536]{1,0:T(8,128)(2,1)S(1)}, bf16[128,1536]{1,0:T(8,128)(2,1)S(1)}, u32[]{:S(2)}, u32[]{:S(2)}) %collective-permute-start.5) | collective-permute-done | bytes 393248 | tf_op jit(solution)/shard_map/ppermute | solution.py:50
  60.5 1.6 %cross.5 = bf16[256,1024]{1,0:T(8,128)(2,1)S(1)} custom-call(s32[9]{0:T(128)S(1)} %stack.35.scalars, bf16[128,1536]{1,0:T(8,128)(2,1)S(1)} %fusion.1.mine, bf16[128,1536]{1,0:T(8,128)(2,1)S(1)} %collective-permute-done.5.other, bf16[1536,2048]{1,0:T(8,128)(2,1)S(1)} %get-tuple-element.33.near, f32[256,1024]{1,0:T(8,128)S(1)} %get-tuple-element.38.refs_0_), custom_call_target="tpu_custom_call" | custom-call | flops 1610612736 | bytes 6291456 | tf_op jit(solution)/shard_map/cross/pallas_call | solution.py:272
  62.2 0.1 collective-permute-start.7
  62.3 0.0 copy-start
  62.3 1.6 %cross.4 = f32[256,1024]{1,0:T(8,128)S(1)} custom-call(s32[9]{0:T(128)S(1)} %stack.35.scalars, bf16[128,1536]{1,0:T(8,128)(2,1)S(1)} %fusion.1.mine, bf16[128,1536]{1,0:T(8,128)(2,1)S(1)} %collective-permute-done.5.other, bf16[1536,2048]{1,0:T(8,128)(2,1)S(1)} %get-tuple-element.33.near, f32[256,1024]{1,0:T(8,128)S(1)} %get-tuple-element.37.refs_0_), custom_call_target="tpu_custom_call" | custom-call | flops 1610612736 | bytes 6291456 | tf_op jit(solution)/shard_map/cross/pallas_call | solution.py:272
  63.9 0.2 collective-permute-done.7
  64.1 1.0 %add_convert_fusion = bf16[256,1024]{1,0:T(8,128)(2,1)} fusion(f32[256,1024]{1,0:T(8,128)S(1)} %cross.4, bf16[256,1024]{1,0:T(8,128)(2,1)S(1)} %collective-permute-done.7), kind=kLoop, calls=%fused_computation.3 | loop fusion | flops 786432 | bytes 2097152 | tf_op jit(solution)/shard_map/convert_element_type | solution.py:365
  65.1 3.6 %all-to-all-start.1 = ((bf16[16,16,1024]{2,1,0:T(8,128)(2,1)}), bf16[16,16,1024]{2,1,0:T(8,128)(2,1)S(1)}, u32[]{:S(2)}, u32[]{:S(2)}) async-start(bf16[16,16,1024]{2,1,0:T(8,128)(2,1)} %bitcast.16), calls=%async_computation.1 | async-start | bytes 1048576 | tf_op jit(solution)/shard_map/all_to_all | solution.py:58
  68.7 0.1 multiply_reduce_fusion
  68.8 0.3 fusion.15
  69.1 11.8 %all-to-all-done.1 = bf16[16,16,1024]{2,1,0:T(8,128)(2,1)S(1)} async-done(((bf16[16,16,1024]{2,1,0:T(8,128)(2,1)}), bf16[16,16,1024]{2,1,0:T(8,128)(2,1)S(1)}, u32[]{:S(2)}, u32[]{:S(2)}) %all-to-all-start.1) | async-done | bytes 524320 | tf_op jit(solution)/shard_map/all_to_all | solution.py:58
  80.9 0.1 convert_reduce_fusion
  81.0 0.0 copy-done
  81.0 0.7 fusion.11
  (11 shorter events, 0.1 us)
Async XLA Ops:
  1.7 19.5 %all-to-all-start = ((bf16[16,16,1024]{2,1,0:T(8,128)(2,1)}), bf16[16,16,1024]{2,1,0:T(8,128)(2,1)S(1)}, u32[]{:S(2)}, u32[]{:S(2)}) async-start(bf16[16,16,1024]{2,1,0:T(8,128)(2,1)} %bitcast), calls=%async_computation | async-start | bytes 1048576 | tf_op jit(solution)/shard_map/all_to_all | solution.py:58
  21.2 2.9 %collective-permute-start = (bf16[256,1024]{1,0:T(8,128)(2,1)S(1)}, bf16[256,1024]{1,0:T(8,128)(2,1)S(1)}, u32[]{:S(2)}, u32[]{:S(2)}) collective-permute-start(bf16[256,1024]{1,0:T(8,128)(2,1)S(1)} %bitcast.21), channel_id=1, source_target_pairs={{0,4},{4,0},{8,12},{12,8},{16,20},{20,16},{24,28},{28,24},{32,36},... | collective-permute-start | bytes 1572872 | tf_op jit(solution)/shard_map/ppermute | solution.py:54
  28.6 8.6 %collective-permute-start.1 = (bf16[128,1792]{1,0:T(8,128)(2,1)S(1)}, bf16[128,1792]{1,0:T(8,128)(2,1)S(1)}, u32[]{:S(2)}, u32[]{:S(2)}) collective-permute-start(bf16[128,1792]{1,0:T(8,128)(2,1)S(1)} %get-tuple-element.27), channel_id=1, source_target_pairs={{0,1},{1,0},{2,3},{3,2},{4,7},{5,6},{6,5},{7,4},{8,9},{9,8},{10,11... | collective-permute-start | bytes 1376264 | tf_op jit(solution)/shard_map/ppermute | solution.py:50
  32.6 9.5 %collective-permute-start.3 = (bf16[128,1536]{1,0:T(8,128)(2,1)S(1)}, bf16[128,1536]{1,0:T(8,128)(2,1)S(1)}, u32[]{:S(2)}, u32[]{:S(2)}) collective-permute-start(bf16[128,1536]{1,0:T(8,128)(2,1)S(1)} %get-tuple-element.35), channel_id=1, source_target_pairs={{0,1},{1,0},{2,3},{3,2},{4,7},{5,6},{6,5},{7,4},{8,9},{9,8},{10,11... | collective-permute-start | bytes 1179656 | tf_op jit(solution)/shard_map/ppermute | solution.py:50
  37.3 10.0 %collective-permute-start.2 = (bf16[128,1792]{1,0:T(8,128)(2,1)S(1)}, bf16[128,1792]{1,0:T(8,128)(2,1)S(1)}, u32[]{:S(2)}, u32[]{:S(2)}) collective-permute-start(bf16[128,1792]{1,0:T(8,128)(2,1)S(1)} %pad_maximum_fusion), channel_id=1, source_target_pairs={{0,3},{1,2},{2,1},{3,0},{4,5},{5,4},{6,7},{7,6},{8,11},{9,10},{10,... | collective-permute-start | bytes 1376264 | tf_op jit(solution)/shard_map/ppermute | solution.py:50
  42.2 10.2 %collective-permute-start.4 = (bf16[128,1536]{1,0:T(8,128)(2,1)S(1)}, bf16[128,1536]{1,0:T(8,128)(2,1)S(1)}, u32[]{:S(2)}, u32[]{:S(2)}) collective-permute-start(bf16[128,1536]{1,0:T(8,128)(2,1)S(1)} %fusion.5), channel_id=1, source_target_pairs={{0,3},{1,2},{2,1},{3,0},{4,5},{5,4},{6,7},{7,6},{8,11},{9,10},{10,... | collective-permute-start | bytes 1179656 | tf_op jit(solution)/shard_map/ppermute | solution.py:50
  47.5 7.9 %collective-permute-start.6 = (bf16[128,1536]{1,0:T(8,128)(2,1)S(1)}, bf16[128,1536]{1,0:T(8,128)(2,1)S(1)}, u32[]{:S(2)}, u32[]{:S(2)}) collective-permute-start(bf16[128,1536]{1,0:T(8,128)(2,1)S(1)} %fusion.3.mine), channel_id=1, source_target_pairs={{0,1},{1,0},{2,3},{3,2},{4,7},{5,6},{6,5},{7,4},{8,9},{9,8},{10,11... | collective-permute-start | bytes 1179656 | tf_op jit(solution)/shard_map/ppermute | solution.py:50
  52.6 7.9 %collective-permute-start.5 = (bf16[128,1536]{1,0:T(8,128)(2,1)S(1)}, bf16[128,1536]{1,0:T(8,128)(2,1)S(1)}, u32[]{:S(2)}, u32[]{:S(2)}) collective-permute-start(bf16[128,1536]{1,0:T(8,128)(2,1)S(1)} %fusion.1.mine), channel_id=1, source_target_pairs={{0,1},{1,0},{2,3},{3,2},{4,7},{5,6},{6,5},{7,4},{8,9},{9,8},{10,11... | collective-permute-start | bytes 1179656 | tf_op jit(solution)/shard_map/ppermute | solution.py:50
  62.2 2.0 %collective-permute-start.7 = (bf16[256,1024]{1,0:T(8,128)(2,1)S(1)}, bf16[256,1024]{1,0:T(8,128)(2,1)S(1)}, u32[]{:S(2)}, u32[]{:S(2)}) collective-permute-start(bf16[256,1024]{1,0:T(8,128)(2,1)S(1)} %cross.5), channel_id=1, source_target_pairs={{0,4},{4,0},{8,12},{12,8},{16,20},{20,16},{24,28},{28,24},{32,36},... | collective-permute-start | bytes 1572872 | tf_op jit(solution)/shard_map/ppermute | solution.py:54
  62.3 18.7 %copy-start = (f32[8,2048]{1,0:T(8,128)S(1)}, f32[8,2048]{1,0:T(8,128)}, u32[]{:S(2)}) copy-start(f32[8,2048]{1,0:T(8,128)} %factors.3) | copy-start | bytes 196612
  65.1 15.8 %all-to-all-start.1 = ((bf16[16,16,1024]{2,1,0:T(8,128)(2,1)}), bf16[16,16,1024]{2,1,0:T(8,128)(2,1)S(1)}, u32[]{:S(2)}, u32[]{:S(2)}) async-start(bf16[16,16,1024]{2,1,0:T(8,128)(2,1)} %bitcast.16), calls=%async_computation.1 | async-start | bytes 1048576 | tf_op jit(solution)/shard_map/all_to_all | solution.py:58

commit v3 on v0

v3 whole, which is shorter than its diff:
```python
import functools

import jax
import jax.numpy as jnp
from jax import lax
from jax.experimental import pallas as pl
from jax.experimental.pallas import tpu as pltpu
from jax.sharding import PartitionSpec as P

BF16 = jnp.bfloat16
F32 = jnp.float32
N_DP = 32
N_FEAT = 4
CHIPS = N_DP // 2
SIZES = (1664, 1408)
GRAM_PART = 0
LANES = 128
PARTS = len(SIZES)
LOADS = 2
PLANES = [[2 * chip + core for chip in range(CHIPS)] for core in range(2)]
VMEM = pl.BlockSpec(memory_space=pltpu.VMEM)
SMEM = pl.BlockSpec(memory_space=pltpu.SMEM)
ANY = pl.BlockSpec(memory_space=pl.ANY)
PARAMS = pltpu.CompilerParams(vmem_limit_bytes=8 << 20)


def in_hbm(array):
    return pltpu.with_memory_space_constraint(array, pltpu.HBM)


def in_vmem(array):
    return pltpu.with_memory_space_constraint(array, pltpu.VMEM)


def partner_first(core, y):
    return y ^ 1 if core == 0 else 3 - y


def partner_second(core, y):
    return 3 - y if core == 0 else y ^ 1


PARTNERS = (partner_first, partner_second)


def feat_swap(x, partner):
    pairs = []
    for dp in range(N_DP):
        for y in range(N_FEAT):
            pairs.append((dp * N_FEAT + y, dp * N_FEAT + partner(dp % 2, y)))
    return lax.ppermute(x, ("dp", "feat"), pairs)


def core_swap(x):
    return lax.ppermute(x, "dp", [(i, i ^ 1) for i in range(N_DP)])


def plane_exchange(x):
    return lax.all_to_all(x, "dp", 0, 0, axis_index_groups=PLANES, tiled=True)


def spread_kernel(factors, out):
    width = out.shape[1]
    block = jnp.concatenate([factors[:, :width], factors[:, width:]], 0).astype(BF16)
    for chip in range(CHIPS):
        out[pl.ds(16 * chip, 16), :] = block


def spread(factors):
    return pl.pallas_call(
        spread_kernel,
        in_specs=[VMEM],
        out_specs=VMEM,
        out_shape=pltpu.VMEM((16 * CHIPS, factors.shape[1] // 2), BF16),
        compiler_params=PARAMS,
        name="spread",
    )(in_hbm(factors))


def unpack(packed, out, top):
    for pair in range(CHIPS // 2):
        block = packed[pl.ds(32 * pair, 32), :].astype(F32)
        upper = jnp.concatenate([block[:8], block[8:16]], 1)
        lower = jnp.concatenate([block[16:24], block[24:]], 1)
        out[pl.ds(top + 16 * pair, 16), :] = jnp.concatenate([upper, lower], 0).astype(BF16)


def parts_of(value):
    high = value.astype(BF16)
    return high, (value - high.astype(F32)).astype(BF16)


def gram_message(gram):
    return jnp.concatenate([part.astype(F32) for part in parts_of(gram)], 0).astype(BF16)


def gram_of(message):
    value = message.astype(F32)
    return value[:8] + value[8:16]


def folded(value):
    return jnp.concatenate([value[:, :LANES], value[:, LANES:]], 0)


def gram_from(message):
    value = message.astype(F32)
    return jnp.concatenate([gram_of(value[:16]), gram_of(value[16:32])], 1)


def start_of(part):
    return sum(SIZES[:part])


def fetch(samples, near, sems, part):
    rows = SIZES[part] // LOADS
    copies = []
    for i in range(LOADS):
        here = pl.ds(i * rows, rows)
        there = pl.ds(start_of(part) + i * rows, rows)
        copies.append(pltpu.make_async_copy(samples.at[there, :], near.at[here, :], sems.at[i]))
        copies[-1].start()
    return copies


def load_kernel(packed, factors, samples, near, rows, left, gram, mine, sem, sems):
    first = pltpu.make_async_copy(factors, mine, sem)
    first.start()
    copies = fetch(samples, near, sems, 0)
    unpack(packed, rows, 0)
    first.wait()
    left[...] = gram_message(mine[...])
    gram[...] = gram_of(nt_dot(left[...], rows[...]))
    for copy in copies:
        copy.wait()


def load(packed, factors, samples):
    depth = samples.shape[1]
    count = packed.shape[0] // 2
    return pl.pallas_call(
        load_kernel,
        in_specs=[VMEM, ANY, ANY],
        out_specs=[VMEM] * 4,
        out_shape=[
            pltpu.VMEM((SIZES[0], depth), BF16),
            jax.ShapeDtypeStruct((count, depth), BF16),
            jax.ShapeDtypeStruct((2 * factors.shape[0], depth), BF16),
            jax.ShapeDtypeStruct((factors.shape[0], count), F32),
        ],
        scratch_shapes=[
            pltpu.VMEM(factors.shape, F32),
            pltpu.SemaphoreType.DMA,
            pltpu.SemaphoreType.DMA((LOADS,)),
        ],
        compiler_params=PARAMS,
        cost_estimate=pl.CostEstimate(
            flops=0, bytes_accessed=4 * SIZES[0] * depth, transcendentals=0
        ),
        name="load",
    )(packed, in_hbm(factors), in_hbm(samples))


def nt_dot(left, right):
    return lax.dot_general(left, right, (((1,), (1,)), ((), ())), preferred_element_type=F32)


def project_part(scalars, other, own, near, sent, kept, scratch, part):
    half, slots = kept.shape
    block = half // 2
    for i in range(4):
        quarter = scalars[i]
        at = pl.ds(pl.multiple_of(lax.rem(quarter, 2) * block, block), block)
        to = slice(i * block, (i + 1) * block)
        for side, ref in enumerate((other, own)):

            @pl.when(quarter // 2 == side)
            def _():
                scratch[to, :] = ref[at, :]

    value = nt_dot(scratch[...], near[...])
    slot = start_of(part) + lax.broadcasted_iota(jnp.int32, (1, slots), 1)
    value = jnp.where(slot < scalars[4], value, 0.0)
    sent[:, :slots] = value[:half].astype(BF16)
    kept[...] = value[half:]


def put_gram(sent, gram):
    slots = sent.shape[1] - LANES
    message = folded(gram_message(gram[...]).astype(F32)).astype(BF16)
    sent[:32, slots:] = message
    sent[32:, slots:] = jnp.zeros((sent.shape[0] - 32, LANES), BF16)


def first_kernel(scalars, packed, own, left, gram_own, near, samples, sent, kept, other, gram, later, scratch, sems):
    copies = fetch(samples, later, sems, 1)
    unpack(packed, other, 0)
    project_part(scalars, other, own, near, sent, kept, scratch, 0)
    gram[...] = jnp.concatenate([gram_of(nt_dot(left[...], other[...])), gram_own[...]], 1)
    if GRAM_PART == 0:
        put_gram(sent, gram)
    for copy in copies:
        copy.wait()


def project_first(scalars, packed, own, left, gram_own, near, samples):
    slots, depth = near.shape
    count = 2 * own.shape[0]
    return pl.pallas_call(
        first_kernel,
        in_specs=[SMEM] + [VMEM] * 5 + [ANY],
        out_specs=[VMEM] * 5,
        out_shape=[
            jax.ShapeDtypeStruct((count // 2, slots + LANES * (GRAM_PART == 0)), BF16),
            jax.ShapeDtypeStruct((count // 2, slots), F32),
            jax.ShapeDtypeStruct((count // 2, depth), BF16),
            jax.ShapeDtypeStruct((left.shape[0] // 2, count), F32),
            pltpu.VMEM((SIZES[1], depth), BF16),
        ],
        scratch_shapes=[
            pltpu.VMEM((count, depth), BF16),
            pltpu.SemaphoreType.DMA((LOADS,)),
        ],
        compiler_params=PARAMS,
        cost_estimate=estimate(slots, depth, count),
        name="project_first",
    )(scalars, packed, own, left, gram_own, in_vmem(near), in_hbm(samples))


def second_kernel(scalars, other, own, gram, near, sent, kept, scratch):
    project_part(scalars, other, own, near, sent, kept, scratch, 1)
    if GRAM_PART == 1:
        put_gram(sent, gram)


def project_second(scalars, other, own, gram, near):
    slots, depth = near.shape
    count = 2 * own.shape[0]
    return pl.pallas_call(
        second_kernel,
        in_specs=[SMEM] + [VMEM] * 4,
        out_specs=[VMEM] * 2,
        out_shape=[
            jax.ShapeDtypeStruct((count // 2, slots + LANES * (GRAM_PART == 1)), BF16),
            jax.ShapeDtypeStruct((count // 2, slots), F32),
        ],
        scratch_shapes=[pltpu.VMEM((count, depth), BF16)],
        compiler_params=PARAMS,
        cost_estimate=estimate(slots, depth, count),
        name="project_second",
    )(scalars, other, own, gram, in_vmem(near))


def estimate(slots, depth, rows):
    return pl.CostEstimate(
        flops=2 * slots * depth * rows, bytes_accessed=2 * slots * depth, transcendentals=0
    )


def model_kernel(pairs, here, gram, other, own, factors, out):
    value = pairs[...] * gram[...] * gram[...] * gram[...]
    diagonal = jnp.sum(here[...] * value, 1, keepdims=True)
    left = gram_message(value)
    half = other.shape[0]
    both = jnp.dot(left[:, :half], other[...], preferred_element_type=F32) + jnp.dot(
        left[:, half:], own[...], preferred_element_type=F32
    )
    rest = factors[...] - factors[...].astype(BF16).astype(F32)
    out[...] = 8.0 * (gram_of(both) + diagonal * rest)


def model(pairs, here, gram, other, own, factors):
    return pl.pallas_call(
        model_kernel,
        in_specs=[VMEM] * 6,
        out_specs=VMEM,
        out_shape=jax.ShapeDtypeStruct(factors.shape, F32),
        compiler_params=PARAMS,
        name="model",
    )(pairs, here, gram, other, own, factors)


def cross_kernel(scalars, mine, other, near, *refs, sides, add, tile):
    terms, refs = (refs[: len(sides)] if add else None), refs[add * len(sides) :]
    outs, rows = refs[:-1], refs[-1]
    block = mine.shape[0] // 2
    half = 2 * block
    for i, piece in enumerate((other[:block], other[block:], mine[:block], mine[block:])):
        at = pl.multiple_of(scalars[i] * block, block)
        rows[pl.ds(at, block), :] = piece
    width = outs[0].shape[1]
    first = sides[0] * half
    used = slice(first, first + len(sides) * half)

    @pl.loop(0, width // tile)
    def _(i):
        here = pl.ds(pl.multiple_of(i * tile, tile), tile)
        there = pl.ds(pl.multiple_of(width + i * tile, tile), tile)
        left, right = (
            jnp.dot(rows[used, :], near[:, at], preferred_element_type=F32) for at in (here, there)
        )
        for place, out in enumerate(outs):
            for chip in range(CHIPS):
                at = place * half + 8 * chip
                to = slice(16 * chip, 16 * chip + 16)
                value = jnp.concatenate([left[at : at + 8], right[at : at + 8]], 0)
                if add:
                    value = value + terms[place][to, here]
                out[to, here] = value.astype(out.dtype)


def cross(scalars, pieces, near, sides, out_type, terms=(), tile=512):
    slots, depth = near.shape
    rows = 2 * pieces[0].shape[0]
    out = jax.ShapeDtypeStruct((rows, depth // 2), out_type)
    return pl.pallas_call(
        functools.partial(cross_kernel, sides=sides, add=bool(terms), tile=tile),
        in_specs=[SMEM] + [VMEM] * (3 + len(terms)),
        out_specs=[VMEM] * len(sides),
        out_shape=[out] * len(sides),
        scratch_shapes=[pltpu.VMEM((rows, slots), BF16)],
        compiler_params=PARAMS,
        cost_estimate=estimate(slots, depth, rows),
        name="cross",
    )(scalars, *pieces, in_vmem(near), *terms)


def add_kernel(left, right, out):
    out[...] = (left[...] + right[...].astype(F32)).astype(BF16)


def add(left, right):
    return pl.pallas_call(
        add_kernel,
        in_specs=[VMEM, VMEM],
        out_specs=VMEM,
        out_shape=pltpu.VMEM(left.shape, BF16),
        compiler_params=PARAMS,
        name="add",
    )(left, right)


def on_device(samples, factors, weights, counts):
    owned, depth = factors.shape
    all_rows = weights.shape[0]
    half_rows = all_rows // 2
    block = all_rows // 4
    dp = lax.axis_index("dp")
    y = lax.axis_index("feat")
    core = lax.rem(dp, 2)
    chip = dp // 2
    first = jnp.where(core == 0, y ^ 1, 3 - y)
    second = jnp.where(core == 0, 3 - y, y ^ 1)
    across = lax.rem(y + 2, 4)
    order = []
    for pair in ((first, across), (y, second)):
        order += [jnp.minimum(*pair), jnp.maximum(*pair)]
    scalars = jnp.stack(order + [counts[dp]]).astype(jnp.int32)
    total = jnp.sum(counts).astype(F32)
    by_core = weights.reshape(CHIPS, 2, owned).transpose(1, 0, 2).reshape(2, half_rows)
    weight_own = lax.dynamic_slice(by_core, (core, 0), (1, half_rows))[0]
    weight_other = lax.dynamic_slice(by_core, (1 - core, 0), (1, half_rows))[0]
    weight = jnp.concatenate([weight_other, weight_own])
    scale = jnp.concatenate(
        [lax.dynamic_slice(weight, (order[i] * block,), (block,)) for i in (2, 3)]
    )
    scales = [scale] * PARTS
    weight_mine = lax.dynamic_slice(weight_own, (chip * owned,), (owned,))
    pairs = weight_mine[:, None] * weight[None, :]
    mine = lax.broadcasted_iota(jnp.int32, pairs.shape, 0) + half_rows + chip * owned
    here = (lax.broadcasted_iota(jnp.int32, pairs.shape, 1) == mine).astype(F32)
    factor = jnp.full((1, 1), 8.0, F32) / total[None, None]

    packed_own = plane_exchange(spread(factors))
    packed_own, scalars, scales, pairs, here, factor, samples = lax.optimization_barrier(
        (packed_own, scalars, scales, pairs, here, factor, samples)
    )
    near0, own, left, gram_own = load(packed_own, factors, samples)
    packed_other = core_swap(packed_own)
    sent0, kept0, other, gram, near1 = project_first(
        scalars, packed_other, own, left, gram_own, near0, samples
    )
    sent1, kept1 = project_second(scalars, other, own, gram, near1)
    nears = (near0, near1)

    pieces = []
    for part, (sent, kept) in enumerate(((sent0, kept0), (sent1, kept1))):
        slots = kept.shape[1]
        carries = part == GRAM_PART
        with jax.named_scope(f"halves{part}"):
            got = feat_swap(sent, partner_first)
        value = kept + got[:, :slots].astype(F32)
        message = value.astype(BF16)
        if carries:
            gram = gram + gram_from(got[:32, slots:])
            high = lax.reduce_precision(gram, 8, 7)
            extra = folded(jnp.concatenate([high, gram - high], 0)).astype(BF16)
            extra = jnp.pad(extra, ((0, kept.shape[0] - 32), (0, 0)))
            message = jnp.concatenate([message, extra], 1)
        with jax.named_scope(f"sums{part}"):
            passed = feat_swap(message, partner_second)
        if carries:
            gram = gram + gram_from(passed[:32, slots:])
        value = value + passed[:, :slots].astype(F32)
        cubes = (scales[part][:, None] * value**3).astype(BF16)
        with jax.named_scope(f"cubes{part}"):
            pieces.append((cubes, feat_swap(cubes, partner_first)))

    terms = ()
    for part in range(PARTS - 1):
        terms = cross(scalars, pieces[part], nears[part], (0, 1), F32, terms)
    (sum_other,) = cross(scalars, pieces[-1], nears[-1], (0,), BF16, terms[:1])
    (sum_own,) = cross(scalars, pieces[-1], nears[-1], (1,), F32, terms[1:])
    total_own = add(sum_own, core_swap(sum_other))
    model_term = model(pairs, here, gram, other, own, factors)
    model_term, total_own = lax.optimization_barrier((model_term, total_own))
    blocks = plane_exchange(total_own).reshape(CHIPS, 2 * owned, depth // 2)
    cross_term = jnp.sum(blocks.astype(F32), axis=0)
    cross_term = jnp.concatenate([cross_term[:owned], cross_term[owned:]], 1)

    return model_term - factor * cross_term


def solution(mesh):
    in_specs = (P("dp", "feat"), P("dp", "feat"), P(), P())
    out_specs = P("dp", "feat")
    return jax.shard_map(
        on_device, mesh=mesh, in_specs=in_specs, out_specs=out_specs, check_vma=False
    )
```

time: 249 us -> 78.7 us (0.32)
  waiting for transfers between devices: 205 us -> 21.5 us
  matrix products: 27.7 us -> 0 us
  starting transfers between devices: 0.08 us -> 17.5 us
  Pallas kernels: 0 us -> 17.3 us
  blocking collectives: 0 us -> 15.1 us
  between operations: 13.8 us -> 0.97 us
    psum x1 -> x0, waiting for transfers between devices: 77.8 us -> none  [on_device(): projection = lax.psum(partial_value, 'feat')]
    reduce_scatter x1 -> x0, waiting for transfers between devices: 77.5 us -> none  [on_device(): lax.psum_scatter(cross_sum, 'dp', scatter_dimension=0, tiled=True)]
    all_gather x1 -> x0, waiting for transfers between devices: 48.8 us -> none  [on_device(): gathered = lax.all_gather(factors, 'dp', axis=0, tiled=True)]
    dot_general x4 -> x0, matrix products: 27.7 us -> none  [the longest x1 10.4 us: on_device(): lax.dot_general(cubes_low, samples, (((0,), (0,)), ((), ())), preferred_e...]
    pallas_call x0 -> x9, Pallas kernels: none -> 17.3 us  [the longest x3 6.45 us: cross(): pl.pallas_call(functools.partial(cross_kernel, sides=sides, add=bool(term...]
    ppermute x0 -> x8, waiting for transfers between devices: none -> 15.3 us  [the longest x6 15.3 us: feat_swap(): return lax.ppermute(x, ('dp', 'feat'), pairs)]
    all_to_all x0 -> x1, blocking collectives: none -> 15.1 us  [plane_exchange(): return lax.all_to_all(x, 'dp', 0, 0, axis_index_groups=PLANES, tiled=True)]
    ppermute x0 -> x8, starting transfers between devices: none -> 9.59 us  [the longest x6 9.5 us: feat_swap(): return lax.ppermute(x, ('dp', 'feat'), pairs)]
  transfers between devices with their start and end apart: 3 -> 9, of which waited for: 3 -> 7; matrix products, arithmetic and copies ran while one was open for 1% -> 7% of each run, Pallas kernels for 0% -> 13%
where the time goes in v3:
time: 78.7 us; the launch traced here: 78.3 us
  waiting for transfers between devices  21.5 us (27%)
  starting transfers between devices  17.5 us (22%)
  Pallas kernels  17.3 us (22%)
  blocking collectives  15.1 us (19%)
  local copies, waits for them, and re-layouts  3.05 us (4%)
  other arithmetic  2.92 us (4%)
  between operations  0.97 us (1%)
    ppermute x6, waiting for transfers between devices, feat_swap(): return lax.ppermute(x, ('dp', 'feat'), pairs)  15.3 us
    all_to_all x1, blocking collectives, plane_exchange(): return lax.all_to_all(x, 'dp', 0, 0, axis_index_groups=PLANES, tiled=True)  15.1 us
    ppermute x6, starting transfers between devices, feat_swap(): return lax.ppermute(x, ('dp', 'feat'), pairs)  9.5 us
    all_to_all x1, starting transfers between devices, plane_exchange(): return lax.all_to_all(x, 'dp', 0, 0, axis_index_groups=PLANES, tiled=True)  7.96 us
    pallas_call x3, Pallas kernels, cross(): pl.pallas_call(functools.partial(cross_kernel, sides=sides, add=bool(term...  6.45 us
    all_to_all x1, waiting for transfers between devices, plane_exchange(): return lax.all_to_all(x, 'dp', 0, 0, axis_index_groups=PLANES, tiled=True)  6.16 us
    pallas_call x1, Pallas kernels, project_first(): pl.pallas_call(first_kernel, in_specs=[SMEM] + [VMEM] * 5 + [ANY], out_sp...  3.25 us
    pallas_call x1, Pallas kernels, load(): pl.pallas_call(load_kernel, in_specs=[VMEM, ANY, ANY], out_specs=[VMEM] *...  3.05 us
  transfers between devices with their start and end apart: 9, of which 7 were waited for; matrix products, arithmetic and copies ran while one was open for 7% of the time, Pallas kernels for 13%

profile of v3, /device:TPU:0, one launch (start us, length us, event | category | flops | bytes accessed | tf_op | source)
XLA Modules:
  0.0 78.3 jit_solution(17583640630676358418)
XLA Ops:
  0.0 1.7 %spread.1 = bf16[256,1024]{1,0:T(8,128)(2,1)} custom-call(f32[8,2048]{1,0:T(8,128)} %factors.5), custom_call_target="tpu_custom_call" | custom-call | tf_op jit(solution)/shard_map/spread/pallas_call | solution.py:70
  1.7 8.0 %all-to-all-start = ((bf16[16,16,1024]{2,1,0:T(8,128)(2,1)}), bf16[16,16,1024]{2,1,0:T(8,128)(2,1)S(1)}, u32[]{:S(2)}, u32[]{:S(2)}) async-start(bf16[16,16,1024]{2,1,0:T(8,128)(2,1)} %bitcast), calls=%async_computation | async-start | bytes 1048576 | tf_op jit(solution)/shard_map/all_to_all | solution.py:59
  9.7 0.8 reshape.20
  10.5 0.1 reshape.21
  10.6 0.1 dynamic-slice_bitcast_fusion
  10.7 0.1 fusion.14
  10.8 0.1 pad_maximum_fusion.2
  10.9 1.3 %reduce_sum.18 = s32[]{:T(128)} reduce(s32[32]{0:T(128)} %param.7, s32[]{:T(128)} %constant.47.clone.1), dimensions={0}, to_apply=%region_0.1 | reduce | flops 31 | bytes 136 | tf_op jit(solution)/shard_map/reduce_sum | solution.py:359
  12.8 1.3 %dynamic_slice.18 = s32[1]{0:T(128)} dynamic-slice(s32[32]{0:T(128)} %param.7, s32[]{:T(128)S(6)} %select_n.35), dynamic_slice_sizes={1} | dynamic-slice | bytes 12 | tf_op jit(solution)/shard_map/dynamic_slice | solution.py:358
  14.2 0.7 stack.19.scalars
  14.9 0.1 fusion.10.here
  15.0 0.1 broadcast_multiply_fusion.pairs
  15.0 6.2 %all-to-all-done = bf16[16,16,1024]{2,1,0:T(8,128)(2,1)S(1)} async-done(((bf16[16,16,1024]{2,1,0:T(8,128)(2,1)}), bf16[16,16,1024]{2,1,0:T(8,128)(2,1)S(1)}, u32[]{:S(2)}, u32[]{:S(2)}) %all-to-all-start) | async-done | bytes 524320 | tf_op jit(solution)/shard_map/all_to_all | solution.py:59
  21.2 0.0 collective-permute-start
  21.2 3.0 %load.1 = (bf16[1664,2048]{1,0:T(8,128)(2,1)S(1)}, bf16[128,2048]{1,0:T(8,128)(2,1)S(1)}, bf16[16,2048]{1,0:T(8,128)(2,1)S(1)}, f32[8,128]{1,0:T(8,128)S(1)}) custom-call(bf16[256,1024]{1,0:T(8,128)(2,1)S(1)} %bitcast.17, f32[8,2048]{1,0:T(8,128)} %factors.5, bf16[3072,2048]{1,0:T(8,128)(2,1)} %samples.1), custom_call_target="tpu_custom_call" | custom-call | bytes 13631488 | tf_op jit(solution)/shard_map/load/pallas_call | solution.py:141
  24.2 0.0 collective-permute-done.packed
  24.3 3.2 %project_first.1 = (bf16[128,1792]{1,0:T(8,128)(2,1)S(1)}, f32[128,1664]{1,0:T(8,128)S(1)}, bf16[128,2048]{1,0:T(8,128)(2,1)S(1)}, f32[8,256]{1,0:T(8,128)S(1)}, bf16[1408,2048]{1,0:T(8,128)(2,1)S(1)}) custom-call(s32[5]{0:T(128)S(1)} %stack.19.scalars, bf16[256,1024]{1,0:T(8,128)(2,1)S(1)} %collective-permute-done.packed, ...), custom_call_target="tpu_custom_call" | custom-call | flops 1744830464 | bytes 6815744 | tf_op jit(solution)/shard_map/project_first/pallas_call | solution.py:209
  27.5 1.7 %collective-permute-start.1 = (bf16[128,1792]{1,0:T(8,128)(2,1)S(1)}, bf16[128,1792]{1,0:T(8,128)(2,1)S(1)}, u32[]{:S(2)}, u32[]{:S(2)}) collective-permute-start(bf16[128,1792]{1,0:T(8,128)(2,1)S(1)} %get-tuple-element.38), channel_id=1, source_target_pairs={{0,1},{1,0},{2,3},{3,2},{4,7},{5,6},{6,5},{7,4},{8,9},{9,8},{10,11... | collective-permute-start | bytes 1376264 | tf_op jit(solution)/shard_map/halves0/ppermute | solution.py:51
  29.2 2.5 %project_second.1 = (bf16[128,1408]{1,0:T(8,128)(2,1)S(1)}, f32[128,1408]{1,0:T(8,128)S(1)}) custom-call(s32[5]{0:T(128)S(1)} %stack.19.scalars, bf16[128,2048]{1,0:T(8,128)(2,1)S(1)} %get-tuple-element.40.other, bf16[128,2048]{1,0:T(8,128)(2,1)S(1)} %get-tuple-element.33.own, f32[8,256]{1,0:T(8,128)S(1)} %get-tuple-element.37.gram, ...), custom_call_target="tpu_custom_call" | custom-call | flops 1476395008 | bytes 5767168 | tf_op jit(solution)/shard_map/project_second/pallas_call | solution.py:239
  31.7 0.5 collective-permute-start.3
  32.2 3.9 %collective-permute-done.1 = bf16[128,1792]{1,0:T(8,128)(2,1)S(1)} collective-permute-done((bf16[128,1792]{1,0:T(8,128)(2,1)S(1)}, bf16[128,1792]{1,0:T(8,128)(2,1)S(1)}, u32[]{:S(2)}, u32[]{:S(2)}) %collective-permute-start.1) | collective-permute-done | bytes 458784 | tf_op jit(solution)/shard_map/halves0/ppermute | solution.py:51
  36.1 0.1 fusion.4
  36.3 3.1 %collective-permute-start.2 = (bf16[128,1792]{1,0:T(8,128)(2,1)S(1)}, bf16[128,1792]{1,0:T(8,128)(2,1)S(1)}, u32[]{:S(2)}, u32[]{:S(2)}) collective-permute-start(bf16[128,1792]{1,0:T(8,128)(2,1)S(1)} %pad_maximum_fusion), channel_id=1, source_target_pairs={{0,3},{1,2},{2,1},{3,0},{4,5},{5,4},{6,7},{7,6},{8,11},{9,10},{10,... | collective-permute-start | bytes 1376264 | tf_op jit(solution)/shard_map/sums0/ppermute | solution.py:51
  39.4 0.9 %collective-permute-done.3 = bf16[128,1408]{1,0:T(8,128)(2,1)S(1)} collective-permute-done((bf16[128,1408]{1,0:T(8,128)(2,1)S(1)}, bf16[128,1408]{1,0:T(8,128)(2,1)S(1)}, u32[]{:S(2)}, u32[]{:S(2)}) %collective-permute-start.3) | collective-permute-done | bytes 360480 | tf_op jit(solution)/shard_map/halves1/ppermute | solution.py:51
  40.3 0.1 fusion.5
  40.4 3.1 %collective-permute-start.4 = (bf16[128,1408]{1,0:T(8,128)(2,1)S(1)}, bf16[128,1408]{1,0:T(8,128)(2,1)S(1)}, u32[]{:S(2)}, u32[]{:S(2)}) collective-permute-start(bf16[128,1408]{1,0:T(8,128)(2,1)S(1)} %fusion.5), channel_id=1, source_target_pairs={{0,3},{1,2},{2,1},{3,0},{4,5},{5,4},{6,7},{7,6},{8,11},{9,10},{10,... | collective-permute-start | bytes 1081352 | tf_op jit(solution)/shard_map/sums1/ppermute | solution.py:51
  43.4 2.6 %collective-permute-done.2 = bf16[128,1792]{1,0:T(8,128)(2,1)S(1)} collective-permute-done((bf16[128,1792]{1,0:T(8,128)(2,1)S(1)}, bf16[128,1792]{1,0:T(8,128)(2,1)S(1)}, u32[]{:S(2)}, u32[]{:S(2)}) %collective-permute-start.2) | collective-permute-done | bytes 458784 | tf_op jit(solution)/shard_map/sums0/ppermute | solution.py:51
  46.0 0.2 fusion.1.mine
  46.3 0.4 collective-permute-start.6
  46.7 3.9 %collective-permute-done.4 = bf16[128,1408]{1,0:T(8,128)(2,1)S(1)} collective-permute-done((bf16[128,1408]{1,0:T(8,128)(2,1)S(1)}, bf16[128,1408]{1,0:T(8,128)(2,1)S(1)}, u32[]{:S(2)}, u32[]{:S(2)}) %collective-permute-start.4) | collective-permute-done | bytes 360480 | tf_op jit(solution)/shard_map/sums1/ppermute | solution.py:51
  50.6 0.2 fusion.3.mine
  50.8 0.7 collective-permute-start.5
  51.5 0.0 copy-start
  51.5 3.0 %collective-permute-done.6.other = bf16[128,1664]{1,0:T(8,128)(2,1)S(1)} collective-permute-done((bf16[128,1664]{1,0:T(8,128)(2,1)S(1)}, bf16[128,1664]{1,0:T(8,128)(2,1)S(1)}, u32[]{:S(2)}, u32[]{:S(2)}) %collective-permute-start.6) | collective-permute-done | bytes 426016 | tf_op jit(solution)/shard_map/cubes0/ppermute | solution.py:51
  54.5 2.8 %cross.3 = (f32[256,1024]{1,0:T(8,128)S(1)}, f32[256,1024]{1,0:T(8,128)S(1)}) custom-call(s32[5]{0:T(128)S(1)} %stack.19.scalars, bf16[128,1664]{1,0:T(8,128)(2,1)S(1)} %fusion.1.mine, bf16[128,1664]{1,0:T(8,128)(2,1)S(1)} %collective-permute-done.6.other, bf16[1664,2048]{1,0:T(8,128)(2,1)S(1)} %get-tuple-element.36.near), custom_call_target="tpu_custom_call" | custom-call | flops 1744830464 | bytes 6815744 | tf_op jit(solution)/shard_map/cross/pallas_call | solution.py:316
  57.3 1.0 %collective-permute-done.5.other = bf16[128,1408]{1,0:T(8,128)(2,1)S(1)} collective-permute-done((bf16[128,1408]{1,0:T(8,128)(2,1)S(1)}, bf16[128,1408]{1,0:T(8,128)(2,1)S(1)}, u32[]{:S(2)}, u32[]{:S(2)}) %collective-permute-start.5) | collective-permute-done | bytes 360480 | tf_op jit(solution)/shard_map/cubes1/ppermute | solution.py:51
  58.3 1.8 %cross.5 = bf16[256,1024]{1,0:T(8,128)(2,1)S(1)} custom-call(s32[5]{0:T(128)S(1)} %stack.19.scalars, bf16[128,1408]{1,0:T(8,128)(2,1)S(1)} %fusion.3.mine, bf16[128,1408]{1,0:T(8,128)(2,1)S(1)} %collective-permute-done.5.other, bf16[1408,2048]{1,0:T(8,128)(2,1)S(1)} %get-tuple-element.42.near, f32[256,1024]{1,0:T(8,128)S(1)} %get-tuple-element.47.refs_0_), custom_call_target="tpu_custom_call" | custom-call | flops 1476395008 | bytes 5767168 | tf_op jit(solution)/shard_map/cross/pallas_call | solution.py:316
  60.2 0.1 collective-permute-start.7
  60.3 0.0 copy-done
  60.3 0.2 model.1
  60.5 1.8 %cross.4.left = f32[256,1024]{1,0:T(8,128)S(1)} custom-call(s32[5]{0:T(128)S(1)} %stack.19.scalars, bf16[128,1408]{1,0:T(8,128)(2,1)S(1)} %fusion.3.mine, bf16[128,1408]{1,0:T(8,128)(2,1)S(1)} %collective-permute-done.5.other, bf16[1408,2048]{1,0:T(8,128)(2,1)S(1)} %get-tuple-element.42.near, f32[256,1024]{1,0:T(8,128)S(1)} %get-tuple-element.46.refs_0_), custom_call_target="tpu_custom_call" | custom-call | flops 1476395008 | bytes 5767168 | tf_op jit(solution)/shard_map/cross/pallas_call | solution.py:316
  62.4 0.0 collective-permute-done.7.right
  62.4 0.1 add.121
  62.5 15.1 %all_to_all.21 = bf16[16,16,1024]{2,1,0:T(8,128)(2,1)S(1)} all-to-all(bf16[16,16,1024]{2,1,0:T(8,128)(2,1)S(1)} %bitcast.18), channel_id=1, replica_groups={{0,8,16,24,32,40,48,56,64,72,80,88,96,104,112,120},{4,12,20,28,36,44,52..., dimensions={0} | all-to-all | bytes 1048576 | tf_op jit(solution)/shard_map/all_to_all | solution.py:59
  77.6 0.1 convert_reduce_fusion
  77.7 0.6 fusion.8
  (15 shorter events, 0.1 us)
Async XLA Ops:
  1.7 19.5 %all-to-all-start = ((bf16[16,16,1024]{2,1,0:T(8,128)(2,1)}), bf16[16,16,1024]{2,1,0:T(8,128)(2,1)S(1)}, u32[]{:S(2)}, u32[]{:S(2)}) async-start(bf16[16,16,1024]{2,1,0:T(8,128)(2,1)} %bitcast), calls=%async_computation | async-start | bytes 1048576 | tf_op jit(solution)/shard_map/all_to_all | solution.py:59
  21.2 3.1 %collective-permute-start = (bf16[256,1024]{1,0:T(8,128)(2,1)S(1)}, bf16[256,1024]{1,0:T(8,128)(2,1)S(1)}, u32[]{:S(2)}, u32[]{:S(2)}) collective-permute-start(bf16[256,1024]{1,0:T(8,128)(2,1)S(1)} %bitcast.16), channel_id=1, source_target_pairs={{0,4},{4,0},{8,12},{12,8},{16,20},{20,16},{24,28},{28,24},{32,36},... | collective-permute-start | bytes 1572872 | tf_op jit(solution)/shard_map/ppermute | solution.py:55
  27.5 8.6 %collective-permute-start.1 = (bf16[128,1792]{1,0:T(8,128)(2,1)S(1)}, bf16[128,1792]{1,0:T(8,128)(2,1)S(1)}, u32[]{:S(2)}, u32[]{:S(2)}) collective-permute-start(bf16[128,1792]{1,0:T(8,128)(2,1)S(1)} %get-tuple-element.38), channel_id=1, source_target_pairs={{0,1},{1,0},{2,3},{3,2},{4,7},{5,6},{6,5},{7,4},{8,9},{9,8},{10,11... | collective-permute-start | bytes 1376264 | tf_op jit(solution)/shard_map/halves0/ppermute | solution.py:51
  31.7 8.6 %collective-permute-start.3 = (bf16[128,1408]{1,0:T(8,128)(2,1)S(1)}, bf16[128,1408]{1,0:T(8,128)(2,1)S(1)}, u32[]{:S(2)}, u32[]{:S(2)}) collective-permute-start(bf16[128,1408]{1,0:T(8,128)(2,1)S(1)} %get-tuple-element.44), channel_id=1, source_target_pairs={{0,1},{1,0},{2,3},{3,2},{4,7},{5,6},{6,5},{7,4},{8,9},{9,8},{10,11... | collective-permute-start | bytes 1081352 | tf_op jit(solution)/shard_map/halves1/ppermute | solution.py:51
  36.3 9.8 %collective-permute-start.2 = (bf16[128,1792]{1,0:T(8,128)(2,1)S(1)}, bf16[128,1792]{1,0:T(8,128)(2,1)S(1)}, u32[]{:S(2)}, u32[]{:S(2)}) collective-permute-start(bf16[128,1792]{1,0:T(8,128)(2,1)S(1)} %pad_maximum_fusion), channel_id=1, source_target_pairs={{0,3},{1,2},{2,1},{3,0},{4,5},{5,4},{6,7},{7,6},{8,11},{9,10},{10,... | collective-permute-start | bytes 1376264 | tf_op jit(solution)/shard_map/sums0/ppermute | solution.py:51
  40.4 10.2 %collective-permute-start.4 = (bf16[128,1408]{1,0:T(8,128)(2,1)S(1)}, bf16[128,1408]{1,0:T(8,128)(2,1)S(1)}, u32[]{:S(2)}, u32[]{:S(2)}) collective-permute-start(bf16[128,1408]{1,0:T(8,128)(2,1)S(1)} %fusion.5), channel_id=1, source_target_pairs={{0,3},{1,2},{2,1},{3,0},{4,5},{5,4},{6,7},{7,6},{8,11},{9,10},{10,... | collective-permute-start | bytes 1081352 | tf_op jit(solution)/shard_map/sums1/ppermute | solution.py:51
  46.3 8.2 %collective-permute-start.6 = (bf16[128,1664]{1,0:T(8,128)(2,1)S(1)}, bf16[128,1664]{1,0:T(8,128)(2,1)S(1)}, u32[]{:S(2)}, u32[]{:S(2)}) collective-permute-start(bf16[128,1664]{1,0:T(8,128)(2,1)S(1)} %fusion.1.mine), channel_id=1, source_target_pairs={{0,1},{1,0},{2,3},{3,2},{4,7},{5,6},{6,5},{7,4},{8,9},{9,8},{10,11... | collective-permute-start | bytes 1277960 | tf_op jit(solution)/shard_map/cubes0/ppermute | solution.py:51
  50.8 7.6 %collective-permute-start.5 = (bf16[128,1408]{1,0:T(8,128)(2,1)S(1)}, bf16[128,1408]{1,0:T(8,128)(2,1)S(1)}, u32[]{:S(2)}, u32[]{:S(2)}) collective-permute-start(bf16[128,1408]{1,0:T(8,128)(2,1)S(1)} %fusion.3.mine), channel_id=1, source_target_pairs={{0,1},{1,0},{2,3},{3,2},{4,7},{5,6},{6,5},{7,4},{8,9},{9,8},{10,11... | collective-permute-start | bytes 1081352 | tf_op jit(solution)/shard_map/cubes1/ppermute | solution.py:51
  51.5 8.8 %copy-start = (f32[8,2048]{1,0:T(8,128)S(1)}, f32[8,2048]{1,0:T(8,128)}, u32[]{:S(2)}) copy-start(f32[8,2048]{1,0:T(8,128)} %factors.5) | copy-start | bytes 196612
  60.2 2.2 %collective-permute-start.7 = (bf16[256,1024]{1,0:T(8,128)(2,1)S(1)}, bf16[256,1024]{1,0:T(8,128)(2,1)S(1)}, u32[]{:S(2)}, u32[]{:S(2)}) collective-permute-start(bf16[256,1024]{1,0:T(8,128)(2,1)S(1)} %cross.5), channel_id=1, source_target_pairs={{0,4},{4,0},{8,12},{12,8},{16,20},{20,16},{24,28},{28,24},{32,36},... | collective-permute-start | bytes 1572872 | tf_op jit(solution)/shard_map/ppermute | solution.py:55

commit v4 on v3

--- a/solution.py
+++ b/solution.py
@@ -123,34 +123,86 @@
     return copies
 
 
-def load_kernel(packed, factors, samples, near, rows, left, gram, mine, sem, sems):
+def place_of():
+    dp = lax.axis_index("dp")
+    return dp, lax.axis_index("feat"), dp & 1, dp >> 1
+
+
+def order_of():
+    _, y, core, _ = place_of()
+    first = jnp.where(core == 0, y ^ 1, 3 - y)
+    second = jnp.where(core == 0, 3 - y, y ^ 1)
+    order = []
+    for pair in ((first, y ^ 2), (y, second)):
+        order += [jnp.minimum(*pair), jnp.maximum(*pair)]
+    return order
+
+
+def chosen(weights, numbers):
+    lanes = lax.broadcasted_iota(jnp.int32, (numbers.shape[0], weights.shape[1]), 1)
+    return jnp.sum(jnp.where(lanes == numbers, weights, 0.0), 1, keepdims=True)
+
+
+def number(place, count, core):
+    half = count // 2
+    inside = place & (half - 1)
+    side = jnp.where(place < half, 1 - core, core)
+    return (inside >> 3) * 16 + side * 8 + (inside & 7)
+
+
+def load_kernel(counts, weights, packed, factors, samples, *refs):
+    near, rows, left, gram, scale, *masks, mine, row, numbers, sem, small, sems = refs
     first = pltpu.make_async_copy(factors, mine, sem)
     first.start()
+    others = [
+        pltpu.make_async_copy(weights, row, small.at[0]),
+        pltpu.make_async_copy(counts, numbers, small.at[1]),
+    ]
+    for copy in others:
+        copy.start()
     copies = fetch(samples, near, sems, 0)
     unpack(packed, rows, 0)
     first.wait()
     left[...] = gram_message(mine[...])
     gram[...] = gram_of(nt_dot(left[...], rows[...]))
+    for copy in others:
+        copy.wait()
+    order = order_of()
+    dp, _, core, _ = place_of()
+    for part, mask in enumerate(masks):
+        slot = start_of(part) + lax.broadcasted_iota(jnp.int32, mask.shape, 1)
+        mask[...] = jnp.where(slot < numbers[dp], 1.0, 0.0)
+    half = scale.shape[0]
+    block = half // 2
+    step = lax.broadcasted_iota(jnp.int32, (half, 1), 0)
+    at = jnp.where(step < block, order[2] * block + step, (order[3] - 1) * block + step)
+    scale[...] = chosen(row[...].reshape(1, 2 * half), number(at, 2 * half, core))
     for copy in copies:
         copy.wait()
 
 
-def load(packed, factors, samples):
+def load(counts, weights, packed, factors, samples):
     depth = samples.shape[1]
-    count = packed.shape[0] // 2
+    owned = factors.shape[0]
+    half = packed.shape[0] // 2
     return pl.pallas_call(
         load_kernel,
-        in_specs=[VMEM, ANY, ANY],
-        out_specs=[VMEM] * 4,
+        in_specs=[ANY, ANY, VMEM, ANY, ANY],
+        out_specs=[VMEM] * (5 + PARTS),
         out_shape=[
             pltpu.VMEM((SIZES[0], depth), BF16),
-            jax.ShapeDtypeStruct((count, depth), BF16),
-            jax.ShapeDtypeStruct((2 * factors.shape[0], depth), BF16),
-            jax.ShapeDtypeStruct((factors.shape[0], count), F32),
-        ],
+            jax.ShapeDtypeStruct((half, depth), BF16),
+            jax.ShapeDtypeStruct((2 * owned, depth), BF16),
+            jax.ShapeDtypeStruct((owned, half), F32),
+            jax.ShapeDtypeStruct((half, 1), F32),
+        ]
+        + [jax.ShapeDtypeStruct((1, size), F32) for size in SIZES],
         scratch_shapes=[
             pltpu.VMEM(factors.shape, F32),
+            pltpu.VMEM(weights.shape, F32),
+            pltpu.SMEM(counts.shape, jnp.int32),
             pltpu.SemaphoreType.DMA,
+            pltpu.SemaphoreType.DMA((2,)),
             pltpu.SemaphoreType.DMA((LOADS,)),
         ],
         compiler_params=PARAMS,
@@ -158,18 +210,37 @@
             flops=0, bytes_accessed=4 * SIZES[0] * depth, transcendentals=0
         ),
         name="load",
-    )(packed, in_hbm(factors), in_hbm(samples))
+    )(in_hbm(counts), in_hbm(weights), packed, in_hbm(factors), in_hbm(samples))
+
+
+def cube_kernel(scale, value, passed, out):
+    slots = value.shape[1]
+    total = value[...] + passed[:, :slots].astype(F32)
+    out[...] = (scale[...] * (total * total * total)).astype(BF16)
+
+
+def cube(scale, value, passed):
+    return pl.pallas_call(
+        cube_kernel,
+        in_specs=[VMEM] * 3,
+        out_specs=VMEM,
+        out_shape=jax.ShapeDtypeStruct(value.shape, BF16),
+        compiler_params=PARAMS,
+        cost_estimate=pl.CostEstimate(
+            flops=4 * value.size, bytes_accessed=8 * value.size, transcendentals=0
+        ),
+        name="cube",
+    )(scale, value, passed)
 
 
 def nt_dot(left, right):
     return lax.dot_general(left, right, (((1,), (1,)), ((), ())), preferred_element_type=F32)
 
 
-def project_part(scalars, other, own, near, sent, kept, scratch, part):
+def project_part(mask, other, own, near, sent, kept, scratch):
     half, slots = kept.shape
     block = half // 2
-    for i in range(4):
-        quarter = scalars[i]
+    for i, quarter in enumerate(order_of()):
         at = pl.ds(pl.multiple_of(lax.rem(quarter, 2) * block, block), block)
         to = slice(i * block, (i + 1) * block)
         for side, ref in enumerate((other, own)):
@@ -179,8 +250,7 @@
                 scratch[to, :] = ref[at, :]
 
     value = nt_dot(scratch[...], near[...])
-    slot = start_of(part) + lax.broadcasted_iota(jnp.int32, (1, slots), 1)
-    value = jnp.where(slot < scalars[4], value, 0.0)
+    value = value * mask[...]
     sent[:, :slots] = value[:half].astype(BF16)
     kept[...] = value[half:]
 
@@ -192,10 +262,10 @@
     sent[32:, slots:] = jnp.zeros((sent.shape[0] - 32, LANES), BF16)
 
 
-def first_kernel(scalars, packed, own, left, gram_own, near, samples, sent, kept, other, gram, later, scratch, sems):
+def first_kernel(mask, packed, own, left, gram_own, near, samples, sent, kept, other, gram, later, scratch, sems):
     copies = fetch(samples, later, sems, 1)
     unpack(packed, other, 0)
-    project_part(scalars, other, own, near, sent, kept, scratch, 0)
+    project_part(mask, other, own, near, sent, kept, scratch)
     gram[...] = jnp.concatenate([gram_of(nt_dot(left[...], other[...])), gram_own[...]], 1)
     if GRAM_PART == 0:
         put_gram(sent, gram)
@@ -203,12 +273,12 @@
         copy.wait()
 
 
-def project_first(scalars, packed, own, left, gram_own, near, samples):
+def project_first(mask, packed, own, left, gram_own, near, samples):
     slots, depth = near.shape
     count = 2 * own.shape[0]
     return pl.pallas_call(
         first_kernel,
-        in_specs=[SMEM] + [VMEM] * 5 + [ANY],
+        in_specs=[VMEM] * 6 + [ANY],
         out_specs=[VMEM] * 5,
         out_shape=[
             jax.ShapeDtypeStruct((count // 2, slots + LANES * (GRAM_PART == 0)), BF16),
@@ -224,21 +294,21 @@
         compiler_params=PARAMS,
         cost_estimate=estimate(slots, depth, count),
         name="project_first",
-    )(scalars, packed, own, left, gram_own, in_vmem(near), in_hbm(samples))
-
-
-def second_kernel(scalars, other, own, gram, near, sent, kept, scratch):
-    project_part(scalars, other, own, near, sent, kept, scratch, 1)
+    )(mask, packed, own, left, gram_own, in_vmem(near), in_hbm(samples))
+
+
+def second_kernel(mask, other, own, gram, near, sent, kept, scratch):
+    project_part(mask, other, own, near, sent, kept, scratch)
     if GRAM_PART == 1:
         put_gram(sent, gram)
 
 
-def project_second(scalars, other, own, gram, near):
+def project_second(mask, other, own, gram, near):
     slots, depth = near.shape
     count = 2 * own.shape[0]
     return pl.pallas_call(
         second_kernel,
-        in_specs=[SMEM] + [VMEM] * 4,
+        in_specs=[VMEM] * 5,
         out_specs=[VMEM] * 2,
         out_shape=[
             jax.ShapeDtypeStruct((count // 2, slots + LANES * (GRAM_PART == 1)), BF16),
@@ -248,7 +318,7 @@
         compiler_params=PARAMS,
         cost_estimate=estimate(slots, depth, count),
         name="project_second",
-    )(scalars, other, own, gram, in_vmem(near))
+    )(mask, other, own, gram, in_vmem(near))
 
 
 def estimate(slots, depth, rows):
@@ -257,36 +327,74 @@
     )
 
 
-def model_kernel(pairs, here, gram, other, own, factors, out):
-    value = pairs[...] * gram[...] * gram[...] * gram[...]
-    diagonal = jnp.sum(here[...] * value, 1, keepdims=True)
+def model_kernel(counts, weights, gram, other, own, factors, out, inverse):
+    _, _, core, chip = place_of()
+    owned, count = gram.shape
+    half = count // 2
+    row = weights[...].reshape(1, count)
+    column = chosen(row, number(lax.broadcasted_iota(jnp.int32, (count, 1), 0), count, core))
+    down = lax.broadcasted_iota(jnp.int32, (count, count), 0)
+    along = lax.broadcasted_iota(jnp.int32, (count, count), 1)
+    weight = jnp.sum(jnp.where(down == along, column, 0.0), 0, keepdims=True)
+    mine = half + chip * owned + lax.broadcasted_iota(jnp.int32, (owned, 1), 0)
+    pairs = chosen(row, number(mine, count, core)) * weight
+    value = pairs * gram[...] * gram[...] * gram[...]
+    lanes = lax.broadcasted_iota(jnp.int32, (owned, count), 1)
+    diagonal = jnp.sum(jnp.where(lanes == mine, value, 0.0), 1, keepdims=True)
     left = gram_message(value)
-    half = other.shape[0]
     both = jnp.dot(left[:, :half], other[...], preferred_element_type=F32) + jnp.dot(
         left[:, half:], own[...], preferred_element_type=F32
     )
     rest = factors[...] - factors[...].astype(BF16).astype(F32)
     out[...] = 8.0 * (gram_of(both) + diagonal * rest)
-
-
-def model(pairs, here, gram, other, own, factors):
+    total = counts[0]
+    for i in range(1, N_DP):
+        total = total + counts[i]
+    inverse[...] = 8.0 / jnp.full(inverse.shape, total, jnp.int32).astype(F32)
+
+
+def model(counts, weights, gram, other, own, factors):
     return pl.pallas_call(
         model_kernel,
-        in_specs=[VMEM] * 6,
+        in_specs=[SMEM] + [VMEM] * 5,
+        out_specs=[VMEM] * 2,
+        out_shape=[
+            jax.ShapeDtypeStruct(factors.shape, F32),
+            jax.ShapeDtypeStruct((1, factors.shape[1]), F32),
+        ],
+        compiler_params=PARAMS,
+        name="model",
+    )(counts, weights, gram, other, own, factors)
+
+
+def finish_kernel(blocks, model_term, inverse, out):
+    rows, width = model_term.shape[0], blocks.shape[1]
+    total = jnp.zeros((2 * rows, width), F32)
+    for chip in range(CHIPS):
+        total = total + blocks[pl.ds(16 * chip, 16), :].astype(F32)
+    total = jnp.concatenate([total[:rows], total[rows:]], 1)
+    out[...] = model_term[...] - inverse[...] * total
+
+
+def finish(blocks, model_term, inverse):
+    return pl.pallas_call(
+        finish_kernel,
+        in_specs=[VMEM] * 3,
         out_specs=VMEM,
-        out_shape=jax.ShapeDtypeStruct(factors.shape, F32),
-        compiler_params=PARAMS,
-        name="model",
-    )(pairs, here, gram, other, own, factors)
-
-
-def cross_kernel(scalars, mine, other, near, *refs, sides, add, tile):
+        out_shape=jax.ShapeDtypeStruct(model_term.shape, F32),
+        compiler_params=PARAMS,
+        name="finish",
+    )(blocks, model_term, inverse)
+
+
+def cross_kernel(mine, other, near, *refs, sides, add, tile):
     terms, refs = (refs[: len(sides)] if add else None), refs[add * len(sides) :]
     outs, rows = refs[:-1], refs[-1]
     block = mine.shape[0] // 2
     half = 2 * block
-    for i, piece in enumerate((other[:block], other[block:], mine[:block], mine[block:])):
-        at = pl.multiple_of(scalars[i] * block, block)
+    pieces = (other[:block], other[block:], mine[:block], mine[block:])
+    for quarter, piece in zip(order_of(), pieces):
+        at = pl.multiple_of(quarter * block, block)
         rows[pl.ds(at, block), :] = piece
     width = outs[0].shape[1]
     first = sides[0] * half
@@ -309,20 +417,20 @@
                 out[to, here] = value.astype(out.dtype)
 
 
-def cross(scalars, pieces, near, sides, out_type, terms=(), tile=512):
+def cross(pieces, near, sides, out_type, terms=(), tile=512):
     slots, depth = near.shape
     rows = 2 * pieces[0].shape[0]
     out = jax.ShapeDtypeStruct((rows, depth // 2), out_type)
     return pl.pallas_call(
         functools.partial(cross_kernel, sides=sides, add=bool(terms), tile=tile),
-        in_specs=[SMEM] + [VMEM] * (3 + len(terms)),
+        in_specs=[VMEM] * (3 + len(terms)),
         out_specs=[VMEM] * len(sides),
         out_shape=[out] * len(sides),
         scratch_shapes=[pltpu.VMEM((rows, slots), BF16)],
         compiler_params=PARAMS,
         cost_estimate=estimate(slots, depth, rows),
         name="cross",
-    )(scalars, *pieces, in_vmem(near), *terms)
+    )(*pieces, in_vmem(near), *terms)
 
 
 def add_kernel(left, right, out):
@@ -342,45 +450,15 @@
 
 def on_device(samples, factors, weights, counts):
     owned, depth = factors.shape
-    all_rows = weights.shape[0]
-    half_rows = all_rows // 2
-    block = all_rows // 4
-    dp = lax.axis_index("dp")
-    y = lax.axis_index("feat")
-    core = lax.rem(dp, 2)
-    chip = dp // 2
-    first = jnp.where(core == 0, y ^ 1, 3 - y)
-    second = jnp.where(core == 0, 3 - y, y ^ 1)
-    across = lax.rem(y + 2, 4)
-    order = []
-    for pair in ((first, across), (y, second)):
-        order += [jnp.minimum(*pair), jnp.maximum(*pair)]
-    scalars = jnp.stack(order + [counts[dp]]).astype(jnp.int32)
-    total = jnp.sum(counts).astype(F32)
-    by_core = weights.reshape(CHIPS, 2, owned).transpose(1, 0, 2).reshape(2, half_rows)
-    weight_own = lax.dynamic_slice(by_core, (core, 0), (1, half_rows))[0]
-    weight_other = lax.dynamic_slice(by_core, (1 - core, 0), (1, half_rows))[0]
-    weight = jnp.concatenate([weight_other, weight_own])
-    scale = jnp.concatenate(
-        [lax.dynamic_slice(weight, (order[i] * block,), (block,)) for i in (2, 3)]
+    packed_own = plane_exchange(spread(factors))
+    near0, own, left, gram_own, scale, mask0, mask1 = load(
+        counts, weights, packed_own, factors, samples
     )
-    scales = [scale] * PARTS
-    weight_mine = lax.dynamic_slice(weight_own, (chip * owned,), (owned,))
-    pairs = weight_mine[:, None] * weight[None, :]
-    mine = lax.broadcasted_iota(jnp.int32, pairs.shape, 0) + half_rows + chip * owned
-    here = (lax.broadcasted_iota(jnp.int32, pairs.shape, 1) == mine).astype(F32)
-    factor = jnp.full((1, 1), 8.0, F32) / total[None, None]
-
-    packed_own = plane_exchange(spread(factors))
-    packed_own, scalars, scales, pairs, here, factor, samples = lax.optimization_barrier(
-        (packed_own, scalars, scales, pairs, here, factor, samples)
-    )
-    near0, own, left, gram_own = load(packed_own, factors, samples)
     packed_other = core_swap(packed_own)
     sent0, kept0, other, gram, near1 = project_first(
-        scalars, packed_other, own, left, gram_own, near0, samples
+        mask0, packed_other, own, left, gram_own, near0, samples
     )
-    sent1, kept1 = project_second(scalars, other, own, gram, near1)
+    sent1, kept1 = project_second(mask1, other, own, gram, near1)
     nears = (near0, near1)
 
     pieces = []
@@ -401,24 +479,20 @@
             passed = feat_swap(message, partner_second)
         if carries:
             gram = gram + gram_from(passed[:32, slots:])
-        value = value + passed[:, :slots].astype(F32)
-        cubes = (scales[part][:, None] * value**3).astype(BF16)
+        if part == PARTS - 1:
+            model_term, inverse = model(counts, weights, gram, other, own, factors)
+            scale, model_term, inverse = lax.optimization_barrier((scale, model_term, inverse))
+        cubes = cube(scale, value, passed)
         with jax.named_scope(f"cubes{part}"):
             pieces.append((cubes, feat_swap(cubes, partner_first)))
 
     terms = ()
     for part in range(PARTS - 1):
-        terms = cross(scalars, pieces[part], nears[part], (0, 1), F32, terms)
-    (sum_other,) = cross(scalars, pieces[-1], nears[-1], (0,), BF16, terms[:1])
-    (sum_own,) = cross(scalars, pieces[-1], nears[-1], (1,), F32, terms[1:])
+        terms = cross(pieces[part], nears[part], (0, 1), F32, terms)
+    (sum_other,) = cross(pieces[-1], nears[-1], (0,), BF16, terms[:1])
+    (sum_own,) = cross(pieces[-1], nears[-1], (1,), F32, terms[1:])
     total_own = add(sum_own, core_swap(sum_other))
-    model_term = model(pairs, here, gram, other, own, factors)
-    model_term, total_own = lax.optimization_barrier((model_term, total_own))
-    blocks = plane_exchange(total_own).reshape(CHIPS, 2 * owned, depth // 2)
-    cross_term = jnp.sum(blocks.astype(F32), axis=0)
-    cross_term = jnp.concatenate([cross_term[:owned], cross_term[owned:]], 1)
-
-    return model_term - factor * cross_term
+    return finish(plane_exchange(total_own), model_term, inverse)
 
 
 def solution(mesh):

time: 78.7 us -> 75.9 us (0.964)
  blocking collectives: 15.1 us -> 34.1 us
  starting transfers between devices: 17.5 us -> 9.66 us
  waiting for transfers between devices: 21.5 us -> 15.9 us
  local copies, waits for them, and re-layouts: 3.05 us -> 0.01 us
  other arithmetic: 2.92 us -> 0.27 us
  Pallas kernels: 17.3 us -> 15.6 us
  between operations: 0.97 us -> 0.16 us
    all_to_all x1 -> x2, blocking collectives: 15.1 us -> 34.1 us  [plane_exchange(): return lax.all_to_all(x, 'dp', 0, 0, axis_index_groups=PLANES, tiled=True)]
    all_to_all x1 -> x0, starting transfers between devices: 7.96 us -> none  [plane_exchange(): return lax.all_to_all(x, 'dp', 0, 0, axis_index_groups=PLANES, tiled=True)]
    all_to_all x1 -> x0, waiting for transfers between devices: 6.16 us -> none  [plane_exchange(): return lax.all_to_all(x, 'dp', 0, 0, axis_index_groups=PLANES, tiled=True)]
    pallas_call x3, Pallas kernels: 6.45 us -> 4.97 us  [cross(): pl.pallas_call(functools.partial(cross_kernel, sides=sides, add=bool(term...]
    reduce_sum x2 -> x0, other arithmetic: 1.39 us -> none  [the longest x1 1.31 us: on_device(): total = jnp.sum(counts).astype(F32)]
    dynamic_slice x2 -> x0, local copies, waits for them, and re-layouts: 1.38 us -> none  [the longest x1 1.3 us: on_device(): scalars = jnp.stack(order + [counts[dp]]).astype(jnp.int32)]
    reshape x2 -> x0, local copies, waits for them, and re-layouts: 0.86 us -> none  [on_device(): weights.reshape(CHIPS, 2, owned).transpose(1, 0, 2).reshape(2, half_rows)]
    pallas_call x1, Pallas kernels: 1.68 us -> 0.88 us  [spread(): pl.pallas_call(spread_kernel, in_specs=[VMEM], out_specs=VMEM, out_shape=...]
  transfers between devices with their start and end apart: 9 -> 8, of which waited for: 7 -> 7; matrix products, arithmetic and copies ran while one was open for 7% -> 0% of each run, Pallas kernels for 13% -> 13%
where the time goes in v4:
time: 75.9 us; the launch traced here: 75.7 us
  blocking collectives  34.1 us (45%)
  waiting for transfers between devices  15.9 us (21%)
  Pallas kernels  15.6 us (21%)
  starting transfers between devices  9.66 us (13%)
    all_to_all x2, blocking collectives, plane_exchange(): return lax.all_to_all(x, 'dp', 0, 0, axis_index_groups=PLANES, tiled=True)  34.1 us
    ppermute x6, waiting for transfers between devices, feat_swap(): return lax.ppermute(x, ('dp', 'feat'), pairs)  15.3 us
    ppermute x6, starting transfers between devices, feat_swap(): return lax.ppermute(x, ('dp', 'feat'), pairs)  9.57 us
    pallas_call x3, Pallas kernels, cross(): pl.pallas_call(functools.partial(cross_kernel, sides=sides, add=bool(term...  4.97 us
    pallas_call x1, Pallas kernels, load(): pl.pallas_call(load_kernel, in_specs=[ANY, ANY, VMEM, ANY, ANY], out_spec...  3.08 us
    pallas_call x1, Pallas kernels, project_first(): pl.pallas_call(first_kernel, in_specs=[VMEM] * 6 + [ANY], out_specs=[VMEM...  2.71 us
    pallas_call x1, Pallas kernels, project_second(): pl.pallas_call(second_kernel, in_specs=[VMEM] * 5, out_specs=[VMEM] * 2,...  1.94 us
  transfers between devices with their start and end apart: 8, of which 7 were waited for; matrix products, arithmetic and copies ran while one was open for 0% of the time, Pallas kernels for 13%

profile of v4, /device:TPU:0, one launch (start us, length us, event | category | flops | bytes accessed | tf_op | source)
XLA Modules:
  0.0 75.7 jit_solution(3132381849871528864)
XLA Ops:
  0.0 0.9 %spread.1 = bf16[256,1024]{1,0:T(8,128)(2,1)S(1)} custom-call(f32[8,2048]{1,0:T(8,128)} %factors.5), custom_call_target="tpu_custom_call" | custom-call | tf_op jit(solution)/shard_map/spread/pallas_call | solution.py:70
  0.9 19.3 %all_to_all.22 = bf16[16,16,1024]{2,1,0:T(8,128)(2,1)S(1)} all-to-all(bf16[16,16,1024]{2,1,0:T(8,128)(2,1)S(1)} %bitcast.5), channel_id=1, replica_groups={{0,8,16,24,32,40,48,56,64,72,80,88,96,104,112,120},{4,12,20,28,36,44,52..., dimensions={0} | all-to-all | bytes 1048576 | tf_op jit(solution)/shard_map/all_to_all | solution.py:59
  20.2 0.0 collective-permute-start
  20.2 3.1 %load.1 = (bf16[1664,2048]{1,0:T(8,128)(2,1)S(1)}, bf16[128,2048]{1,0:T(8,128)(2,1)S(1)}, bf16[16,2048]{1,0:T(8,128)(2,1)S(1)}, f32[8,128]{1,0:T(8,128)S(1)}, f3...) custom-call(s32[32]{0:T(128)} %counts.3, f32[256]{0:T(256)} %weights.3, ...), custom_call_target="tpu_custom_call" | custom-call | bytes 13631488 | tf_op jit(solution)/shard_map/load/pallas_call | solution.py:188
  23.3 0.0 collective-permute-done.packed
  23.3 2.7 %project_first.1 = (bf16[128,1792]{1,0:T(8,128)(2,1)S(1)}, f32[128,1664]{1,0:T(8,128)S(1)}, bf16[128,2048]{1,0:T(8,128)(2,1)S(1)}, f32[8,256]{1,0:T(8,128)S(1)}, bf16[1408,2048]{1,0:T(8,128)(2,1)S(1)}) custom-call(f32[1,1664]{1,0:T(1,128)S(1)} %get-tuple-element.27.mask, bf16[256,1024]{1,0:T(8,128)(2,1)S(1)} %collective-permute-done.packed, ...), custom_call_target="tpu_custom_call" | custom-call | flops 1744830464 | bytes 6815744 | tf_op jit(solution)/shard_map/project_first/pallas_call | solution.py:279
  26.0 1.7 %collective-permute-start.1 = (bf16[128,1792]{1,0:T(8,128)(2,1)S(1)}, bf16[128,1792]{1,0:T(8,128)(2,1)S(1)}, u32[]{:S(2)}, u32[]{:S(2)}) collective-permute-start(bf16[128,1792]{1,0:T(8,128)(2,1)S(1)} %get-tuple-element.33), channel_id=1, source_target_pairs={{0,1},{1,0},{2,3},{3,2},{4,7},{5,6},{6,5},{7,4},{8,9},{9,8},{10,11... | collective-permute-start | bytes 1376264 | tf_op jit(solution)/shard_map/halves0/ppermute | solution.py:51
  27.7 0.0 copy-start
  27.7 0.0 copy-start.1
  27.7 0.0 copy-start.2
  27.7 1.9 %project_second.1 = (bf16[128,1408]{1,0:T(8,128)(2,1)S(1)}, f32[128,1408]{1,0:T(8,128)S(1)}) custom-call(f32[1,1408]{1,0:T(1,128)S(1)} %get-tuple-element.39.mask, bf16[128,2048]{1,0:T(8,128)(2,1)S(1)} %get-tuple-element.35.other, bf16[128,2048]{1,0:T(8,128)(2,1)S(1)} %get-tuple-element.28.own, f32[8,256]{1,0:T(8,128)S(1)} %get-tuple-element.32.gram, ...), custom_call_target="tpu_custom_call" | custom-call | flops 1476395008 | bytes 5767168 | tf_op jit(solution)/shard_map/project_second/pallas_call | solution.py:309
  29.6 0.5 collective-permute-start.3
  30.1 4.4 %collective-permute-done.1 = bf16[128,1792]{1,0:T(8,128)(2,1)S(1)} collective-permute-done((bf16[128,1792]{1,0:T(8,128)(2,1)S(1)}, bf16[128,1792]{1,0:T(8,128)(2,1)S(1)}, u32[]{:S(2)}, u32[]{:S(2)}) %collective-permute-start.1) | collective-permute-done | bytes 458784 | tf_op jit(solution)/shard_map/halves0/ppermute | solution.py:51
  34.6 0.1 fusion.5
  34.8 3.1 %collective-permute-start.2 = (bf16[128,1792]{1,0:T(8,128)(2,1)S(1)}, bf16[128,1792]{1,0:T(8,128)(2,1)S(1)}, u32[]{:S(2)}, u32[]{:S(2)}) collective-permute-start(bf16[128,1792]{1,0:T(8,128)(2,1)S(1)} %pad_maximum_fusion), channel_id=1, source_target_pairs={{0,3},{1,2},{2,1},{3,0},{4,5},{5,4},{6,7},{7,6},{8,11},{9,10},{10,... | collective-permute-start | bytes 1376264 | tf_op jit(solution)/shard_map/sums0/ppermute | solution.py:51
  37.9 0.9 %collective-permute-done.3 = bf16[128,1408]{1,0:T(8,128)(2,1)S(1)} collective-permute-done((bf16[128,1408]{1,0:T(8,128)(2,1)S(1)}, bf16[128,1408]{1,0:T(8,128)(2,1)S(1)}, u32[]{:S(2)}, u32[]{:S(2)}) %collective-permute-start.3) | collective-permute-done | bytes 360480 | tf_op jit(solution)/shard_map/halves1/ppermute | solution.py:51
  38.8 0.1 fusion.4
  38.9 3.1 %collective-permute-start.4 = (bf16[128,1408]{1,0:T(8,128)(2,1)S(1)}, bf16[128,1408]{1,0:T(8,128)(2,1)S(1)}, u32[]{:S(2)}, u32[]{:S(2)}) collective-permute-start(bf16[128,1408]{1,0:T(8,128)(2,1)S(1)} %get-tuple-element.47), channel_id=1, source_target_pairs={{0,3},{1,2},{2,1},{3,0},{4,5},{5,4},{6,7},{7,6},{8,11},{9,10},{10,... | collective-permute-start | bytes 1081352 | tf_op jit(solution)/shard_map/sums1/ppermute | solution.py:51
  42.0 2.6 %collective-permute-done.2.passed = bf16[128,1792]{1,0:T(8,128)(2,1)S(1)} collective-permute-done((bf16[128,1792]{1,0:T(8,128)(2,1)S(1)}, bf16[128,1792]{1,0:T(8,128)(2,1)S(1)}, u32[]{:S(2)}, u32[]{:S(2)}) %collective-permute-start.2) | collective-permute-done | bytes 458784 | tf_op jit(solution)/shard_map/sums0/ppermute | solution.py:51
  44.5 0.2 cube.3.mine
  44.7 0.4 collective-permute-start.6
  45.2 0.0 copy-done
  45.2 0.0 copy-done.1
  45.2 0.0 copy-done.2
  45.2 0.9 %model.1 = (f32[8,2048]{1,0:T(8,128)S(1)}, f32[1,2048]{1,0:T(1,128)S(1)}) custom-call(s32[32]{0:T(128)S(1)} %copy-done.2, f32[256]{0:T(256)S(1)} %copy-done.1, f32[8,256]{1,0:T(8,128)S(1)} %maximum_add_fusion.1.gram, bf16[128,2048]{1,0:T(8,128)(2,1)S(1)} %get-tuple-element.35.other, bf16[128,2048]{1,0:T(8,128)(2,1)S(1)} %get-tuple-element.28.own, ...), custom_call_target="tpu_custom_call" | custom-call | tf_op jit(solution)/shard_map/model/pallas_call | solution.py:357
  46.1 3.1 %collective-permute-done.4.passed = bf16[128,1408]{1,0:T(8,128)(2,1)S(1)} collective-permute-done((bf16[128,1408]{1,0:T(8,128)(2,1)S(1)}, bf16[128,1408]{1,0:T(8,128)(2,1)S(1)}, u32[]{:S(2)}, u32[]{:S(2)}) %collective-permute-start.4) | collective-permute-done | bytes 360480 | tf_op jit(solution)/shard_map/sums1/ppermute | solution.py:51
  49.1 0.1 cube.2.mine
  49.3 0.8 %collective-permute-start.5 = (bf16[128,1408]{1,0:T(8,128)(2,1)S(1)}, bf16[128,1408]{1,0:T(8,128)(2,1)S(1)}, u32[]{:S(2)}, u32[]{:S(2)}) collective-permute-start(bf16[128,1408]{1,0:T(8,128)(2,1)S(1)} %cube.2.mine), channel_id=1, source_target_pairs={{0,1},{1,0},{2,3},{3,2},{4,7},{5,6},{6,5},{7,4},{8,9},{9,8},{10,11... | collective-permute-start | bytes 1081352 | tf_op jit(solution)/shard_map/cubes1/ppermute | solution.py:51
  50.1 2.9 %collective-permute-done.6.other = bf16[128,1664]{1,0:T(8,128)(2,1)S(1)} collective-permute-done((bf16[128,1664]{1,0:T(8,128)(2,1)S(1)}, bf16[128,1664]{1,0:T(8,128)(2,1)S(1)}, u32[]{:S(2)}, u32[]{:S(2)}) %collective-permute-start.6) | collective-permute-done | bytes 426016 | tf_op jit(solution)/shard_map/cubes0/ppermute | solution.py:51
  52.9 2.4 %cross.3 = (f32[256,1024]{1,0:T(8,128)S(1)}, f32[256,1024]{1,0:T(8,128)S(1)}) custom-call(bf16[128,1664]{1,0:T(8,128)(2,1)S(1)} %cube.3.mine, bf16[128,1664]{1,0:T(8,128)(2,1)S(1)} %collective-permute-done.6.other, bf16[1664,2048]{1,0:T(8,128)(2,1)S(1)} %get-tuple-element.31.near), custom_call_target="tpu_custom_call" | custom-call | flops 1744830464 | bytes 6815744 | tf_op jit(solution)/shard_map/cross/pallas_call | solution.py:424
  55.3 1.5 %collective-permute-done.5.other = bf16[128,1408]{1,0:T(8,128)(2,1)S(1)} collective-permute-done((bf16[128,1408]{1,0:T(8,128)(2,1)S(1)}, bf16[128,1408]{1,0:T(8,128)(2,1)S(1)}, u32[]{:S(2)}, u32[]{:S(2)}) %collective-permute-start.5) | collective-permute-done | bytes 360480 | tf_op jit(solution)/shard_map/cubes1/ppermute | solution.py:51
  56.8 1.3 %cross.5 = bf16[256,1024]{1,0:T(8,128)(2,1)S(1)} custom-call(bf16[128,1408]{1,0:T(8,128)(2,1)S(1)} %cube.2.mine, bf16[128,1408]{1,0:T(8,128)(2,1)S(1)} %collective-permute-done.5.other, bf16[1408,2048]{1,0:T(8,128)(2,1)S(1)} %get-tuple-element.40.near, f32[256,1024]{1,0:T(8,128)S(1)} %get-tuple-element.44.refs_0_), custom_call_target="tpu_custom_call" | custom-call | flops 1476395008 | bytes 5767168 | tf_op jit(solution)/shard_map/cross/pallas_call | solution.py:424
  58.1 0.1 collective-permute-start.7
  58.2 1.3 %cross.4.left = f32[256,1024]{1,0:T(8,128)S(1)} custom-call(bf16[128,1408]{1,0:T(8,128)(2,1)S(1)} %cube.2.mine, bf16[128,1408]{1,0:T(8,128)(2,1)S(1)} %collective-permute-done.5.other, bf16[1408,2048]{1,0:T(8,128)(2,1)S(1)} %get-tuple-element.40.near, f32[256,1024]{1,0:T(8,128)S(1)} %get-tuple-element.43.refs_0_), custom_call_target="tpu_custom_call" | custom-call | flops 1476395008 | bytes 5767168 | tf_op jit(solution)/shard_map/cross/pallas_call | solution.py:424
  59.5 0.6 collective-permute-done.7.right
  60.1 0.1 add.51
  60.2 14.8 %all_to_all.23 = bf16[16,16,1024]{2,1,0:T(8,128)(2,1)S(1)} all-to-all(bf16[16,16,1024]{2,1,0:T(8,128)(2,1)S(1)} %bitcast.6), channel_id=1, replica_groups={{0,8,16,24,32,40,48,56,64,72,80,88,96,104,112,120},{4,12,20,28,36,44,52..., dimensions={0} | all-to-all | bytes 1048576 | tf_op jit(solution)/shard_map/all_to_all | solution.py:59
  75.0 0.7 finish.1
  (10 shorter events, 0.1 us)
Async XLA Ops:
  20.2 3.1 %collective-permute-start = (bf16[256,1024]{1,0:T(8,128)(2,1)S(1)}, bf16[256,1024]{1,0:T(8,128)(2,1)S(1)}, u32[]{:S(2)}, u32[]{:S(2)}) collective-permute-start(bf16[256,1024]{1,0:T(8,128)(2,1)S(1)} %bitcast.7), channel_id=1, source_target_pairs={{0,4},{4,0},{8,12},{12,8},{16,20},{20,16},{24,28},{28,24},{32,36},... | collective-permute-start | bytes 1572872 | tf_op jit(solution)/shard_map/ppermute | solution.py:55
  26.0 8.6 %collective-permute-start.1 = (bf16[128,1792]{1,0:T(8,128)(2,1)S(1)}, bf16[128,1792]{1,0:T(8,128)(2,1)S(1)}, u32[]{:S(2)}, u32[]{:S(2)}) collective-permute-start(bf16[128,1792]{1,0:T(8,128)(2,1)S(1)} %get-tuple-element.33), channel_id=1, source_target_pairs={{0,1},{1,0},{2,3},{3,2},{4,7},{5,6},{6,5},{7,4},{8,9},{9,8},{10,11... | collective-permute-start | bytes 1376264 | tf_op jit(solution)/shard_map/halves0/ppermute | solution.py:51
  27.7 17.5 %copy-start = (f32[8,2048]{1,0:T(8,128)S(1)}, f32[8,2048]{1,0:T(8,128)}, u32[]{:S(2)}) copy-start(f32[8,2048]{1,0:T(8,128)} %factors.5) | copy-start | bytes 196612
  27.7 17.5 %copy-start.1 = (f32[256]{0:T(256)S(1)}, f32[256]{0:T(256)}, u32[]{:S(2)}) copy-start(f32[256]{0:T(256)} %weights.3) | copy-start | bytes 3076
  27.7 17.5 %copy-start.2 = (s32[32]{0:T(128)S(1)}, s32[32]{0:T(128)}, u32[]{:S(2)}) copy-start(s32[32]{0:T(128)} %counts.3) | copy-start | bytes 388
  29.6 9.2 %collective-permute-start.3 = (bf16[128,1408]{1,0:T(8,128)(2,1)S(1)}, bf16[128,1408]{1,0:T(8,128)(2,1)S(1)}, u32[]{:S(2)}, u32[]{:S(2)}) collective-permute-start(bf16[128,1408]{1,0:T(8,128)(2,1)S(1)} %get-tuple-element.42), channel_id=1, source_target_pairs={{0,1},{1,0},{2,3},{3,2},{4,7},{5,6},{6,5},{7,4},{8,9},{9,8},{10,11... | collective-permute-start | bytes 1081352 | tf_op jit(solution)/shard_map/halves1/ppermute | solution.py:51
  34.8 9.8 %collective-permute-start.2 = (bf16[128,1792]{1,0:T(8,128)(2,1)S(1)}, bf16[128,1792]{1,0:T(8,128)(2,1)S(1)}, u32[]{:S(2)}, u32[]{:S(2)}) collective-permute-start(bf16[128,1792]{1,0:T(8,128)(2,1)S(1)} %pad_maximum_fusion), channel_id=1, source_target_pairs={{0,3},{1,2},{2,1},{3,0},{4,5},{5,4},{6,7},{7,6},{8,11},{9,10},{10,... | collective-permute-start | bytes 1376264 | tf_op jit(solution)/shard_map/sums0/ppermute | solution.py:51
  38.9 10.3 %collective-permute-start.4 = (bf16[128,1408]{1,0:T(8,128)(2,1)S(1)}, bf16[128,1408]{1,0:T(8,128)(2,1)S(1)}, u32[]{:S(2)}, u32[]{:S(2)}) collective-permute-start(bf16[128,1408]{1,0:T(8,128)(2,1)S(1)} %get-tuple-element.47), channel_id=1, source_target_pairs={{0,3},{1,2},{2,1},{3,0},{4,5},{5,4},{6,7},{7,6},{8,11},{9,10},{10,... | collective-permute-start | bytes 1081352 | tf_op jit(solution)/shard_map/sums1/ppermute | solution.py:51
  44.7 8.2 %collective-permute-start.6 = (bf16[128,1664]{1,0:T(8,128)(2,1)S(1)}, bf16[128,1664]{1,0:T(8,128)(2,1)S(1)}, u32[]{:S(2)}, u32[]{:S(2)}) collective-permute-start(bf16[128,1664]{1,0:T(8,128)(2,1)S(1)} %cube.3.mine), channel_id=1, source_target_pairs={{0,1},{1,0},{2,3},{3,2},{4,7},{5,6},{6,5},{7,4},{8,9},{9,8},{10,11... | collective-permute-start | bytes 1277960 | tf_op jit(solution)/shard_map/cubes0/ppermute | solution.py:51
  49.3 7.5 %collective-permute-start.5 = (bf16[128,1408]{1,0:T(8,128)(2,1)S(1)}, bf16[128,1408]{1,0:T(8,128)(2,1)S(1)}, u32[]{:S(2)}, u32[]{:S(2)}) collective-permute-start(bf16[128,1408]{1,0:T(8,128)(2,1)S(1)} %cube.2.mine), channel_id=1, source_target_pairs={{0,1},{1,0},{2,3},{3,2},{4,7},{5,6},{6,5},{7,4},{8,9},{9,8},{10,11... | collective-permute-start | bytes 1081352 | tf_op jit(solution)/shard_map/cubes1/ppermute | solution.py:51
  58.1 2.0 %collective-permute-start.7 = (bf16[256,1024]{1,0:T(8,128)(2,1)S(1)}, bf16[256,1024]{1,0:T(8,128)(2,1)S(1)}, u32[]{:S(2)}, u32[]{:S(2)}) collective-permute-start(bf16[256,1024]{1,0:T(8,128)(2,1)S(1)} %cross.5), channel_id=1, source_target_pairs={{0,4},{4,0},{8,12},{12,8},{16,20},{20,16},{24,28},{28,24},{32,36},... | collective-permute-start | bytes 1572872 | tf_op jit(solution)/shard_map/ppermute | solution.py:55

commit v5 on v4

--- a/solution.py
+++ b/solution.py
@@ -16,7 +16,7 @@
 GRAM_PART = 0
 LANES = 128
 PARTS = len(SIZES)
-LOADS = 2
+LOADS = 1
 PLANES = [[2 * chip + core for chip in range(CHIPS)] for core in range(2)]
 VMEM = pl.BlockSpec(memory_space=pltpu.VMEM)
 SMEM = pl.BlockSpec(memory_space=pltpu.SMEM)
@@ -128,8 +128,9 @@
     return dp, lax.axis_index("feat"), dp & 1, dp >> 1
 
 
-def order_of():
-    _, y, core, _ = place_of()
+def order_of(core=None):
+    _, y, mine, _ = place_of()
+    core = mine if core is None else core
     first = jnp.where(core == 0, y ^ 1, 3 - y)
     second = jnp.where(core == 0, 3 - y, y ^ 1)
     order = []
@@ -175,7 +176,8 @@
     half = scale.shape[0]
     block = half // 2
     step = lax.broadcasted_iota(jnp.int32, (half, 1), 0)
-    at = jnp.where(step < block, order[2] * block + step, (order[3] - 1) * block + step)
+    tops = [(quarter & 1) * half + (quarter >> 1) * block for quarter in order[2:]]
+    at = jnp.where(step < block, tops[0] + step, tops[1] + step - block)
     scale[...] = chosen(row[...].reshape(1, 2 * half), number(at, 2 * half, core))
     for copy in copies:
         copy.wait()
@@ -241,11 +243,11 @@
     half, slots = kept.shape
     block = half // 2
     for i, quarter in enumerate(order_of()):
-        at = pl.ds(pl.multiple_of(lax.rem(quarter, 2) * block, block), block)
+        at = pl.ds(pl.multiple_of((quarter >> 1) * block, block), block)
         to = slice(i * block, (i + 1) * block)
         for side, ref in enumerate((other, own)):
 
-            @pl.when(quarter // 2 == side)
+            @pl.when(quarter & 1 == side)
             def _():
                 scratch[to, :] = ref[at, :]
 
@@ -394,7 +396,7 @@
     half = 2 * block
     pieces = (other[:block], other[block:], mine[:block], mine[block:])
     for quarter, piece in zip(order_of(), pieces):
-        at = pl.multiple_of(quarter * block, block)
+        at = pl.multiple_of((quarter & 1) * half + (quarter >> 1) * block, block)
         rows[pl.ds(at, block), :] = piece
     width = outs[0].shape[1]
     first = sides[0] * half
@@ -417,7 +419,7 @@
                 out[to, here] = value.astype(out.dtype)
 
 
-def cross(pieces, near, sides, out_type, terms=(), tile=512):
+def cross(pieces, near, sides, out_type, terms=(), tile=1024):
     slots, depth = near.shape
     rows = 2 * pieces[0].shape[0]
     out = jax.ShapeDtypeStruct((rows, depth // 2), out_type)
@@ -433,19 +435,75 @@
     )(*pieces, in_vmem(near), *terms)
 
 
-def add_kernel(left, right, out):
-    out[...] = (left[...] + right[...].astype(F32)).astype(BF16)
-
-
-def add(left, right):
+def pair_kernel(piece, near, term_other, term_own, out_other, out_own, rows, *, first, tile):
+    block = piece.shape[0] // 2
+    pair = order_of()[first : first + 2]
+    for i, quarter in enumerate(pair):
+        at = pl.multiple_of((quarter & 1) * block, block)
+        rows[pl.ds(at, block), :] = piece[i * block : (i + 1) * block, : rows.shape[1]]
+    swapped = pair[0] & 1 == 1
+    tops = [
+        pl.multiple_of((jnp.where(swapped, pair[1 - i], pair[i]) >> 1) * 2 * block, 2 * block)
+        for i in range(2)
+    ]
+    width = out_own.shape[1]
+
+    @pl.loop(0, width // tile)
+    def _(i):
+        here = pl.ds(pl.multiple_of(i * tile, tile), tile)
+        there = pl.ds(pl.multiple_of(width + i * tile, tile), tile)
+        left, right = (
+            jnp.dot(rows[...], near[:, at], preferred_element_type=F32) for at in (here, there)
+        )
+        for side, (out, term) in enumerate(((out_other, term_other), (out_own, term_own))):
+            for chip in range(CHIPS // 2):
+                at = side * block + 8 * chip
+                to = slice(16 * chip, 16 * chip + 16)
+                value = jnp.concatenate([left[at : at + 8], right[at : at + 8]], 0)
+                value = value + term[pl.ds(tops[side] + 16 * chip, 16), here]
+                out[to, here] = value.astype(out.dtype)
+
+
+def cross_pair(piece, near, terms, first, kind, tile=1024):
+    slots, depth = near.shape
+    rows = piece.shape[0]
+    return pl.pallas_call(
+        functools.partial(pair_kernel, first=first, tile=tile),
+        in_specs=[VMEM] * 4,
+        out_specs=[VMEM] * 2,
+        out_shape=[
+            jax.ShapeDtypeStruct((rows, depth // 2), kind),
+            jax.ShapeDtypeStruct((rows, depth // 2), F32),
+        ],
+        scratch_shapes=[pltpu.VMEM((rows, slots), BF16)],
+        compiler_params=PARAMS,
+        cost_estimate=estimate(slots, depth, rows),
+        name="cross_pair",
+    )(piece, in_vmem(near), *terms)
+
+
+def add_kernel(kept, sent, from_kept, from_sent, out):
+    half = kept.shape[0]
+    _, _, core, _ = place_of()
+    pair = order_of()[2:]
+    mine = jnp.where(pair[0] & 1 == 1, pair[0], pair[1]) >> 1
+    pair = order_of(1 - core)[2:]
+    theirs = jnp.where(pair[0] & 1 == 0, pair[0], pair[1]) >> 1
+    for i in range(2):
+        own = jnp.where(mine == i, kept[...], sent[...])
+        other = jnp.where(theirs == i, from_kept[...].astype(F32), from_sent[...].astype(F32))
+        out[i * half : (i + 1) * half, :] = (own + other).astype(BF16)
+
+
+def add(kept, sent, from_kept, from_sent):
     return pl.pallas_call(
         add_kernel,
-        in_specs=[VMEM, VMEM],
+        in_specs=[VMEM] * 4,
         out_specs=VMEM,
-        out_shape=pltpu.VMEM(left.shape, BF16),
+        out_shape=pltpu.VMEM((2 * kept.shape[0], kept.shape[1]), BF16),
         compiler_params=PARAMS,
         name="add",
-    )(left, right)
+    )(kept, sent, from_kept, from_sent)
 
 
 def on_device(samples, factors, weights, counts):
@@ -489,9 +547,12 @@
     terms = ()
     for part in range(PARTS - 1):
         terms = cross(pieces[part], nears[part], (0, 1), F32, terms)
-    (sum_other,) = cross(pieces[-1], nears[-1], (0,), BF16, terms[:1])
-    (sum_own,) = cross(pieces[-1], nears[-1], (1,), F32, terms[1:])
-    total_own = add(sum_own, core_swap(sum_other))
+    cubes, got = pieces[-1]
+    other_kept, own_kept = cross_pair(cubes, nears[-1], terms, 2, F32)
+    from_kept = core_swap(other_kept)
+    other_sent, own_sent = cross_pair(got, nears[-1], terms, 0, BF16)
+    total_own = add(own_kept, own_sent, from_kept, core_swap(other_sent))
+
     return finish(plane_exchange(total_own), model_term, inverse)
 
 

time: 75.9 us -> 75.4 us (level)
    pallas_call x3 -> x1, Pallas kernels: 4.97 us -> 2.16 us  [cross(): pl.pallas_call(functools.partial(cross_kernel, sides=sides, add=bool(term...]
    pallas_call x1 -> x3, Pallas kernels: 0.09 us -> 2.34 us  [the longest x2 2.17 us: cross_pair(): pl.pallas_call(functools.partial(pair_kernel, first=first, tile=tile), in...]
    ppermute x6, waiting for transfers between devices: 15.3 us -> 14.4 us  [feat_swap(): return lax.ppermute(x, ('dp', 'feat'), pairs)]
    ppermute x2 -> x3, waiting for transfers between devices: 0.59 us -> 1.53 us  [core_swap(): return lax.ppermute(x, 'dp', [(i, i ^ 1) for i in range(N_DP)])]
  transfers between devices with their start and end apart: 8 -> 9, of which waited for: 7 -> 7; matrix products, arithmetic and copies ran while one was open for 0% -> 0% of each run, Pallas kernels for 13% -> 14%
where the time goes in v5:
time: 75.4 us; the launch traced here: 75.1 us
  blocking collectives  34.1 us (45%)
  waiting for transfers between devices  15.9 us (21%)
  Pallas kernels  14.9 us (20%)
  starting transfers between devices  9.75 us (13%)
    all_to_all x2, blocking collectives, plane_exchange(): return lax.all_to_all(x, 'dp', 0, 0, axis_index_groups=PLANES, tiled=True)  34.1 us
    ppermute x6, waiting for transfers between devices, feat_swap(): return lax.ppermute(x, ('dp', 'feat'), pairs)  14.4 us
    ppermute x6, starting transfers between devices, feat_swap(): return lax.ppermute(x, ('dp', 'feat'), pairs)  9.58 us
    pallas_call x1, Pallas kernels, load(): pl.pallas_call(load_kernel, in_specs=[ANY, ANY, VMEM, ANY, ANY], out_spec...  3.02 us
    pallas_call x1, Pallas kernels, project_first(): pl.pallas_call(first_kernel, in_specs=[VMEM] * 6 + [ANY], out_specs=[VMEM...  2.65 us
    pallas_call x2, Pallas kernels, cross_pair(): pl.pallas_call(functools.partial(pair_kernel, first=first, tile=tile), in...  2.17 us
    pallas_call x1, Pallas kernels, cross(): pl.pallas_call(functools.partial(cross_kernel, sides=sides, add=bool(term...  2.16 us
    pallas_call x1, Pallas kernels, project_second(): pl.pallas_call(second_kernel, in_specs=[VMEM] * 5, out_specs=[VMEM] * 2,...  1.91 us
  transfers between devices with their start and end apart: 9, of which 7 were waited for; matrix products, arithmetic and copies ran while one was open for 0% of the time, Pallas kernels for 14%

profile of v5, /device:TPU:0, one launch (start us, length us, event | category | flops | bytes accessed | tf_op | source)
XLA Modules:
  0.0 75.1 jit_solution(12324294046875493146)
XLA Ops:
  0.0 0.9 %spread.1 = bf16[256,1024]{1,0:T(8,128)(2,1)S(1)} custom-call(f32[8,2048]{1,0:T(8,128)} %factors.5), custom_call_target="tpu_custom_call" | custom-call | tf_op jit(solution)/shard_map/spread/pallas_call | solution.py:70
  0.9 19.3 %all_to_all.22 = bf16[16,16,1024]{2,1,0:T(8,128)(2,1)S(1)} all-to-all(bf16[16,16,1024]{2,1,0:T(8,128)(2,1)S(1)} %bitcast.5), channel_id=1, replica_groups={{0,8,16,24,32,40,48,56,64,72,80,88,96,104,112,120},{4,12,20,28,36,44,52..., dimensions={0} | all-to-all | bytes 1048576 | tf_op jit(solution)/shard_map/all_to_all | solution.py:59
  20.2 0.0 collective-permute-start
  20.2 3.0 %load.1 = (bf16[1664,2048]{1,0:T(8,128)(2,1)S(1)}, bf16[128,2048]{1,0:T(8,128)(2,1)S(1)}, bf16[16,2048]{1,0:T(8,128)(2,1)S(1)}, f32[8,128]{1,0:T(8,128)S(1)}, f3...) custom-call(s32[32]{0:T(128)} %counts.3, f32[256]{0:T(256)} %weights.3, ...), custom_call_target="tpu_custom_call" | custom-call | bytes 13631488 | tf_op jit(solution)/shard_map/load/pallas_call | solution.py:190
  23.2 0.0 collective-permute-done.packed
  23.2 2.6 %project_first.1 = (bf16[128,1792]{1,0:T(8,128)(2,1)S(1)}, f32[128,1664]{1,0:T(8,128)S(1)}, bf16[128,2048]{1,0:T(8,128)(2,1)S(1)}, f32[8,256]{1,0:T(8,128)S(1)}, bf16[1408,2048]{1,0:T(8,128)(2,1)S(1)}) custom-call(f32[1,1664]{1,0:T(1,128)S(1)} %get-tuple-element.31.mask, bf16[256,1024]{1,0:T(8,128)(2,1)S(1)} %collective-permute-done.packed, ...), custom_call_target="tpu_custom_call" | custom-call | flops 1744830464 | bytes 6815744 | tf_op jit(solution)/shard_map/project_first/pallas_call | solution.py:281
  25.9 1.7 %collective-permute-start.1 = (bf16[128,1792]{1,0:T(8,128)(2,1)S(1)}, bf16[128,1792]{1,0:T(8,128)(2,1)S(1)}, u32[]{:S(2)}, u32[]{:S(2)}) collective-permute-start(bf16[128,1792]{1,0:T(8,128)(2,1)S(1)} %get-tuple-element.37), channel_id=1, source_target_pairs={{0,1},{1,0},{2,3},{3,2},{4,7},{5,6},{6,5},{7,4},{8,9},{9,8},{10,11... | collective-permute-start | bytes 1376264 | tf_op jit(solution)/shard_map/halves0/ppermute | solution.py:51
  27.5 0.0 copy-start
  27.5 0.0 copy-start.1
  27.5 0.0 copy-start.2
  27.6 1.9 %project_second.1 = (bf16[128,1408]{1,0:T(8,128)(2,1)S(1)}, f32[128,1408]{1,0:T(8,128)S(1)}) custom-call(f32[1,1408]{1,0:T(1,128)S(1)} %get-tuple-element.43.mask, bf16[128,2048]{1,0:T(8,128)(2,1)S(1)} %get-tuple-element.39.other, bf16[128,2048]{1,0:T(8,128)(2,1)S(1)} %get-tuple-element.32.own, f32[8,256]{1,0:T(8,128)S(1)} %get-tuple-element.36.gram, ...), custom_call_target="tpu_custom_call" | custom-call | flops 1476395008 | bytes 5767168 | tf_op jit(solution)/shard_map/project_second/pallas_call | solution.py:311
  29.5 0.5 collective-permute-start.3
  30.0 4.4 %collective-permute-done.1 = bf16[128,1792]{1,0:T(8,128)(2,1)S(1)} collective-permute-done((bf16[128,1792]{1,0:T(8,128)(2,1)S(1)}, bf16[128,1792]{1,0:T(8,128)(2,1)S(1)}, u32[]{:S(2)}, u32[]{:S(2)}) %collective-permute-start.1) | collective-permute-done | bytes 458784 | tf_op jit(solution)/shard_map/halves0/ppermute | solution.py:51
  34.5 0.1 fusion.5
  34.6 3.1 %collective-permute-start.2 = (bf16[128,1792]{1,0:T(8,128)(2,1)S(1)}, bf16[128,1792]{1,0:T(8,128)(2,1)S(1)}, u32[]{:S(2)}, u32[]{:S(2)}) collective-permute-start(bf16[128,1792]{1,0:T(8,128)(2,1)S(1)} %pad_maximum_fusion), channel_id=1, source_target_pairs={{0,3},{1,2},{2,1},{3,0},{4,5},{5,4},{6,7},{7,6},{8,11},{9,10},{10,... | collective-permute-start | bytes 1376264 | tf_op jit(solution)/shard_map/sums0/ppermute | solution.py:51
  37.7 0.9 %collective-permute-done.3 = bf16[128,1408]{1,0:T(8,128)(2,1)S(1)} collective-permute-done((bf16[128,1408]{1,0:T(8,128)(2,1)S(1)}, bf16[128,1408]{1,0:T(8,128)(2,1)S(1)}, u32[]{:S(2)}, u32[]{:S(2)}) %collective-permute-start.3) | collective-permute-done | bytes 360480 | tf_op jit(solution)/shard_map/halves1/ppermute | solution.py:51
  38.7 0.1 fusion.4
  38.8 3.1 %collective-permute-start.4 = (bf16[128,1408]{1,0:T(8,128)(2,1)S(1)}, bf16[128,1408]{1,0:T(8,128)(2,1)S(1)}, u32[]{:S(2)}, u32[]{:S(2)}) collective-permute-start(bf16[128,1408]{1,0:T(8,128)(2,1)S(1)} %get-tuple-element.55), channel_id=1, source_target_pairs={{0,3},{1,2},{2,1},{3,0},{4,5},{5,4},{6,7},{7,6},{8,11},{9,10},{10,... | collective-permute-start | bytes 1081352 | tf_op jit(solution)/shard_map/sums1/ppermute | solution.py:51
  41.9 2.6 %collective-permute-done.2.passed = bf16[128,1792]{1,0:T(8,128)(2,1)S(1)} collective-permute-done((bf16[128,1792]{1,0:T(8,128)(2,1)S(1)}, bf16[128,1792]{1,0:T(8,128)(2,1)S(1)}, u32[]{:S(2)}, u32[]{:S(2)}) %collective-permute-start.2) | collective-permute-done | bytes 458784 | tf_op jit(solution)/shard_map/sums0/ppermute | solution.py:51
  44.4 0.2 cube.3.mine
  44.6 0.4 collective-permute-start.5
  45.0 0.0 copy-done
  45.1 0.0 copy-done.1
  45.1 0.0 copy-done.2
  45.1 0.9 %model.1 = (f32[8,2048]{1,0:T(8,128)S(1)}, f32[1,2048]{1,0:T(1,128)S(1)}) custom-call(s32[32]{0:T(128)S(1)} %copy-done.2, f32[256]{0:T(256)S(1)} %copy-done.1, f32[8,256]{1,0:T(8,128)S(1)} %maximum_add_fusion.1.gram, bf16[128,2048]{1,0:T(8,128)(2,1)S(1)} %get-tuple-element.39.other, bf16[128,2048]{1,0:T(8,128)(2,1)S(1)} %get-tuple-element.32.own, ...), custom_call_target="tpu_custom_call" | custom-call | tf_op jit(solution)/shard_map/model/pallas_call | solution.py:359
  46.0 3.1 %collective-permute-done.4.passed = bf16[128,1408]{1,0:T(8,128)(2,1)S(1)} collective-permute-done((bf16[128,1408]{1,0:T(8,128)(2,1)S(1)}, bf16[128,1408]{1,0:T(8,128)(2,1)S(1)}, u32[]{:S(2)}, u32[]{:S(2)}) %collective-permute-start.4) | collective-permute-done | bytes 360480 | tf_op jit(solution)/shard_map/sums1/ppermute | solution.py:51
  49.0 0.2 cube.2.piece
  49.2 0.8 %collective-permute-start.6 = (bf16[128,1408]{1,0:T(8,128)(2,1)S(1)}, bf16[128,1408]{1,0:T(8,128)(2,1)S(1)}, u32[]{:S(2)}, u32[]{:S(2)}) collective-permute-start(bf16[128,1408]{1,0:T(8,128)(2,1)S(1)} %cube.2.piece), channel_id=1, source_target_pairs={{0,1},{1,0},{2,3},{3,2},{4,7},{5,6},{6,5},{7,4},{8,9},{9,8},{10,11... | collective-permute-start | bytes 1081352 | tf_op jit(solution)/shard_map/cubes1/ppermute | solution.py:51
  50.0 2.8 %collective-permute-done.5.other = bf16[128,1664]{1,0:T(8,128)(2,1)S(1)} collective-permute-done((bf16[128,1664]{1,0:T(8,128)(2,1)S(1)}, bf16[128,1664]{1,0:T(8,128)(2,1)S(1)}, u32[]{:S(2)}, u32[]{:S(2)}) %collective-permute-start.5) | collective-permute-done | bytes 426016 | tf_op jit(solution)/shard_map/cubes0/ppermute | solution.py:51
  52.8 2.2 %cross.1 = (f32[256,1024]{1,0:T(8,128)S(1)}, f32[256,1024]{1,0:T(8,128)S(1)}) custom-call(bf16[128,1664]{1,0:T(8,128)(2,1)S(1)} %cube.3.mine, bf16[128,1664]{1,0:T(8,128)(2,1)S(1)} %collective-permute-done.5.other, bf16[1664,2048]{1,0:T(8,128)(2,1)S(1)} %get-tuple-element.35.near), custom_call_target="tpu_custom_call" | custom-call | flops 1744830464 | bytes 6815744 | tf_op jit(solution)/shard_map/cross/pallas_call | solution.py:426
  55.0 1.1 %cross_pair.2 = (f32[128,1024]{1,0:T(8,128)S(1)}, f32[128,1024]{1,0:T(8,128)S(1)}) custom-call(bf16[128,1408]{1,0:T(8,128)(2,1)S(1)} %cube.2.piece, bf16[1408,2048]{1,0:T(8,128)(2,1)S(1)} %get-tuple-element.44.near, f32[256,1024]{1,0:T(8,128)S(1)} %get-tuple-element.47.term_other, f32[256,1024]{1,0:T(8,128)S(1)} %get-tuple-element.48.term_own), custom_call_target="tpu_custom_call" | custom-call | flops 738197504 | bytes 5767168 | tf_op jit(solution)/shard_map/cross_pair/pallas_call | solution.py:470
  56.0 0.1 collective-permute-start.7
  56.1 0.6 collective-permute-done.6.piece
  56.7 1.1 %cross_pair.3 = (bf16[128,1024]{1,0:T(8,128)(2,1)S(1)}, f32[128,1024]{1,0:T(8,128)S(1)}) custom-call(bf16[128,1408]{1,0:T(8,128)(2,1)S(1)} %collective-permute-done.6.piece, bf16[1408,2048]{1,0:T(8,128)(2,1)S(1)} %get-tuple-element.44.near, f32[256,1024]{1,0:T(8,128)S(1)} %get-tuple-element.47.term_other, f32[256,1024]{1,0:T(8,128)S(1)} %get-tuple-element.48.term_own), custom_call_target="tpu_custom_call" | custom-call | flops 738197504 | bytes 5767168 | tf_op jit(solution)/shard_map/cross_pair/pallas_call | solution.py:470
  57.8 0.1 collective-permute-start.8
  57.9 1.5 %collective-permute-done.8.from_sent = bf16[128,1024]{1,0:T(8,128)(2,1)S(1)} collective-permute-done((bf16[128,1024]{1,0:T(8,128)(2,1)S(1)}, bf16[128,1024]{1,0:T(8,128)(2,1)S(1)}, u32[]{:S(2)}, u32[]{:S(2)}) %collective-permute-start.8) | collective-permute-done | bytes 262176 | tf_op jit(solution)/shard_map/ppermute | solution.py:55
  59.4 0.0 collective-permute-done.7.from_kept
  59.4 0.2 add.51
  59.6 14.8 %all_to_all.23 = bf16[16,16,1024]{2,1,0:T(8,128)(2,1)S(1)} all-to-all(bf16[16,16,1024]{2,1,0:T(8,128)(2,1)S(1)} %bitcast.6), channel_id=1, replica_groups={{0,8,16,24,32,40,48,56,64,72,80,88,96,104,112,120},{4,12,20,28,36,44,52..., dimensions={0} | all-to-all | bytes 1048576 | tf_op jit(solution)/shard_map/all_to_all | solution.py:59
  74.4 0.7 finish.1
  (10 shorter events, 0.1 us)
Async XLA Ops:
  20.2 3.0 %collective-permute-start = (bf16[256,1024]{1,0:T(8,128)(2,1)S(1)}, bf16[256,1024]{1,0:T(8,128)(2,1)S(1)}, u32[]{:S(2)}, u32[]{:S(2)}) collective-permute-start(bf16[256,1024]{1,0:T(8,128)(2,1)S(1)} %bitcast.7), channel_id=1, source_target_pairs={{0,4},{4,0},{8,12},{12,8},{16,20},{20,16},{24,28},{28,24},{32,36},... | collective-permute-start | bytes 1572872 | tf_op jit(solution)/shard_map/ppermute | solution.py:55
  25.9 8.6 %collective-permute-start.1 = (bf16[128,1792]{1,0:T(8,128)(2,1)S(1)}, bf16[128,1792]{1,0:T(8,128)(2,1)S(1)}, u32[]{:S(2)}, u32[]{:S(2)}) collective-permute-start(bf16[128,1792]{1,0:T(8,128)(2,1)S(1)} %get-tuple-element.37), channel_id=1, source_target_pairs={{0,1},{1,0},{2,3},{3,2},{4,7},{5,6},{6,5},{7,4},{8,9},{9,8},{10,11... | collective-permute-start | bytes 1376264 | tf_op jit(solution)/shard_map/halves0/ppermute | solution.py:51
  27.5 17.5 %copy-start = (f32[8,2048]{1,0:T(8,128)S(1)}, f32[8,2048]{1,0:T(8,128)}, u32[]{:S(2)}) copy-start(f32[8,2048]{1,0:T(8,128)} %factors.5) | copy-start | bytes 196612
  27.5 17.5 %copy-start.1 = (f32[256]{0:T(256)S(1)}, f32[256]{0:T(256)}, u32[]{:S(2)}) copy-start(f32[256]{0:T(256)} %weights.3) | copy-start | bytes 3076
  27.5 17.5 %copy-start.2 = (s32[32]{0:T(128)S(1)}, s32[32]{0:T(128)}, u32[]{:S(2)}) copy-start(s32[32]{0:T(128)} %counts.3) | copy-start | bytes 388
  29.5 9.2 %collective-permute-start.3 = (bf16[128,1408]{1,0:T(8,128)(2,1)S(1)}, bf16[128,1408]{1,0:T(8,128)(2,1)S(1)}, u32[]{:S(2)}, u32[]{:S(2)}) collective-permute-start(bf16[128,1408]{1,0:T(8,128)(2,1)S(1)} %get-tuple-element.46), channel_id=1, source_target_pairs={{0,1},{1,0},{2,3},{3,2},{4,7},{5,6},{6,5},{7,4},{8,9},{9,8},{10,11... | collective-permute-start | bytes 1081352 | tf_op jit(solution)/shard_map/halves1/ppermute | solution.py:51
  34.6 9.8 %collective-permute-start.2 = (bf16[128,1792]{1,0:T(8,128)(2,1)S(1)}, bf16[128,1792]{1,0:T(8,128)(2,1)S(1)}, u32[]{:S(2)}, u32[]{:S(2)}) collective-permute-start(bf16[128,1792]{1,0:T(8,128)(2,1)S(1)} %pad_maximum_fusion), channel_id=1, source_target_pairs={{0,3},{1,2},{2,1},{3,0},{4,5},{5,4},{6,7},{7,6},{8,11},{9,10},{10,... | collective-permute-start | bytes 1376264 | tf_op jit(solution)/shard_map/sums0/ppermute | solution.py:51
  38.8 10.3 %collective-permute-start.4 = (bf16[128,1408]{1,0:T(8,128)(2,1)S(1)}, bf16[128,1408]{1,0:T(8,128)(2,1)S(1)}, u32[]{:S(2)}, u32[]{:S(2)}) collective-permute-start(bf16[128,1408]{1,0:T(8,128)(2,1)S(1)} %get-tuple-element.55), channel_id=1, source_target_pairs={{0,3},{1,2},{2,1},{3,0},{4,5},{5,4},{6,7},{7,6},{8,11},{9,10},{10,... | collective-permute-start | bytes 1081352 | tf_op jit(solution)/shard_map/sums1/ppermute | solution.py:51
  44.6 8.2 %collective-permute-start.5 = (bf16[128,1664]{1,0:T(8,128)(2,1)S(1)}, bf16[128,1664]{1,0:T(8,128)(2,1)S(1)}, u32[]{:S(2)}, u32[]{:S(2)}) collective-permute-start(bf16[128,1664]{1,0:T(8,128)(2,1)S(1)} %cube.3.mine), channel_id=1, source_target_pairs={{0,1},{1,0},{2,3},{3,2},{4,7},{5,6},{6,5},{7,4},{8,9},{9,8},{10,11... | collective-permute-start | bytes 1277960 | tf_op jit(solution)/shard_map/cubes0/ppermute | solution.py:51
  49.2 7.5 %collective-permute-start.6 = (bf16[128,1408]{1,0:T(8,128)(2,1)S(1)}, bf16[128,1408]{1,0:T(8,128)(2,1)S(1)}, u32[]{:S(2)}, u32[]{:S(2)}) collective-permute-start(bf16[128,1408]{1,0:T(8,128)(2,1)S(1)} %cube.2.piece), channel_id=1, source_target_pairs={{0,1},{1,0},{2,3},{3,2},{4,7},{5,6},{6,5},{7,4},{8,9},{9,8},{10,11... | collective-permute-start | bytes 1081352 | tf_op jit(solution)/shard_map/cubes1/ppermute | solution.py:51
  56.0 3.4 %collective-permute-start.7 = (f32[128,1024]{1,0:T(8,128)S(1)}, f32[128,1024]{1,0:T(8,128)S(1)}, u32[]{:S(2)}, u32[]{:S(2)}) collective-permute-start(f32[128,1024]{1,0:T(8,128)S(1)} %get-tuple-element.51), channel_id=1, source_target_pairs={{0,4},{4,0},{8,12},{12,8},{16,20},{20,16},{24,28},{28,24},{32,36},... | collective-permute-start | bytes 1572872 | tf_op jit(solution)/shard_map/ppermute | solution.py:55
  57.8 1.6 %collective-permute-start.8 = (bf16[128,1024]{1,0:T(8,128)(2,1)S(1)}, bf16[128,1024]{1,0:T(8,128)(2,1)S(1)}, u32[]{:S(2)}, u32[]{:S(2)}) collective-permute-start(bf16[128,1024]{1,0:T(8,128)(2,1)S(1)} %get-tuple-element.52), channel_id=1, source_target_pairs={{0,4},{4,0},{8,12},{12,8},{16,20},{20,16},{24,28},{28,24},{32,36},... | collective-permute-start | bytes 786440 | tf_op jit(solution)/shard_map/ppermute | solution.py:55

commit v6 on v5

--- a/solution.py
+++ b/solution.py
@@ -239,9 +239,8 @@
     return lax.dot_general(left, right, (((1,), (1,)), ((), ())), preferred_element_type=F32)
 
 
-def project_part(mask, other, own, near, sent, kept, scratch):
-    half, slots = kept.shape
-    block = half // 2
+def arrange(other, own, scratch):
+    block = scratch.shape[0] // 4
     for i, quarter in enumerate(order_of()):
         at = pl.ds(pl.multiple_of((quarter >> 1) * block, block), block)
         to = slice(i * block, (i + 1) * block)
@@ -251,6 +250,9 @@
             def _():
                 scratch[to, :] = ref[at, :]
 
+
+def project_part(mask, near, sent, kept, scratch):
+    half, slots = kept.shape
     value = nt_dot(scratch[...], near[...])
     value = value * mask[...]
     sent[:, :slots] = value[:half].astype(BF16)
@@ -267,7 +269,8 @@
 def first_kernel(mask, packed, own, left, gram_own, near, samples, sent, kept, other, gram, later, scratch, sems):
     copies = fetch(samples, later, sems, 1)
     unpack(packed, other, 0)
-    project_part(mask, other, own, near, sent, kept, scratch)
+    arrange(other, own, scratch)
+    project_part(mask, near, sent, kept, scratch)
     gram[...] = jnp.concatenate([gram_of(nt_dot(left[...], other[...])), gram_own[...]], 1)
     if GRAM_PART == 0:
         put_gram(sent, gram)
@@ -281,16 +284,16 @@
     return pl.pallas_call(
         first_kernel,
         in_specs=[VMEM] * 6 + [ANY],
-        out_specs=[VMEM] * 5,
+        out_specs=[VMEM] * 6,
         out_shape=[
             jax.ShapeDtypeStruct((count // 2, slots + LANES * (GRAM_PART == 0)), BF16),
             jax.ShapeDtypeStruct((count // 2, slots), F32),
             jax.ShapeDtypeStruct((count // 2, depth), BF16),
             jax.ShapeDtypeStruct((left.shape[0] // 2, count), F32),
             pltpu.VMEM((SIZES[1], depth), BF16),
+            jax.ShapeDtypeStruct((count, depth), BF16),
         ],
         scratch_shapes=[
-            pltpu.VMEM((count, depth), BF16),
             pltpu.SemaphoreType.DMA((LOADS,)),
         ],
         compiler_params=PARAMS,
@@ -299,28 +302,27 @@
     )(mask, packed, own, left, gram_own, in_vmem(near), in_hbm(samples))
 
 
-def second_kernel(mask, other, own, gram, near, sent, kept, scratch):
-    project_part(mask, other, own, near, sent, kept, scratch)
+def second_kernel(mask, scratch, gram, near, sent, kept):
+    project_part(mask, near, sent, kept, scratch)
     if GRAM_PART == 1:
         put_gram(sent, gram)
 
 
-def project_second(mask, other, own, gram, near):
+def project_second(mask, rows, gram, near):
     slots, depth = near.shape
-    count = 2 * own.shape[0]
+    count = rows.shape[0]
     return pl.pallas_call(
         second_kernel,
-        in_specs=[VMEM] * 5,
+        in_specs=[VMEM] * 4,
         out_specs=[VMEM] * 2,
         out_shape=[
             jax.ShapeDtypeStruct((count // 2, slots + LANES * (GRAM_PART == 1)), BF16),
             jax.ShapeDtypeStruct((count // 2, slots), F32),
         ],
-        scratch_shapes=[pltpu.VMEM((count, depth), BF16)],
         compiler_params=PARAMS,
         cost_estimate=estimate(slots, depth, count),
         name="project_second",
-    )(mask, other, own, gram, in_vmem(near))
+    )(mask, rows, gram, in_vmem(near))
 
 
 def estimate(slots, depth, rows):
@@ -513,10 +515,10 @@
         counts, weights, packed_own, factors, samples
     )
     packed_other = core_swap(packed_own)
-    sent0, kept0, other, gram, near1 = project_first(
+    sent0, kept0, other, gram, near1, rows = project_first(
         mask0, packed_other, own, left, gram_own, near0, samples
     )
-    sent1, kept1 = project_second(mask1, other, own, gram, near1)
+    sent1, kept1 = project_second(mask1, rows, gram, near1)
     nears = (near0, near1)
 
     pieces = []

time: 75.4 us -> 75.3 us (level)
  no operation moved by 1% of the time
where the time goes in v6:
time: 75.3 us; the launch traced here: 75.1 us
  blocking collectives  34.1 us (45%)
  waiting for transfers between devices  16 us (21%)
  Pallas kernels  14.8 us (20%)
  starting transfers between devices  9.75 us (13%)
    all_to_all x2, blocking collectives, plane_exchange(): return lax.all_to_all(x, 'dp', 0, 0, axis_index_groups=PLANES, tiled=True)  34.1 us
    ppermute x6, waiting for transfers between devices, feat_swap(): return lax.ppermute(x, ('dp', 'feat'), pairs)  14.5 us
    ppermute x6, starting transfers between devices, feat_swap(): return lax.ppermute(x, ('dp', 'feat'), pairs)  9.58 us
    pallas_call x1, Pallas kernels, load(): pl.pallas_call(load_kernel, in_specs=[ANY, ANY, VMEM, ANY, ANY], out_spec...  3.02 us
    pallas_call x1, Pallas kernels, project_first(): pl.pallas_call(first_kernel, in_specs=[VMEM] * 6 + [ANY], out_specs=[VMEM...  2.65 us
    pallas_call x1, Pallas kernels, cross(): pl.pallas_call(functools.partial(cross_kernel, sides=sides, add=bool(term...  2.16 us
    pallas_call x2, Pallas kernels, cross_pair(): pl.pallas_call(functools.partial(pair_kernel, first=first, tile=tile), in...  2.15 us
    pallas_call x1, Pallas kernels, project_second(): pl.pallas_call(second_kernel, in_specs=[VMEM] * 4, out_specs=[VMEM] * 2,...  1.82 us
  transfers between devices with their start and end apart: 9, of which 7 were waited for; matrix products, arithmetic and copies ran while one was open for 0% of the time, Pallas kernels for 14%

profile of v6, /device:TPU:0, one launch (start us, length us, event | category | flops | bytes accessed | tf_op | source)
XLA Modules:
  0.0 75.1 jit_solution(7480122047228654287)
XLA Ops:
  0.0 0.9 %spread.1 = bf16[256,1024]{1,0:T(8,128)(2,1)S(1)} custom-call(f32[8,2048]{1,0:T(8,128)} %factors.5), custom_call_target="tpu_custom_call" | custom-call | tf_op jit(solution)/shard_map/spread/pallas_call | solution.py:70
  0.9 19.3 %all_to_all.22 = bf16[16,16,1024]{2,1,0:T(8,128)(2,1)S(1)} all-to-all(bf16[16,16,1024]{2,1,0:T(8,128)(2,1)S(1)} %bitcast.5), channel_id=1, replica_groups={{0,8,16,24,32,40,48,56,64,72,80,88,96,104,112,120},{4,12,20,28,36,44,52..., dimensions={0} | all-to-all | bytes 1048576 | tf_op jit(solution)/shard_map/all_to_all | solution.py:59
  20.2 0.0 collective-permute-start
  20.2 3.0 %load.1 = (bf16[1664,2048]{1,0:T(8,128)(2,1)S(1)}, bf16[128,2048]{1,0:T(8,128)(2,1)S(1)}, bf16[16,2048]{1,0:T(8,128)(2,1)S(1)}, f32[8,128]{1,0:T(8,128)S(1)}, f3...) custom-call(s32[32]{0:T(128)} %counts.3, f32[256]{0:T(256)} %weights.3, ...), custom_call_target="tpu_custom_call" | custom-call | bytes 13631488 | tf_op jit(solution)/shard_map/load/pallas_call | solution.py:190
  23.2 0.0 collective-permute-done.packed
  23.2 2.6 %project_first.1 = (bf16[128,1792]{1,0:T(8,128)(2,1)S(1)}, f32[128,1664]{1,0:T(8,128)S(1)}, bf16[128,2048]{1,0:T(8,128)(2,1)S(1)}, f32[8,256]{1,0:T(8,128)S(1)},...) custom-call(f32[1,1664]{1,0:T(1,128)S(1)} %get-tuple-element.32.mask, ...), custom_call_target="tpu_custom_call" | custom-call | flops 1744830464 | bytes 6815744 | tf_op jit(solution)/shard_map/project_first/pallas_call | solution.py:284
  25.9 1.7 %collective-permute-start.1 = (bf16[128,1792]{1,0:T(8,128)(2,1)S(1)}, bf16[128,1792]{1,0:T(8,128)(2,1)S(1)}, u32[]{:S(2)}, u32[]{:S(2)}) collective-permute-start(bf16[128,1792]{1,0:T(8,128)(2,1)S(1)} %get-tuple-element.38), channel_id=1, source_target_pairs={{0,1},{1,0},{2,3},{3,2},{4,7},{5,6},{6,5},{7,4},{8,9},{9,8},{10,11... | collective-permute-start | bytes 1376264 | tf_op jit(solution)/shard_map/halves0/ppermute | solution.py:51
  27.5 0.0 copy-start
  27.5 0.0 copy-start.1
  27.6 0.0 copy-start.2
  27.6 1.8 %project_second.1 = (bf16[128,1408]{1,0:T(8,128)(2,1)S(1)}, f32[128,1408]{1,0:T(8,128)S(1)}) custom-call(f32[1,1408]{1,0:T(1,128)S(1)} %get-tuple-element.44.mask, bf16[256,2048]{1,0:T(8,128)(2,1)S(1)} %get-tuple-element.45.scratch, f32[8,256]{1,0:T(8,128)S(1)} %get-tuple-element.37.gram, bf16[1408,2048]{1,0:T(8,128)(2,1)S(1)} %get-tuple-element.46.near), custom_call_target="tpu_custom_call" | custom-call | flops 1476395008 | bytes 5767168 | tf_op jit(solution)/shard_map/project_second/pallas_call | solution.py:314
  29.4 0.5 collective-permute-start.3
  29.9 4.5 %collective-permute-done.1 = bf16[128,1792]{1,0:T(8,128)(2,1)S(1)} collective-permute-done((bf16[128,1792]{1,0:T(8,128)(2,1)S(1)}, bf16[128,1792]{1,0:T(8,128)(2,1)S(1)}, u32[]{:S(2)}, u32[]{:S(2)}) %collective-permute-start.1) | collective-permute-done | bytes 458784 | tf_op jit(solution)/shard_map/halves0/ppermute | solution.py:51
  34.5 0.1 fusion.5
  34.6 3.1 %collective-permute-start.2 = (bf16[128,1792]{1,0:T(8,128)(2,1)S(1)}, bf16[128,1792]{1,0:T(8,128)(2,1)S(1)}, u32[]{:S(2)}, u32[]{:S(2)}) collective-permute-start(bf16[128,1792]{1,0:T(8,128)(2,1)S(1)} %pad_maximum_fusion), channel_id=1, source_target_pairs={{0,3},{1,2},{2,1},{3,0},{4,5},{5,4},{6,7},{7,6},{8,11},{9,10},{10,... | collective-permute-start | bytes 1376264 | tf_op jit(solution)/shard_map/sums0/ppermute | solution.py:51
  37.7 0.9 %collective-permute-done.3 = bf16[128,1408]{1,0:T(8,128)(2,1)S(1)} collective-permute-done((bf16[128,1408]{1,0:T(8,128)(2,1)S(1)}, bf16[128,1408]{1,0:T(8,128)(2,1)S(1)}, u32[]{:S(2)}, u32[]{:S(2)}) %collective-permute-start.3) | collective-permute-done | bytes 360480 | tf_op jit(solution)/shard_map/halves1/ppermute | solution.py:51
  38.7 0.1 fusion.4
  38.8 3.1 %collective-permute-start.4 = (bf16[128,1408]{1,0:T(8,128)(2,1)S(1)}, bf16[128,1408]{1,0:T(8,128)(2,1)S(1)}, u32[]{:S(2)}, u32[]{:S(2)}) collective-permute-start(bf16[128,1408]{1,0:T(8,128)(2,1)S(1)} %get-tuple-element.57), channel_id=1, source_target_pairs={{0,3},{1,2},{2,1},{3,0},{4,5},{5,4},{6,7},{7,6},{8,11},{9,10},{10,... | collective-permute-start | bytes 1081352 | tf_op jit(solution)/shard_map/sums1/ppermute | solution.py:51
  41.9 2.6 %collective-permute-done.2.passed = bf16[128,1792]{1,0:T(8,128)(2,1)S(1)} collective-permute-done((bf16[128,1792]{1,0:T(8,128)(2,1)S(1)}, bf16[128,1792]{1,0:T(8,128)(2,1)S(1)}, u32[]{:S(2)}, u32[]{:S(2)}) %collective-permute-start.2) | collective-permute-done | bytes 458784 | tf_op jit(solution)/shard_map/sums0/ppermute | solution.py:51
  44.4 0.2 cube.3.mine
  44.6 0.4 collective-permute-start.5
  45.1 0.0 copy-done
  45.1 0.0 copy-done.1
  45.1 0.0 copy-done.2
  45.1 0.9 %model.1 = (f32[8,2048]{1,0:T(8,128)S(1)}, f32[1,2048]{1,0:T(1,128)S(1)}) custom-call(s32[32]{0:T(128)S(1)} %copy-done.2, f32[256]{0:T(256)S(1)} %copy-done.1, f32[8,256]{1,0:T(8,128)S(1)} %maximum_add_fusion.1.gram, bf16[128,2048]{1,0:T(8,128)(2,1)S(1)} %get-tuple-element.40.other, bf16[128,2048]{1,0:T(8,128)(2,1)S(1)} %get-tuple-element.33.own, ...), custom_call_target="tpu_custom_call" | custom-call | tf_op jit(solution)/shard_map/model/pallas_call | solution.py:361
  46.0 3.0 %collective-permute-done.4.passed = bf16[128,1408]{1,0:T(8,128)(2,1)S(1)} collective-permute-done((bf16[128,1408]{1,0:T(8,128)(2,1)S(1)}, bf16[128,1408]{1,0:T(8,128)(2,1)S(1)}, u32[]{:S(2)}, u32[]{:S(2)}) %collective-permute-start.4) | collective-permute-done | bytes 360480 | tf_op jit(solution)/shard_map/sums1/ppermute | solution.py:51
  49.0 0.1 cube.2.piece
  49.2 0.8 %collective-permute-start.6 = (bf16[128,1408]{1,0:T(8,128)(2,1)S(1)}, bf16[128,1408]{1,0:T(8,128)(2,1)S(1)}, u32[]{:S(2)}, u32[]{:S(2)}) collective-permute-start(bf16[128,1408]{1,0:T(8,128)(2,1)S(1)} %cube.2.piece), channel_id=1, source_target_pairs={{0,1},{1,0},{2,3},{3,2},{4,7},{5,6},{6,5},{7,4},{8,9},{9,8},{10,11... | collective-permute-start | bytes 1081352 | tf_op jit(solution)/shard_map/cubes1/ppermute | solution.py:51
  49.9 2.9 %collective-permute-done.5.other = bf16[128,1664]{1,0:T(8,128)(2,1)S(1)} collective-permute-done((bf16[128,1664]{1,0:T(8,128)(2,1)S(1)}, bf16[128,1664]{1,0:T(8,128)(2,1)S(1)}, u32[]{:S(2)}, u32[]{:S(2)}) %collective-permute-start.5) | collective-permute-done | bytes 426016 | tf_op jit(solution)/shard_map/cubes0/ppermute | solution.py:51
  52.8 2.2 %cross.1 = (f32[256,1024]{1,0:T(8,128)S(1)}, f32[256,1024]{1,0:T(8,128)S(1)}) custom-call(bf16[128,1664]{1,0:T(8,128)(2,1)S(1)} %cube.3.mine, bf16[128,1664]{1,0:T(8,128)(2,1)S(1)} %collective-permute-done.5.other, bf16[1664,2048]{1,0:T(8,128)(2,1)S(1)} %get-tuple-element.36.near), custom_call_target="tpu_custom_call" | custom-call | flops 1744830464 | bytes 6815744 | tf_op jit(solution)/shard_map/cross/pallas_call | solution.py:428
  55.0 1.1 %cross_pair.2 = (f32[128,1024]{1,0:T(8,128)S(1)}, f32[128,1024]{1,0:T(8,128)S(1)}) custom-call(bf16[128,1408]{1,0:T(8,128)(2,1)S(1)} %cube.2.piece, bf16[1408,2048]{1,0:T(8,128)(2,1)S(1)} %get-tuple-element.46.near, f32[256,1024]{1,0:T(8,128)S(1)} %get-tuple-element.49.term_other, f32[256,1024]{1,0:T(8,128)S(1)} %get-tuple-element.50.term_own), custom_call_target="tpu_custom_call" | custom-call | flops 738197504 | bytes 5767168 | tf_op jit(solution)/shard_map/cross_pair/pallas_call | solution.py:472
  56.0 0.1 collective-permute-start.7
  56.1 0.5 collective-permute-done.6.piece
  56.7 1.1 %cross_pair.3 = (bf16[128,1024]{1,0:T(8,128)(2,1)S(1)}, f32[128,1024]{1,0:T(8,128)S(1)}) custom-call(bf16[128,1408]{1,0:T(8,128)(2,1)S(1)} %collective-permute-done.6.piece, bf16[1408,2048]{1,0:T(8,128)(2,1)S(1)} %get-tuple-element.46.near, f32[256,1024]{1,0:T(8,128)S(1)} %get-tuple-element.49.term_other, f32[256,1024]{1,0:T(8,128)S(1)} %get-tuple-element.50.term_own), custom_call_target="tpu_custom_call" | custom-call | flops 738197504 | bytes 5767168 | tf_op jit(solution)/shard_map/cross_pair/pallas_call | solution.py:472
  57.8 0.1 collective-permute-start.8
  57.8 1.5 %collective-permute-done.8.from_sent = bf16[128,1024]{1,0:T(8,128)(2,1)S(1)} collective-permute-done((bf16[128,1024]{1,0:T(8,128)(2,1)S(1)}, bf16[128,1024]{1,0:T(8,128)(2,1)S(1)}, u32[]{:S(2)}, u32[]{:S(2)}) %collective-permute-start.8) | collective-permute-done | bytes 262176 | tf_op jit(solution)/shard_map/ppermute | solution.py:55
  59.4 0.0 collective-permute-done.7.from_kept
  59.4 0.2 add.51
  59.6 14.8 %all_to_all.23 = bf16[16,16,1024]{2,1,0:T(8,128)(2,1)S(1)} all-to-all(bf16[16,16,1024]{2,1,0:T(8,128)(2,1)S(1)} %bitcast.6), channel_id=1, replica_groups={{0,8,16,24,32,40,48,56,64,72,80,88,96,104,112,120},{4,12,20,28,36,44,52..., dimensions={0} | all-to-all | bytes 1048576 | tf_op jit(solution)/shard_map/all_to_all | solution.py:59
  74.3 0.7 finish.1
  (10 shorter events, 0.1 us)
Async XLA Ops:
  20.2 3.0 %collective-permute-start = (bf16[256,1024]{1,0:T(8,128)(2,1)S(1)}, bf16[256,1024]{1,0:T(8,128)(2,1)S(1)}, u32[]{:S(2)}, u32[]{:S(2)}) collective-permute-start(bf16[256,1024]{1,0:T(8,128)(2,1)S(1)} %bitcast.7), channel_id=1, source_target_pairs={{0,4},{4,0},{8,12},{12,8},{16,20},{20,16},{24,28},{28,24},{32,36},... | collective-permute-start | bytes 1572872 | tf_op jit(solution)/shard_map/ppermute | solution.py:55
  25.9 8.6 %collective-permute-start.1 = (bf16[128,1792]{1,0:T(8,128)(2,1)S(1)}, bf16[128,1792]{1,0:T(8,128)(2,1)S(1)}, u32[]{:S(2)}, u32[]{:S(2)}) collective-permute-start(bf16[128,1792]{1,0:T(8,128)(2,1)S(1)} %get-tuple-element.38), channel_id=1, source_target_pairs={{0,1},{1,0},{2,3},{3,2},{4,7},{5,6},{6,5},{7,4},{8,9},{9,8},{10,11... | collective-permute-start | bytes 1376264 | tf_op jit(solution)/shard_map/halves0/ppermute | solution.py:51
  27.5 17.5 %copy-start = (f32[8,2048]{1,0:T(8,128)S(1)}, f32[8,2048]{1,0:T(8,128)}, u32[]{:S(2)}) copy-start(f32[8,2048]{1,0:T(8,128)} %factors.5) | copy-start | bytes 196612
  27.5 17.5 %copy-start.1 = (f32[256]{0:T(256)S(1)}, f32[256]{0:T(256)}, u32[]{:S(2)}) copy-start(f32[256]{0:T(256)} %weights.3) | copy-start | bytes 3076
  27.6 17.5 %copy-start.2 = (s32[32]{0:T(128)S(1)}, s32[32]{0:T(128)}, u32[]{:S(2)}) copy-start(s32[32]{0:T(128)} %counts.3) | copy-start | bytes 388
  29.4 9.3 %collective-permute-start.3 = (bf16[128,1408]{1,0:T(8,128)(2,1)S(1)}, bf16[128,1408]{1,0:T(8,128)(2,1)S(1)}, u32[]{:S(2)}, u32[]{:S(2)}) collective-permute-start(bf16[128,1408]{1,0:T(8,128)(2,1)S(1)} %get-tuple-element.48), channel_id=1, source_target_pairs={{0,1},{1,0},{2,3},{3,2},{4,7},{5,6},{6,5},{7,4},{8,9},{9,8},{10,11... | collective-permute-start | bytes 1081352 | tf_op jit(solution)/shard_map/halves1/ppermute | solution.py:51
  34.6 9.8 %collective-permute-start.2 = (bf16[128,1792]{1,0:T(8,128)(2,1)S(1)}, bf16[128,1792]{1,0:T(8,128)(2,1)S(1)}, u32[]{:S(2)}, u32[]{:S(2)}) collective-permute-start(bf16[128,1792]{1,0:T(8,128)(2,1)S(1)} %pad_maximum_fusion), channel_id=1, source_target_pairs={{0,3},{1,2},{2,1},{3,0},{4,5},{5,4},{6,7},{7,6},{8,11},{9,10},{10,... | collective-permute-start | bytes 1376264 | tf_op jit(solution)/shard_map/sums0/ppermute | solution.py:51
  38.8 10.2 %collective-permute-start.4 = (bf16[128,1408]{1,0:T(8,128)(2,1)S(1)}, bf16[128,1408]{1,0:T(8,128)(2,1)S(1)}, u32[]{:S(2)}, u32[]{:S(2)}) collective-permute-start(bf16[128,1408]{1,0:T(8,128)(2,1)S(1)} %get-tuple-element.57), channel_id=1, source_target_pairs={{0,3},{1,2},{2,1},{3,0},{4,5},{5,4},{6,7},{7,6},{8,11},{9,10},{10,... | collective-permute-start | bytes 1081352 | tf_op jit(solution)/shard_map/sums1/ppermute | solution.py:51
  44.6 8.2 %collective-permute-start.5 = (bf16[128,1664]{1,0:T(8,128)(2,1)S(1)}, bf16[128,1664]{1,0:T(8,128)(2,1)S(1)}, u32[]{:S(2)}, u32[]{:S(2)}) collective-permute-start(bf16[128,1664]{1,0:T(8,128)(2,1)S(1)} %cube.3.mine), channel_id=1, source_target_pairs={{0,1},{1,0},{2,3},{3,2},{4,7},{5,6},{6,5},{7,4},{8,9},{9,8},{10,11... | collective-permute-start | bytes 1277960 | tf_op jit(solution)/shard_map/cubes0/ppermute | solution.py:51
  49.2 7.5 %collective-permute-start.6 = (bf16[128,1408]{1,0:T(8,128)(2,1)S(1)}, bf16[128,1408]{1,0:T(8,128)(2,1)S(1)}, u32[]{:S(2)}, u32[]{:S(2)}) collective-permute-start(bf16[128,1408]{1,0:T(8,128)(2,1)S(1)} %cube.2.piece), channel_id=1, source_target_pairs={{0,1},{1,0},{2,3},{3,2},{4,7},{5,6},{6,5},{7,4},{8,9},{9,8},{10,11... | collective-permute-start | bytes 1081352 | tf_op jit(solution)/shard_map/cubes1/ppermute | solution.py:51
  56.0 3.3 %collective-permute-start.7 = (f32[128,1024]{1,0:T(8,128)S(1)}, f32[128,1024]{1,0:T(8,128)S(1)}, u32[]{:S(2)}, u32[]{:S(2)}) collective-permute-start(f32[128,1024]{1,0:T(8,128)S(1)} %get-tuple-element.53), channel_id=1, source_target_pairs={{0,4},{4,0},{8,12},{12,8},{16,20},{20,16},{24,28},{28,24},{32,36},... | collective-permute-start | bytes 1572872 | tf_op jit(solution)/shard_map/ppermute | solution.py:55
  57.8 1.6 %collective-permute-start.8 = (bf16[128,1024]{1,0:T(8,128)(2,1)S(1)}, bf16[128,1024]{1,0:T(8,128)(2,1)S(1)}, u32[]{:S(2)}, u32[]{:S(2)}) collective-permute-start(bf16[128,1024]{1,0:T(8,128)(2,1)S(1)} %get-tuple-element.54), channel_id=1, source_target_pairs={{0,4},{4,0},{8,12},{12,8},{16,20},{20,16},{24,28},{28,24},{32,36},... | collective-permute-start | bytes 786440 | tf_op jit(solution)/shard_map/ppermute | solution.py:55
